TPU v7x, 32 devices: a whole 2x2x4 slice. The times are simulated.
32 devices in a mesh: patch: 16 (over z, y, core), band: 2 (over x).
Axes of the slice: x: 2, y: 2, z: 4, core: 2. Of those that a mesh axis runs over, the one named last changes fastest.
Arguments:
- tile_flux: bfloat16 [6, 512, 8, 128], P(None, ('patch', 'band')), may hold values from -6 to 6
- tile_weight: bfloat16 [6, 512, 8, 128], P(None, ('patch', 'band')), may hold values from 0.19921875 to 5
- dest_patch: int32 [6, 512], P(None, ('patch', 'band')), may hold values from 0 to 15, as said below
- dest_block: int32 [6, 512], P(None, ('patch', 'band')), may hold values from 0 to 15, as said below
- basis: bfloat16 [2, 21, 31], replicated, may hold values from -1 to 1
- spatial: float32 [16, 6, 3, 21], P('patch'), may hold values from -1.25 to 1.25
Outputs:
- coadd: float32 [16, 64, 512], P('patch', 'band')
Inputs may be any that keep to these rules, and one draw needn't show every extreme that they name: `dest_patch`: for each visit, the tiles held by one device go to exactly 8 different patches, 2 tiles to each. `dest_block`: for each visit, every block of every band of every patch receives exactly one tile.
All inputs are finite; a program needn't handle non-finite values.
Results may differ from a plain program's by a relative error of at most 0.0029.
Values may be sent and summed in bfloat16 or wider, within the bound.
No kernel may reach another device: no remote copies, remote signals or barrier semaphores. Data moves between devices by JAX's collectives and lax.ppermute only.
A program may use at most 64 MiB of HBM per device.

v0:
```python
import jax
import jax.numpy as jnp
from jax import lax
from jax.sharding import PartitionSpec as P

BASIS = 21
TAPS = 31
ROWS = 32
COLS = 512
CAP = 2


def extended(value, sides, width):
    for axis, dim in sides:
        count, length = (lax.axis_size(axis), value.shape[dim])
        up = [(i, (i + 1) % count) for i in range(count - 1)]
        down = [(j, i) for i, j in up]
        last = lax.slice_in_dim(value, length - width, length, axis=dim)
        leading = lax.slice_in_dim(value, 0, width, axis=dim)
        before = lax.ppermute(last, axis, up)
        after = lax.ppermute(leading, axis, down)
        value = jnp.concatenate([before, value, after], axis=dim)
    return value


def column_table(basis):
    width = 128 + TAPS - 1
    inner = jnp.arange(width)[:, None, None]
    outer = jnp.arange(128)[None, :, None]
    offset = jnp.arange(TAPS)[None, None, :]
    ones = (inner - outer == offset).astype(jnp.float32)
    table = jnp.einsum("iot,bt->ibo", ones, basis[0].astype(jnp.float32))
    return table.reshape(width, BASIS * 128).astype(jnp.bfloat16)


def row_table(basis):
    target = jnp.arange(ROWS)[:, None, None]
    source = jnp.arange(ROWS + TAPS - 1)[None, :, None]
    offset = jnp.arange(TAPS)[None, None, :]
    ones = (source - target == offset).astype(jnp.float32)
    table = jnp.einsum("stk,bk->bst", ones, basis[1].astype(jnp.float32))
    return table.astype(jnp.bfloat16)


def column_filter(rows_block, table):
    margin = TAPS // 2
    padded = jnp.pad(rows_block, ((0, 0), (margin, margin)))
    pieces = jnp.stack(
        [padded[:, 128 * column : 128 * column + 128 + TAPS - 1] for column in range(COLS // 128)],
        axis=1,
    )
    result = jnp.einsum("rci,in->rcn", pieces, table, preferred_element_type=jnp.float32)
    return result.astype(jnp.bfloat16).reshape(rows_block.shape[0], COLS // 128, BASIS, 128)


def per_device(tile_flux, tile_weight, dest_patch, dest_block, basis, spatial):
    visits, tile_count, tile_height, tile_width = tile_flux.shape
    patches = lax.axis_size("patch")
    slot_count = patches * CAP
    pixels = tile_height * tile_width
    margin = TAPS // 2
    earlier = jnp.arange(tile_count)[None, :] < jnp.arange(tile_count)[:, None]
    matches = dest_patch[:, :, None] == dest_patch[:, None, :]
    ordinal = jnp.sum(jnp.logical_and(matches, earlier[None]), axis=2)
    slot_index = dest_patch * CAP + ordinal
    routing = slot_index[:, None, :] == jnp.arange(slot_count)[None, :, None]
    routing_b = routing.astype(jnp.bfloat16)
    send_flux = jnp.einsum(
        "vnt,vtx->vnx",
        routing_b,
        tile_flux.reshape(visits, tile_count, pixels),
        preferred_element_type=jnp.float32,
    )
    send_flux = send_flux.astype(jnp.bfloat16).reshape(
        visits, patches, CAP, tile_height, tile_width
    )
    send_weight = jnp.einsum(
        "vnt,vtx->vnx",
        routing_b,
        tile_weight.reshape(visits, tile_count, pixels),
        preferred_element_type=jnp.float32,
    )
    send_weight = send_weight.astype(jnp.bfloat16).reshape(
        visits, patches, CAP, tile_height, tile_width
    )
    send_block = jnp.sum(jnp.where(routing, dest_block[:, None, :] + 1, 0), axis=2) - 1
    send_block = send_block.astype(jnp.bfloat16).reshape(visits, patches, CAP)
    block_ids = jnp.arange(tile_count).astype(jnp.bfloat16)
    across = COLS // tile_width
    ctable = column_table(basis)
    rtable = row_table(basis)
    patch_rows = ROWS * lax.axis_size("band")
    first_row = (lax.axis_index("band") * ROWS).astype(jnp.float32)
    row_coord = (2.0 * (first_row + jnp.arange(ROWS, dtype=jnp.float32)) + 1.0) / patch_rows - 1.0
    col_coord = ((2.0 * jnp.arange(COLS, dtype=jnp.float32) + 1.0) / COLS - 1.0).reshape(
        COLS // 128, 128
    )

    def one_visit(inputs):
        flux_k, weight_k, block_k, spatial_row = inputs
        placing = (block_k.reshape(slot_count)[None, :] == block_ids[:, None]).astype(jnp.bfloat16)
        placed = jnp.dot(
            placing, flux_k.reshape(slot_count, pixels), preferred_element_type=jnp.float32
        )
        placed_weight = jnp.dot(
            placing, weight_k.reshape(slot_count, pixels), preferred_element_type=jnp.float32
        )
        frame = placed.astype(jnp.bfloat16).reshape(
            ROWS // tile_height, across, tile_height, tile_width
        )
        frame = frame.transpose(0, 2, 1, 3).reshape(ROWS, COLS)
        weight_frame = placed_weight.reshape(ROWS // tile_height, across, tile_height, tile_width)
        weight_frame = weight_frame.transpose(0, 2, 1, 3).reshape(ROWS, COLS)
        widened = extended(frame, (("band", 0),), margin)
        filtered = column_filter(widened, ctable)
        smoothed = jnp.einsum(
            "bst,tcbo->scbo", rtable, filtered, preferred_element_type=jnp.float32
        )
        mixture = jnp.einsum(
            "scbo,jb->jsco",
            smoothed,
            spatial_row,
            precision=lax.Precision.HIGHEST,
            preferred_element_type=jnp.float32,
        )
        matched = mixture[0] + row_coord[:, None, None] * mixture[1] + col_coord[None] * mixture[2]
        matched = matched.reshape(ROWS, COLS)
        return (weight_frame * matched, weight_frame)

    flux_in, weight_in, block_in = (
        lax.all_to_all(send_flux, "patch", split_axis=1, concat_axis=1, tiled=True),
        lax.all_to_all(send_weight, "patch", split_axis=1, concat_axis=1, tiled=True),
        lax.all_to_all(send_block, "patch", split_axis=1, concat_axis=1, tiled=True),
    )
    weighted, weight_sums = lax.map(one_visit, (flux_in, weight_in, block_in, spatial[0]))
    numerator = jnp.sum(weighted, axis=0)
    denominator = jnp.sum(weight_sums, axis=0)
    coadd = numerator / denominator
    return coadd[None]


def solution(mesh):
    in_specs = (
        P(None, ("patch", "band"), None, None),
        P(None, ("patch", "band"), None, None),
        P(None, ("patch", "band")),
        P(None, ("patch", "band")),
        P(),
        P("patch", None, None, None),
    )
    out_specs = P("patch", "band", None)
    return jax.shard_map(
        per_device, mesh=mesh, in_specs=in_specs, out_specs=out_specs, check_vma=False
    )
```

profile of v0, /device:TPU:0, one launch (start us, length us, event | category | flops | bytes accessed | tf_op | source)
XLA Modules:
  0.0 139.1 jit_solution(2035870134129517686)
XLA Ops:
  0.0 1.0 convert_reduce_fusion
  1.0 0.7 multiply_add_fusion.2
  1.9 0.7 copy.30
  2.5 7.4 %all-to-all-start = ((bf16[6,16,2]{0,2,1:T(2,128)(2,1)}), bf16[6,16,2]{0,2,1:T(2,128)(2,1)S(1)}, u32[]{:S(2)}, u32[]{:S(2)}) async-start(bf16[6,16,2]{0,2,1:T(2,128)(2,1)} %bitcast), calls=%async_computation | async-start | bytes 16384 | tf_op jit(solution)/shard_map/all_to_all | solution.py:133
  9.9 1.0 reshape.247
  11.4 0.8 copy.31
  12.2 4.1 %all-to-all-done = bf16[6,16,2]{0,2,1:T(2,128)(2,1)S(1)} async-done(((bf16[6,16,2]{0,2,1:T(2,128)(2,1)}), bf16[6,16,2]{0,2,1:T(2,128)(2,1)S(1)}, u32[]{:S(2)}, u32[]{:S(2)}) %all-to-all-start) | async-done | bytes 416 | tf_op jit(solution)/shard_map/all_to_all | solution.py:133
  16.3 3.6 %all-to-all-start.1 = ((bf16[6,16,2,8,128]{4,3,2,0,1:T(8,128)(2,1)}), bf16[6,16,2,8,128]{4,3,2,0,1:T(8,128)(2,1)S(1)}, u32[]{:S(2)}, u32[]{:S(2)}) async-start(bf16[6,16,2,8,128]{4,3,2,0,1:T(8,128)(2,1)} %copy.31), calls=%async_computation.1 | async-start | bytes 786432 | tf_op jit(solution)/shard_map/all_to_all | solution.py:132
  20.4 0.8 copy.32
  21.2 10.8 %all-to-all-done.1 = bf16[6,16,2,8,128]{4,3,2,0,1:T(8,128)(2,1)S(1)} async-done(((bf16[6,16,2,8,128]{4,3,2,0,1:T(8,128)(2,1)}), bf16[6,16,2,8,128]{4,3,2,0,1:T(8,128)(2,1)S(1)}, u32[]{:S(2)}, u32[]{:S(2)}) %all-to-all-start.1) | async-done | bytes 393248 | tf_op jit(solution)/shard_map/all_to_all | solution.py:132
  32.0 4.2 %all-to-all-start.2 = ((bf16[6,16,2,8,128]{4,3,2,0,1:T(8,128)(2,1)}), bf16[6,16,2,8,128]{4,3,2,0,1:T(8,128)(2,1)}, u32[]{:S(2)}, u32[]{:S(2)}) async-start(bf16[6,16,2,8,128]{4,3,2,0,1:T(8,128)(2,1)} %copy.32), calls=%async_computation.2 | async-start | bytes 786432 | tf_op jit(solution)/shard_map/all_to_all | solution.py:131
  37.6 0.8 copy.35
  38.4 10.0 %all-to-all-done.2 = bf16[6,16,2,8,128]{4,3,2,0,1:T(8,128)(2,1)} async-done(((bf16[6,16,2,8,128]{4,3,2,0,1:T(8,128)(2,1)}), bf16[6,16,2,8,128]{4,3,2,0,1:T(8,128)(2,1)}, u32[]{:S(2)}, u32[]{:S(2)}) %all-to-all-start.2) | async-done | bytes 393248 | tf_op jit(solution)/shard_map/all_to_all | solution.py:131
  48.4 88.0 %while.16 = (s32[]{:T(128)}, f32[6,32,512]{2,1,0:T(8,128)}, f32[6,32,512]{2,1,0:T(8,128)}, bf16[6,16,2]{2,1,0:T(8,128)(2,1)}, bf16[6,16,2,8,128]{4,3,2,0,1:T(8,1...) while((s32[]{:T(128)}, f32[6,32,512]{2,1,0:T(8,128)}, ...), condition=%wide.region_3.4_spmd.clone.clone, body=%wide.region_2.3_spmd.clone.clone.sunk | while | flops 268877792 | bytes 18484208 | solution.py:135
  48.4 0.7 constant_dynamic-slice_fusion.5
  49.2 0.9 constant_dynamic-slice_fusion.6
  50.3 1.3 collective-permute-start
  51.6 4.5 %collective-permute-start.1 = (bf16[15,512]{1,0:T(8,128)(2,1)S(1)}, bf16[15,512]{1,0:T(8,128)(2,1)S(1)}, u32[]{:S(2)}, u32[]{:S(2)}) collective-permute-start(bf16[15,512]{1,0:T(8,128)(2,1)S(1)} %get-tuple-element.367), channel_id=1, source_target_pairs={{0,1},{2,3},{4,5},{6,7},{8,9},{10,11},{12,13},{14,15},{16,17},{18,... | collective-permute-start | bytes 46088 | tf_op jit(solution)/shard_map/while/body/eval_jaxpr/ppermute | solution.py:20
  56.5 1.1 collective-permute-done.1
  58.3 1.0 reshape.290
  59.6 2.1 %fusion.72 = f32[3,32,4,128]{3,0,2,1:T(4,128)S(1)} fusion(f32[32,4,21,128]{3,0,1,2:T(8,128)S(1)} %convolution_bitcast_fusion.5, f32[6,3,21]{2,1,0:T(4,128)S(1)} %get-tuple-element.404, s32[]{:T(128)S(6)} %copy.92), kind=kOutput, calls=%fused_computation.4.clone.1 | convolution fusion | flops 12386304 | bytes 1574916 | tf_op jit(solution)/shard_map/while/body/eval_jaxpr/scbo,jb->jsco/dot_general | solution.py:119
  62.4 0.7 constant_dynamic-update-slice_fusion.2
  63.1 0.7 constant_dynamic-slice_fusion.5
  63.9 0.9 constant_dynamic-slice_fusion.6
  65.0 1.3 collective-permute-start
  66.3 4.5 %collective-permute-start.1 = (bf16[15,512]{1,0:T(8,128)(2,1)S(1)}, bf16[15,512]{1,0:T(8,128)(2,1)S(1)}, u32[]{:S(2)}, u32[]{:S(2)}) collective-permute-start(bf16[15,512]{1,0:T(8,128)(2,1)S(1)} %get-tuple-element.367), channel_id=1, source_target_pairs={{0,1},{2,3},{4,5},{6,7},{8,9},{10,11},{12,13},{14,15},{16,17},{18,... | collective-permute-start | bytes 46088 | tf_op jit(solution)/shard_map/while/body/eval_jaxpr/ppermute | solution.py:20
  71.2 1.1 collective-permute-done.1
  72.9 1.0 reshape.290
  74.3 2.1 %fusion.72 = f32[3,32,4,128]{3,0,2,1:T(4,128)S(1)} fusion(f32[32,4,21,128]{3,0,1,2:T(8,128)S(1)} %convolution_bitcast_fusion.5, f32[6,3,21]{2,1,0:T(4,128)S(1)} %get-tuple-element.404, s32[]{:T(128)S(6)} %copy.92), kind=kOutput, calls=%fused_computation.4.clone.1 | convolution fusion | flops 12386304 | bytes 1574916 | tf_op jit(solution)/shard_map/while/body/eval_jaxpr/scbo,jb->jsco/dot_general | solution.py:119
  77.0 0.7 constant_dynamic-update-slice_fusion.2
  77.7 0.7 constant_dynamic-slice_fusion.5
  78.6 0.9 constant_dynamic-slice_fusion.6
  79.6 1.3 collective-permute-start
  80.9 4.5 %collective-permute-start.1 = (bf16[15,512]{1,0:T(8,128)(2,1)S(1)}, bf16[15,512]{1,0:T(8,128)(2,1)S(1)}, u32[]{:S(2)}, u32[]{:S(2)}) collective-permute-start(bf16[15,512]{1,0:T(8,128)(2,1)S(1)} %get-tuple-element.367), channel_id=1, source_target_pairs={{0,1},{2,3},{4,5},{6,7},{8,9},{10,11},{12,13},{14,15},{16,17},{18,... | collective-permute-start | bytes 46088 | tf_op jit(solution)/shard_map/while/body/eval_jaxpr/ppermute | solution.py:20
  85.9 1.1 collective-permute-done.1
  87.6 1.0 reshape.290
  88.9 2.1 %fusion.72 = f32[3,32,4,128]{3,0,2,1:T(4,128)S(1)} fusion(f32[32,4,21,128]{3,0,1,2:T(8,128)S(1)} %convolution_bitcast_fusion.5, f32[6,3,21]{2,1,0:T(4,128)S(1)} %get-tuple-element.404, s32[]{:T(128)S(6)} %copy.92), kind=kOutput, calls=%fused_computation.4.clone.1 | convolution fusion | flops 12386304 | bytes 1574916 | tf_op jit(solution)/shard_map/while/body/eval_jaxpr/scbo,jb->jsco/dot_general | solution.py:119
  91.7 0.7 constant_dynamic-update-slice_fusion.2
  92.4 0.7 constant_dynamic-slice_fusion.5
  93.2 0.9 constant_dynamic-slice_fusion.6
  94.3 1.3 collective-permute-start
  95.6 4.5 %collective-permute-start.1 = (bf16[15,512]{1,0:T(8,128)(2,1)S(1)}, bf16[15,512]{1,0:T(8,128)(2,1)S(1)}, u32[]{:S(2)}, u32[]{:S(2)}) collective-permute-start(bf16[15,512]{1,0:T(8,128)(2,1)S(1)} %get-tuple-element.367), channel_id=1, source_target_pairs={{0,1},{2,3},{4,5},{6,7},{8,9},{10,11},{12,13},{14,15},{16,17},{18,... | collective-permute-start | bytes 46088 | tf_op jit(solution)/shard_map/while/body/eval_jaxpr/ppermute | solution.py:20
  100.5 1.1 collective-permute-done.1
  102.3 1.0 reshape.290
  103.6 2.1 %fusion.72 = f32[3,32,4,128]{3,0,2,1:T(4,128)S(1)} fusion(f32[32,4,21,128]{3,0,1,2:T(8,128)S(1)} %convolution_bitcast_fusion.5, f32[6,3,21]{2,1,0:T(4,128)S(1)} %get-tuple-element.404, s32[]{:T(128)S(6)} %copy.92), kind=kOutput, calls=%fused_computation.4.clone.1 | convolution fusion | flops 12386304 | bytes 1574916 | tf_op jit(solution)/shard_map/while/body/eval_jaxpr/scbo,jb->jsco/dot_general | solution.py:119
  106.3 0.7 constant_dynamic-update-slice_fusion.2
  107.1 0.7 constant_dynamic-slice_fusion.5
  107.9 0.9 constant_dynamic-slice_fusion.6
  109.0 1.3 collective-permute-start
  110.3 4.5 %collective-permute-start.1 = (bf16[15,512]{1,0:T(8,128)(2,1)S(1)}, bf16[15,512]{1,0:T(8,128)(2,1)S(1)}, u32[]{:S(2)}, u32[]{:S(2)}) collective-permute-start(bf16[15,512]{1,0:T(8,128)(2,1)S(1)} %get-tuple-element.367), channel_id=1, source_target_pairs={{0,1},{2,3},{4,5},{6,7},{8,9},{10,11},{12,13},{14,15},{16,17},{18,... | collective-permute-start | bytes 46088 | tf_op jit(solution)/shard_map/while/body/eval_jaxpr/ppermute | solution.py:20
  115.2 1.1 collective-permute-done.1
  116.9 1.0 reshape.290
  118.3 2.1 %fusion.72 = f32[3,32,4,128]{3,0,2,1:T(4,128)S(1)} fusion(f32[32,4,21,128]{3,0,1,2:T(8,128)S(1)} %convolution_bitcast_fusion.5, f32[6,3,21]{2,1,0:T(4,128)S(1)} %get-tuple-element.404, s32[]{:T(128)S(6)} %copy.92), kind=kOutput, calls=%fused_computation.4.clone.1 | convolution fusion | flops 12386304 | bytes 1574916 | tf_op jit(solution)/shard_map/while/body/eval_jaxpr/scbo,jb->jsco/dot_general | solution.py:119
  121.0 0.7 constant_dynamic-update-slice_fusion.2
  121.7 0.7 constant_dynamic-slice_fusion.5
  122.5 0.9 constant_dynamic-slice_fusion.6
  123.6 1.3 collective-permute-start
  124.9 4.5 %collective-permute-start.1 = (bf16[15,512]{1,0:T(8,128)(2,1)S(1)}, bf16[15,512]{1,0:T(8,128)(2,1)S(1)}, u32[]{:S(2)}, u32[]{:S(2)}) collective-permute-start(bf16[15,512]{1,0:T(8,128)(2,1)S(1)} %get-tuple-element.367), channel_id=1, source_target_pairs={{0,1},{2,3},{4,5},{6,7},{8,9},{10,11},{12,13},{14,15},{16,17},{18,... | collective-permute-start | bytes 46088 | tf_op jit(solution)/shard_map/while/body/eval_jaxpr/ppermute | solution.py:20
  129.8 1.1 collective-permute-done.1
  131.6 1.0 reshape.290
  132.9 2.1 %fusion.72 = f32[3,32,4,128]{3,0,2,1:T(4,128)S(1)} fusion(f32[32,4,21,128]{3,0,1,2:T(8,128)S(1)} %convolution_bitcast_fusion.5, f32[6,3,21]{2,1,0:T(4,128)S(1)} %get-tuple-element.404, s32[]{:T(128)S(6)} %copy.92), kind=kOutput, calls=%fused_computation.4.clone.1 | convolution fusion | flops 12386304 | bytes 1574916 | tf_op jit(solution)/shard_map/while/body/eval_jaxpr/scbo,jb->jsco/dot_general | solution.py:119
  135.7 0.7 constant_dynamic-update-slice_fusion.2
  136.4 1.0 reduce_sum.38
  137.4 1.0 reduce_sum.39
  (164 shorter events, 16.7 us)
Async XLA Ops:
  2.5 13.7 %all-to-all-start = ((bf16[6,16,2]{0,2,1:T(2,128)(2,1)}), bf16[6,16,2]{0,2,1:T(2,128)(2,1)S(1)}, u32[]{:S(2)}, u32[]{:S(2)}) async-start(bf16[6,16,2]{0,2,1:T(2,128)(2,1)} %bitcast), calls=%async_computation | async-start | bytes 16384 | tf_op jit(solution)/shard_map/all_to_all | solution.py:133
  11.0 8.9 %copy-start.2 = (bf16[6,16,8,128]{3,2,1,0:T(8,128)(2,1)S(1)}, bf16[6,16,8,128]{3,2,1,0:T(8,128)(2,1)}, u32[]{:S(2)}) copy-start(bf16[6,16,8,128]{3,2,1,0:T(8,128)(2,1)} %param.8) | copy-start | bytes 589828
  16.3 15.7 %all-to-all-start.1 = ((bf16[6,16,2,8,128]{4,3,2,0,1:T(8,128)(2,1)}), bf16[6,16,2,8,128]{4,3,2,0,1:T(8,128)(2,1)S(1)}, u32[]{:S(2)}, u32[]{:S(2)}) async-start(bf16[6,16,2,8,128]{4,3,2,0,1:T(8,128)(2,1)} %copy.31), calls=%async_computation.1 | async-start | bytes 786432 | tf_op jit(solution)/shard_map/all_to_all | solution.py:132
  19.9 16.3 %copy-start.3 = (bf16[2,21,31]{2,0,1:T(2,128)(2,1)S(1)}, bf16[2,21,31]{2,0,1:T(2,128)(2,1)}, u32[]{:S(2)}) copy-start(bf16[2,21,31]{2,0,1:T(2,128)(2,1)} %param.12) | copy-start | bytes 7816
  20.0 16.3 %copy-start.4 = (f32[1,6,3,21]{3,0,2,1:T(1,128)S(1)}, f32[1,6,3,21]{3,0,2,1:T(1,128)}, u32[]{:S(2)}) copy-start(f32[1,6,3,21]{3,0,2,1:T(1,128)} %param.13) | copy-start | bytes 4540
  32.0 16.4 %all-to-all-start.2 = ((bf16[6,16,2,8,128]{4,3,2,0,1:T(8,128)(2,1)}), bf16[6,16,2,8,128]{4,3,2,0,1:T(8,128)(2,1)}, u32[]{:S(2)}, u32[]{:S(2)}) async-start(bf16[6,16,2,8,128]{4,3,2,0,1:T(8,128)(2,1)} %copy.32), calls=%async_computation.2 | async-start | bytes 786432 | tf_op jit(solution)/shard_map/all_to_all | solution.py:131
  48.4 9.3 %copy-start = (bf16[158,2688]{1,0:T(8,128)(2,1)}, bf16[158,2688]{1,0:T(8,128)(2,1)S(1)}, u32[]{:S(2)}) copy-start(bf16[158,2688]{1,0:T(8,128)(2,1)S(1)} %get-tuple-element.406) | copy-start | bytes 2548228 | tf_op jit(solution)/shard_map/while
  50.3 6.2 %collective-permute-start = (bf16[15,512]{1,0:T(8,128)(2,1)S(1)}, bf16[15,512]{1,0:T(8,128)(2,1)S(1)}, u32[]{:S(2)}, u32[]{:S(2)}) collective-permute-start(bf16[15,512]{1,0:T(8,128)(2,1)S(1)} %get-tuple-element.366), channel_id=1, source_target_pairs={{1,0},{3,2},{5,4},{7,6},{9,8},{11,10},{13,12},{15,14},{17,16},{19,... | collective-permute-start | bytes 46088 | tf_op jit(solution)/shard_map/while/body/eval_jaxpr/ppermute | solution.py:21
  51.6 6.0 %collective-permute-start.1 = (bf16[15,512]{1,0:T(8,128)(2,1)S(1)}, bf16[15,512]{1,0:T(8,128)(2,1)S(1)}, u32[]{:S(2)}, u32[]{:S(2)}) collective-permute-start(bf16[15,512]{1,0:T(8,128)(2,1)S(1)} %get-tuple-element.367), channel_id=1, source_target_pairs={{0,1},{2,3},{4,5},{6,7},{8,9},{10,11},{12,13},{14,15},{16,17},{18,... | collective-permute-start | bytes 46088 | tf_op jit(solution)/shard_map/while/body/eval_jaxpr/ppermute | solution.py:20
  59.6 3.5 %copy-start.1 = (bf16[158,2688]{1,0:T(8,128)(2,1)S(1)}, bf16[158,2688]{1,0:T(8,128)(2,1)}, u32[]{:S(2)}) copy-start(bf16[158,2688]{1,0:T(8,128)(2,1)} %copy-done) | copy-start | bytes 2548228 | tf_op jit(solution)/shard_map/while
  63.1 9.3 %copy-start = (bf16[158,2688]{1,0:T(8,128)(2,1)}, bf16[158,2688]{1,0:T(8,128)(2,1)S(1)}, u32[]{:S(2)}) copy-start(bf16[158,2688]{1,0:T(8,128)(2,1)S(1)} %get-tuple-element.406) | copy-start | bytes 2548228 | tf_op jit(solution)/shard_map/while
  65.0 6.2 %collective-permute-start = (bf16[15,512]{1,0:T(8,128)(2,1)S(1)}, bf16[15,512]{1,0:T(8,128)(2,1)S(1)}, u32[]{:S(2)}, u32[]{:S(2)}) collective-permute-start(bf16[15,512]{1,0:T(8,128)(2,1)S(1)} %get-tuple-element.366), channel_id=1, source_target_pairs={{1,0},{3,2},{5,4},{7,6},{9,8},{11,10},{13,12},{15,14},{17,16},{19,... | collective-permute-start | bytes 46088 | tf_op jit(solution)/shard_map/while/body/eval_jaxpr/ppermute | solution.py:21
  66.3 6.0 %collective-permute-start.1 = (bf16[15,512]{1,0:T(8,128)(2,1)S(1)}, bf16[15,512]{1,0:T(8,128)(2,1)S(1)}, u32[]{:S(2)}, u32[]{:S(2)}) collective-permute-start(bf16[15,512]{1,0:T(8,128)(2,1)S(1)} %get-tuple-element.367), channel_id=1, source_target_pairs={{0,1},{2,3},{4,5},{6,7},{8,9},{10,11},{12,13},{14,15},{16,17},{18,... | collective-permute-start | bytes 46088 | tf_op jit(solution)/shard_map/while/body/eval_jaxpr/ppermute | solution.py:20
  74.3 3.5 %copy-start.1 = (bf16[158,2688]{1,0:T(8,128)(2,1)S(1)}, bf16[158,2688]{1,0:T(8,128)(2,1)}, u32[]{:S(2)}) copy-start(bf16[158,2688]{1,0:T(8,128)(2,1)} %copy-done) | copy-start | bytes 2548228 | tf_op jit(solution)/shard_map/while
  77.7 9.3 %copy-start = (bf16[158,2688]{1,0:T(8,128)(2,1)}, bf16[158,2688]{1,0:T(8,128)(2,1)S(1)}, u32[]{:S(2)}) copy-start(bf16[158,2688]{1,0:T(8,128)(2,1)S(1)} %get-tuple-element.406) | copy-start | bytes 2548228 | tf_op jit(solution)/shard_map/while
  79.6 6.2 %collective-permute-start = (bf16[15,512]{1,0:T(8,128)(2,1)S(1)}, bf16[15,512]{1,0:T(8,128)(2,1)S(1)}, u32[]{:S(2)}, u32[]{:S(2)}) collective-permute-start(bf16[15,512]{1,0:T(8,128)(2,1)S(1)} %get-tuple-element.366), channel_id=1, source_target_pairs={{1,0},{3,2},{5,4},{7,6},{9,8},{11,10},{13,12},{15,14},{17,16},{19,... | collective-permute-start | bytes 46088 | tf_op jit(solution)/shard_map/while/body/eval_jaxpr/ppermute | solution.py:21
  80.9 6.0 %collective-permute-start.1 = (bf16[15,512]{1,0:T(8,128)(2,1)S(1)}, bf16[15,512]{1,0:T(8,128)(2,1)S(1)}, u32[]{:S(2)}, u32[]{:S(2)}) collective-permute-start(bf16[15,512]{1,0:T(8,128)(2,1)S(1)} %get-tuple-element.367), channel_id=1, source_target_pairs={{0,1},{2,3},{4,5},{6,7},{8,9},{10,11},{12,13},{14,15},{16,17},{18,... | collective-permute-start | bytes 46088 | tf_op jit(solution)/shard_map/while/body/eval_jaxpr/ppermute | solution.py:20
  88.9 3.5 %copy-start.1 = (bf16[158,2688]{1,0:T(8,128)(2,1)S(1)}, bf16[158,2688]{1,0:T(8,128)(2,1)}, u32[]{:S(2)}) copy-start(bf16[158,2688]{1,0:T(8,128)(2,1)} %copy-done) | copy-start | bytes 2548228 | tf_op jit(solution)/shard_map/while
  92.4 9.3 %copy-start = (bf16[158,2688]{1,0:T(8,128)(2,1)}, bf16[158,2688]{1,0:T(8,128)(2,1)S(1)}, u32[]{:S(2)}) copy-start(bf16[158,2688]{1,0:T(8,128)(2,1)S(1)} %get-tuple-element.406) | copy-start | bytes 2548228 | tf_op jit(solution)/shard_map/while
  94.3 6.2 %collective-permute-start = (bf16[15,512]{1,0:T(8,128)(2,1)S(1)}, bf16[15,512]{1,0:T(8,128)(2,1)S(1)}, u32[]{:S(2)}, u32[]{:S(2)}) collective-permute-start(bf16[15,512]{1,0:T(8,128)(2,1)S(1)} %get-tuple-element.366), channel_id=1, source_target_pairs={{1,0},{3,2},{5,4},{7,6},{9,8},{11,10},{13,12},{15,14},{17,16},{19,... | collective-permute-start | bytes 46088 | tf_op jit(solution)/shard_map/while/body/eval_jaxpr/ppermute | solution.py:21
  95.6 6.0 %collective-permute-start.1 = (bf16[15,512]{1,0:T(8,128)(2,1)S(1)}, bf16[15,512]{1,0:T(8,128)(2,1)S(1)}, u32[]{:S(2)}, u32[]{:S(2)}) collective-permute-start(bf16[15,512]{1,0:T(8,128)(2,1)S(1)} %get-tuple-element.367), channel_id=1, source_target_pairs={{0,1},{2,3},{4,5},{6,7},{8,9},{10,11},{12,13},{14,15},{16,17},{18,... | collective-permute-start | bytes 46088 | tf_op jit(solution)/shard_map/while/body/eval_jaxpr/ppermute | solution.py:20
  103.6 3.5 %copy-start.1 = (bf16[158,2688]{1,0:T(8,128)(2,1)S(1)}, bf16[158,2688]{1,0:T(8,128)(2,1)}, u32[]{:S(2)}) copy-start(bf16[158,2688]{1,0:T(8,128)(2,1)} %copy-done) | copy-start | bytes 2548228 | tf_op jit(solution)/shard_map/while
  107.1 9.3 %copy-start = (bf16[158,2688]{1,0:T(8,128)(2,1)}, bf16[158,2688]{1,0:T(8,128)(2,1)S(1)}, u32[]{:S(2)}) copy-start(bf16[158,2688]{1,0:T(8,128)(2,1)S(1)} %get-tuple-element.406) | copy-start | bytes 2548228 | tf_op jit(solution)/shard_map/while
  109.0 6.2 %collective-permute-start = (bf16[15,512]{1,0:T(8,128)(2,1)S(1)}, bf16[15,512]{1,0:T(8,128)(2,1)S(1)}, u32[]{:S(2)}, u32[]{:S(2)}) collective-permute-start(bf16[15,512]{1,0:T(8,128)(2,1)S(1)} %get-tuple-element.366), channel_id=1, source_target_pairs={{1,0},{3,2},{5,4},{7,6},{9,8},{11,10},{13,12},{15,14},{17,16},{19,... | collective-permute-start | bytes 46088 | tf_op jit(solution)/shard_map/while/body/eval_jaxpr/ppermute | solution.py:21
  110.3 6.0 %collective-permute-start.1 = (bf16[15,512]{1,0:T(8,128)(2,1)S(1)}, bf16[15,512]{1,0:T(8,128)(2,1)S(1)}, u32[]{:S(2)}, u32[]{:S(2)}) collective-permute-start(bf16[15,512]{1,0:T(8,128)(2,1)S(1)} %get-tuple-element.367), channel_id=1, source_target_pairs={{0,1},{2,3},{4,5},{6,7},{8,9},{10,11},{12,13},{14,15},{16,17},{18,... | collective-permute-start | bytes 46088 | tf_op jit(solution)/shard_map/while/body/eval_jaxpr/ppermute | solution.py:20
  118.3 3.5 %copy-start.1 = (bf16[158,2688]{1,0:T(8,128)(2,1)S(1)}, bf16[158,2688]{1,0:T(8,128)(2,1)}, u32[]{:S(2)}) copy-start(bf16[158,2688]{1,0:T(8,128)(2,1)} %copy-done) | copy-start | bytes 2548228 | tf_op jit(solution)/shard_map/while
  121.7 9.3 %copy-start = (bf16[158,2688]{1,0:T(8,128)(2,1)}, bf16[158,2688]{1,0:T(8,128)(2,1)S(1)}, u32[]{:S(2)}) copy-start(bf16[158,2688]{1,0:T(8,128)(2,1)S(1)} %get-tuple-element.406) | copy-start | bytes 2548228 | tf_op jit(solution)/shard_map/while
  123.6 6.2 %collective-permute-start = (bf16[15,512]{1,0:T(8,128)(2,1)S(1)}, bf16[15,512]{1,0:T(8,128)(2,1)S(1)}, u32[]{:S(2)}, u32[]{:S(2)}) collective-permute-start(bf16[15,512]{1,0:T(8,128)(2,1)S(1)} %get-tuple-element.366), channel_id=1, source_target_pairs={{1,0},{3,2},{5,4},{7,6},{9,8},{11,10},{13,12},{15,14},{17,16},{19,... | collective-permute-start | bytes 46088 | tf_op jit(solution)/shard_map/while/body/eval_jaxpr/ppermute | solution.py:21
  124.9 6.0 %collective-permute-start.1 = (bf16[15,512]{1,0:T(8,128)(2,1)S(1)}, bf16[15,512]{1,0:T(8,128)(2,1)S(1)}, u32[]{:S(2)}, u32[]{:S(2)}) collective-permute-start(bf16[15,512]{1,0:T(8,128)(2,1)S(1)} %get-tuple-element.367), channel_id=1, source_target_pairs={{0,1},{2,3},{4,5},{6,7},{8,9},{10,11},{12,13},{14,15},{16,17},{18,... | collective-permute-start | bytes 46088 | tf_op jit(solution)/shard_map/while/body/eval_jaxpr/ppermute | solution.py:20
  132.9 3.5 %copy-start.1 = (bf16[158,2688]{1,0:T(8,128)(2,1)S(1)}, bf16[158,2688]{1,0:T(8,128)(2,1)}, u32[]{:S(2)}) copy-start(bf16[158,2688]{1,0:T(8,128)(2,1)} %copy-done) | copy-start | bytes 2548228 | tf_op jit(solution)/shard_map/while
where the time goes:
time: 140 us; the launch traced here: 139 us
  starting transfers between devices  50.2 us (36%)
  waiting for transfers between devices  31.3 us (22%)
  local copies, waits for them, and re-layouts  25.8 us (18%)
  matrix products  21.8 us (16%)
  other arithmetic  9.09 us (6%)
    ppermute x6, starting transfers between devices, extended(): before = lax.ppermute(last, axis, up)  27.3 us
    dot_general x6, matrix products, one_visit(): jnp.einsum('scbo,jb->jsco', smoothed, spatial_row, precision=lax.Precisio...  12.5 us
    all_to_all x1, waiting for transfers between devices, per_device(): lax.all_to_all(send_weight, 'patch', split_axis=1, concat_axis=1, tiled=T...  10.8 us
    all_to_all x1, waiting for transfers between devices, per_device(): lax.all_to_all(send_flux, 'patch', split_axis=1, concat_axis=1, tiled=True)  10 us
    dynamic_slice x12, local copies, waits for them, and re-layouts, per_device(): lax.map(one_visit, (flux_in, weight_in, block_in, spatial[0]))  9.47 us
    ppermute x6, starting transfers between devices, extended(): after = lax.ppermute(leading, axis, down)  7.75 us
    all_to_all x1, starting transfers between devices, per_device(): lax.all_to_all(send_block, 'patch', split_axis=1, concat_axis=1, tiled=True)  7.39 us
    ppermute x6, waiting for transfers between devices, extended(): before = lax.ppermute(last, axis, up)  6.38 us
  transfers between devices with their start and end apart: 15, of which 9 were waited for; matrix products, arithmetic and copies ran while one was open for 6% of the time, Pallas kernels for 0%

commit v1 on v0

v1 whole, which is shorter than its diff:
```python
import jax
import jax.numpy as jnp
from jax import lax
from jax.experimental import pallas as pl
from jax.experimental.pallas import tpu as pltpu
from jax.sharding import PartitionSpec as P

BASIS = 21
GROUPS = 24
TAPS = 31
MARGIN = TAPS // 2
ROWS = 32
COLS = 512
TILE_ROWS = 8
LANES = 128
ACROSS = COLS // LANES
DOWN = ROWS // TILE_ROWS
CAP = 2
HALO = 16
PAIR = 2 * LANES
F32 = jnp.float32
BF16 = jnp.bfloat16
I32 = jnp.int32


def iota(shape, dim):
    return lax.broadcasted_iota(I32, shape, dim)


def vmem():
    return pl.BlockSpec(memory_space=pltpu.VMEM)


def smem():
    return pl.BlockSpec(memory_space=pltpu.SMEM)


def params():
    return pltpu.CompilerParams(vmem_limit_bytes=40 * 1024 * 1024)


def cost(flops, moved):
    return pl.CostEstimate(flops=flops, bytes_accessed=moved, transcendentals=0)


def slots_of(dest):
    count = dest.shape[1]
    lane = iota(dest.shape, 1)
    ordinal = jnp.zeros(dest.shape, I32)
    for t in range(count - 1):
        same = jnp.logical_and(dest == dest[:, t : t + 1], lane > t)
        ordinal = ordinal + jnp.where(same, 1, 0)
    return dest * CAP + ordinal, ordinal


def spread(values, width, repeat):
    m = values.shape[1]
    hot = (iota((m, width), 1) // repeat == iota((m, width), 0)).astype(F32).astype(BF16)
    return jnp.dot(values.astype(F32).astype(BF16), hot, preferred_element_type=F32).astype(I32)


def pack(dest, tiles_ref, out_ref):
    visits, depth, _ = tiles_ref.shape
    patches = out_ref.shape[0]
    block = CAP * TILE_ROWS
    slot, _ = slots_of(dest)
    goal = spread(slot, depth, TILE_ROWS) * TILE_ROWS + iota((visits, depth), 1) % TILE_ROWS
    row = iota((patches * block, depth), 0)
    for k in range(visits):
        hot = jnp.where(row == goal[k : k + 1], 1.0, 0.0).astype(BF16)
        moved = jnp.dot(hot, tiles_ref[k], preferred_element_type=F32).astype(BF16)
        out_ref[:, k * block : (k + 1) * block, :] = moved.reshape(patches, block, LANES)


def pack_flux_kernel(me_ref, dest_ref, block_ref, tiles_ref, out_ref):
    dest = dest_ref[...]
    visits = dest.shape[0]
    patches = out_ref.shape[0]
    pack(dest, tiles_ref, out_ref)
    _, ordinal = slots_of(dest)
    place = block_ref[...] % ACROSS * DOWN + block_ref[...] // ACROSS + 1
    lane = iota((TILE_ROWS, LANES), 1)
    first = CAP * me_ref[0]
    for q in range(patches):
        note = jnp.zeros((TILE_ROWS, LANES), F32)
        for o in range(CAP):
            chosen = jnp.logical_and(dest == q, ordinal == o)
            value = jnp.sum(jnp.where(chosen, place, 0).astype(F32), axis=1, keepdims=True)
            value = jnp.concatenate([value, jnp.zeros((TILE_ROWS - visits, 1), F32)], axis=0)
            note = jnp.where(lane == first + o, value, note)
        out_ref[q, visits * CAP * TILE_ROWS :, :] = note.astype(BF16)


def pack_weight_kernel(dest_ref, tiles_ref, out_ref):
    pack(dest_ref[...], tiles_ref, out_ref)


def placing(note, senders):
    width = senders * CAP * TILE_ROWS
    hot = (iota((LANES, width), 1) // TILE_ROWS == iota((LANES, width), 0)).astype(F32).astype(BF16)
    place = jnp.dot(note.astype(BF16), hot, preferred_element_type=F32).astype(I32) - 1
    return place * TILE_ROWS + iota((TILE_ROWS, width), 1) % TILE_ROWS


def placed(goal, received):
    hot = jnp.where(iota((ACROSS * ROWS, goal.shape[1]), 0) == goal, 1.0, 0.0).astype(BF16)
    return jnp.dot(hot, received, preferred_element_type=F32)


def place_kernel(recv_ref, frame_ref, top_ref, bottom_ref, note_ref):
    senders = recv_ref.shape[0]
    visits = frame_ref.shape[0]
    block = CAP * TILE_ROWS
    note = jnp.sum(recv_ref[:, visits * block :, :].astype(F32), axis=0)
    note_ref[...] = note
    goal = placing(note, senders)
    for k in range(visits):
        received = recv_ref[:, k * block : (k + 1) * block, :].reshape(senders * block, LANES)
        frame = placed(goal[k : k + 1], received).astype(BF16).reshape(ACROSS, ROWS, LANES)
        frame_ref[k] = frame
        top_ref[k] = frame[:, :HALO]
        bottom_ref[k] = frame[:, ROWS - HALO :]


def hot_rows(taps, shift_lane, width, used=None):
    lane = iota((TAPS, width), 1)
    tap = iota((TAPS, width), 0)
    hot = lane == shift_lane(tap)
    if used is not None:
        hot = jnp.logical_and(hot, used(tap))
    hot = hot.astype(F32).astype(BF16)
    return jnp.dot(taps, hot, preferred_element_type=F32)


def table_kernel(first_ref, up_ref, column_ref, row_ref, spatial_ref, coord_ref, table_ref, own_ref, halo_ref):
    low = LANES // 2 - MARGIN
    lines = hot_rows(column_ref[...], lambda tap: (-low - tap) % LANES, LANES)
    gap = iota((PAIR, LANES), 0) - iota((PAIR, LANES), 1) - low
    inside = jnp.logical_and(gap >= 0, gap < TAPS)
    for b in range(table_ref.shape[1] // LANES):
        if b < BASIS:
            line = jnp.broadcast_to(lines[b : b + 1], (PAIR, LANES))
            rolled = pltpu.roll(line, 0, 1, stride=1, stride_axis=0)
            part = jnp.where(inside, rolled, 0.0)
        else:
            part = jnp.zeros((PAIR, LANES), F32)
        table_ref[:, b * LANES : (b + 1) * LANES] = part.astype(BF16)

    visits = own_ref.shape[0]
    coord = coord_ref[...]
    spatial = spatial_ref[...]

    def fill(out_ref, height, offset, used=None):
        fit = LANES // height
        line = 0.0
        which = iota((GROUPS, LANES), 0)
        for j in range(fit):
            part = hot_rows(
                row_ref[...], lambda tap: (height * j + tap - offset + 2 * LANES) % LANES, LANES, used
            )
            line = line + jnp.where(which % fit == j, part, 0.0)
        t = iota((ROWS, LANES), 1) % height
        tap = t - iota((ROWS, LANES), 0) + offset
        good = jnp.logical_and(tap >= 0, tap < TAPS)
        width = GROUPS * height
        hot = (iota((BASIS, width), 1) // height == iota((BASIS, width), 0)).astype(F32)
        coef = jnp.dot(spatial, hot, precision=lax.Precision.HIGHEST, preferred_element_type=F32)
        for g in range(GROUPS // fit):
            here = jnp.sum(line[g * fit : (g + 1) * fit], axis=0, keepdims=True)
            rolled = pltpu.roll(jnp.broadcast_to(here, (ROWS, LANES)), 0, 1, stride=1, stride_axis=0)
            taps = jnp.where(good, rolled, 0.0)
            lanes = slice(g * LANES, (g + 1) * LANES)
            for k in range(visits):
                c = coef[3 * k : 3 * k + 3, lanes]
                out_ref[k, :ROWS, lanes] = ((c[0:1] + coord * c[1:2]) * taps).astype(BF16)
                out_ref[k, ROWS:, lanes] = (c[2:3] * taps).astype(BF16)

    fill(own_ref, ROWS, MARGIN)
    up = up_ref[0] > 0
    low = jnp.where(up, 0, MARGIN + 1)
    fill(
        halo_ref,
        HALO,
        jnp.where(up, MARGIN - HALO, MARGIN + ROWS),
        lambda tap: jnp.logical_and(tap >= low, tap < low + MARGIN),
    )


def filter_kernel(frame_ref, table_ref, mix_ref, out_ref, windows, filtered):
    visits, _, height, _ = frame_ref.shape
    half = LANES // 2
    left = iota((height, LANES), 1) < half
    count = ACROSS * height
    for k in range(visits):
        rolled = [pltpu.roll(frame_ref[k, c].astype(F32), half, 1) for c in range(ACROSS)]
        zero = jnp.zeros((height, LANES), F32)
        padded = [zero] + rolled + [zero]
        pieces = [jnp.where(left, padded[c], padded[c + 1]).astype(BF16) for c in range(ACROSS + 1)]
        for c in range(ACROSS):
            rows = slice(k * count + c * height, k * count + (c + 1) * height)
            windows[rows, :LANES] = pieces[c]
            windows[rows, LANES:] = pieces[c + 1]
    done = table_ref.shape[1] // LANES
    filtered[:, done * height :, :] = jnp.zeros((visits, filtered.shape[1] - done * height, COLS), BF16)
    for p in range(done // 2):
        part = jnp.dot(windows[...], table_ref[:, p * PAIR : (p + 1) * PAIR], preferred_element_type=F32).astype(BF16)
        for k in range(visits):
            for c in range(ACROSS):
                for j in range(2):
                    b = 2 * p + j
                    filtered[k, b * height : (b + 1) * height, c * LANES : (c + 1) * LANES] = part[
                        k * count + c * height : k * count + (c + 1) * height, j * LANES : (j + 1) * LANES
                    ]
    col = (2.0 * iota((1, COLS), 1).astype(F32) + 1.0) / COLS - 1.0
    for k in range(visits):
        both = jnp.dot(mix_ref[k], filtered[k], preferred_element_type=F32)
        out_ref[k] = both[:ROWS] + col * both[ROWS:]


def final_kernel(note_ref, recv_ref, *refs):
    parts, out_ref = refs[:-1], refs[-1]
    senders = recv_ref.shape[0]
    visits = parts[0].shape[0]
    block = CAP * TILE_ROWS
    goal = placing(note_ref[...], senders)
    total = jnp.zeros((ACROSS * ROWS, LANES), F32)
    sums = [jnp.zeros((ROWS, LANES), F32) for _ in range(ACROSS)]
    for k in range(visits):
        received = recv_ref[:, k * block : (k + 1) * block, :].reshape(senders * block, LANES)
        weight = placed(goal[k : k + 1], received)
        total = total + weight
        for c in range(ACROSS):
            lanes = slice(c * LANES, (c + 1) * LANES)
            value = parts[0][k, :, lanes]
            for other in parts[1:]:
                value = value + other[k, :, lanes]
            sums[c] = sums[c] + weight[c * ROWS : (c + 1) * ROWS] * value
    for c in range(ACROSS):
        out_ref[0, :, c * LANES : (c + 1) * LANES] = sums[c] / total[c * ROWS : (c + 1) * ROWS]


def shape(dims, kind):
    return jax.ShapeDtypeStruct(dims, kind)


def filter_rows(frame, table, mix, name):
    visits, _, height, _ = frame.shape
    return pl.pallas_call(
        filter_kernel,
        out_shape=shape((visits, ROWS, COLS), F32),
        in_specs=[vmem()] * 3,
        out_specs=vmem(),
        scratch_shapes=[
            pltpu.VMEM((visits * ACROSS * height, PAIR), BF16),
            pltpu.VMEM((visits, GROUPS * height, COLS), BF16),
        ],
        compiler_params=params(),
        cost_estimate=cost(4 * visits * ACROSS * height * PAIR * BASIS * LANES, 4 * 1024 * 1024),
        name=name,
    )(frame, table, mix)


def per_device(tile_flux, tile_weight, dest_patch, dest_block, basis, spatial):
    visits, tile_count, tile_height, tile_width = tile_flux.shape
    patches, bands = lax.axis_size("patch"), lax.axis_size("band")
    me, band = lax.axis_index("patch"), lax.axis_index("band")
    depth = tile_count * tile_height
    block = CAP * TILE_ROWS
    flux = tile_flux.reshape(visits, depth, tile_width)
    weight = tile_weight.reshape(visits, depth, tile_width)
    send_flux = pl.pallas_call(
        pack_flux_kernel,
        out_shape=shape((patches, visits * block + TILE_ROWS, LANES), BF16),
        in_specs=[smem()] + [vmem()] * 3,
        out_specs=vmem(),
        compiler_params=params(),
        name="pack_flux",
    )(me.reshape(1), dest_patch, dest_block, flux)
    send_weight = pl.pallas_call(
        pack_weight_kernel,
        out_shape=shape((patches, visits * block, LANES), BF16),
        in_specs=[vmem()] * 2,
        out_specs=vmem(),
        compiler_params=params(),
        name="pack_weight",
    )(dest_patch, weight)
    recv_flux = lax.all_to_all(send_flux, "patch", split_axis=0, concat_axis=0, tiled=True)
    recv_weight = lax.all_to_all(send_weight, "patch", split_axis=0, concat_axis=0, tiled=True)

    row = (band * ROWS).astype(F32) + jnp.arange(ROWS, dtype=F32)
    coord = jnp.broadcast_to(((2.0 * row + 1.0) / (ROWS * bands) - 1.0)[:, None], (ROWS, LANES))
    taps = jnp.pad(basis, ((0, 0), (0, GROUPS - BASIS), (0, 0)))
    coefs = spatial[0].reshape(visits * 3, BASIS)

    def tables(up):
        return pl.pallas_call(
            table_kernel,
            out_shape=(
                shape((PAIR, 2 * pl.cdiv(BASIS, 2) * LANES), BF16),
                shape((visits, 2 * ROWS, GROUPS * ROWS), BF16),
                shape((visits, 2 * ROWS, GROUPS * HALO), BF16),
            ),
            in_specs=[smem()] * 2 + [vmem()] * 4,
            out_specs=(vmem(),) * 3,
            compiler_params=params(),
            cost_estimate=cost(10**9, 4 * 1024 * 1024),
            name="tables",
        )(band.reshape(1), up.reshape(1).astype(I32), taps[0], taps[1], coefs, coord)

    frame, top, bottom, note = pl.pallas_call(
        place_kernel,
        out_shape=(
            shape((visits, ACROSS, ROWS, LANES), BF16),
            shape((visits, ACROSS, HALO, LANES), BF16),
            shape((visits, ACROSS, HALO, LANES), BF16),
            shape((TILE_ROWS, LANES), F32),
        ),
        in_specs=[vmem()],
        out_specs=(vmem(),) * 4,
        compiler_params=params(),
        name="place_flux",
    )(recv_flux)

    if bands == 2:
        edge = jnp.where(band == 0, bottom, top)
        halos = [lax.ppermute(edge, "band", [(0, 1), (1, 0)])]
        ups = [band]
    else:
        down = [(i, i + 1) for i in range(bands - 1)]
        halos = [
            lax.ppermute(bottom, "band", down),
            lax.ppermute(top, "band", [(j, i) for i, j in down]),
        ]
        ups = [jnp.int32(1), jnp.int32(0)]
    built = [tables(up) for up in ups]
    table, own_mix, _ = built[0]
    parts = [filter_rows(frame, table, own_mix, "filter_own")]
    for halo, (_, _, halo_mix) in zip(halos, built):
        parts.append(filter_rows(halo, table, halo_mix, "filter_halo"))
    return pl.pallas_call(
        final_kernel,
        out_shape=shape((1, ROWS, COLS), F32),
        in_specs=[vmem()] * (2 + len(parts)),
        out_specs=vmem(),
        compiler_params=params(),
        name="final",
    )(note, recv_weight, *parts)


def solution(mesh):
    in_specs = (
        P(None, ("patch", "band"), None, None),
        P(None, ("patch", "band"), None, None),
        P(None, ("patch", "band")),
        P(None, ("patch", "band")),
        P(),
        P("patch", None, None, None),
    )
    out_specs = P("patch", "band", None)
    return jax.shard_map(
        per_device, mesh=mesh, in_specs=in_specs, out_specs=out_specs, check_vma=False
    )
```

time: 140 us -> 41 us (0.29)
  starting transfers between devices: 50.2 us -> 12.6 us
  local copies, waits for them, and re-layouts: 25.8 us -> 2.43 us
  matrix products: 21.8 us -> 0 us
  waiting for transfers between devices: 31.3 us -> 17.4 us
  other arithmetic: 9.09 us -> 0.07 us
  Pallas kernels: 0 us -> 7.97 us
    ppermute x12 -> x1, starting transfers between devices: 35 us -> 1.56 us  [per_device(): halos = [lax.ppermute(edge, 'band', [(0, 1), (1, 0)])]]
    dot_general x34 -> x0, matrix products: 21.8 us -> none  [the longest x6 12.5 us: one_visit(): jnp.einsum('scbo,jb->jsco', smoothed, spatial_row, precision=lax.Precisio...]
    dynamic_slice x12 -> x0, local copies, waits for them, and re-layouts: 9.47 us -> none  [per_device(): lax.map(one_visit, (flux_in, weight_in, block_in, spatial[0]))]
    all_to_all x3 -> x2, waiting for transfers between devices: 24.9 us -> 15.9 us  [the longest x1 11.4 us: per_device(): lax.all_to_all(send_flux, 'patch', split_axis=0, concat_axis=0, tiled=True)]
    reshape x16 -> x0, local copies, waits for them, and re-layouts: 8.63 us -> none  [the longest x6 5.82 us: column_filter(): result.astype(jnp.bfloat16)]
    pallas_call x0 -> x7, Pallas kernels: none -> 7.97 us  [the longest x2 3.29 us: filter_rows(): pl.pallas_call(filter_kernel, out_shape=shape((visits, ROWS, COLS), F32),...]
    ppermute x12 -> x1, waiting for transfers between devices: 6.4 us -> 1.54 us  [per_device(): halos = [lax.ppermute(edge, 'band', [(0, 1), (1, 0)])]]
    dynamic_update_slice x6 -> x0, other arithmetic: 4.24 us -> none  [per_device(): lax.map(one_visit, (flux_in, weight_in, block_in, spatial[0]))]
  transfers between devices with their start and end apart: 15 -> 3, of which waited for: 9 -> 3; matrix products, arithmetic and copies ran while one was open for 6% -> 0% of each run, Pallas kernels for 0% -> 14%
where the time goes in v1:
time: 41 us; the launch traced here: 40.6 us
  waiting for transfers between devices  17.4 us (42%)
  starting transfers between devices  12.6 us (31%)
  Pallas kernels  7.97 us (19%)
  local copies, waits for them, and re-layouts  2.43 us (6%)
    all_to_all x1, waiting for transfers between devices, per_device(): lax.all_to_all(send_flux, 'patch', split_axis=0, concat_axis=0, tiled=True)  11.4 us
    all_to_all x1, starting transfers between devices, per_device(): lax.all_to_all(send_flux, 'patch', split_axis=0, concat_axis=0, tiled=True)  7.39 us
    all_to_all x1, waiting for transfers between devices, per_device(): lax.all_to_all(send_weight, 'patch', split_axis=0, concat_axis=0, tiled=T...  4.45 us
    all_to_all x1, starting transfers between devices, per_device(): lax.all_to_all(send_weight, 'patch', split_axis=0, concat_axis=0, tiled=T...  3.7 us
    pallas_call x2, Pallas kernels, filter_rows(): pl.pallas_call(filter_kernel, out_shape=shape((visits, ROWS, COLS), F32),...  3.29 us
    unnamed x15, local copies, waits for them, and re-layouts  2.33 us
    ppermute x1, starting transfers between devices, per_device(): halos = [lax.ppermute(edge, 'band', [(0, 1), (1, 0)])]  1.56 us
    ppermute x1, waiting for transfers between devices, per_device(): halos = [lax.ppermute(edge, 'band', [(0, 1), (1, 0)])]  1.54 us
  transfers between devices with their start and end apart: 3, of which 3 were waited for; matrix products, arithmetic and copies ran while one was open for 0% of the time, Pallas kernels for 14%

profile of v1, /device:TPU:0, one launch (start us, length us, event | category | flops | bytes accessed | tf_op | source)
XLA Modules:
  0.0 40.6 jit_solution(17064530062998679064)
XLA Ops:
  0.0 0.0 copy-start.3
  0.0 0.0 copy-start
  0.0 0.9 %copy-done = bf16[6,16,8,128]{3,2,1,0:T(8,128)(2,1)S(1)} copy-done((bf16[6,16,8,128]{3,2,1,0:T(8,128)(2,1)S(1)}, bf16[6,16,8,128]{3,2,1,0:T(8,128)(2,1)}, u32[]{:S(2)}) %copy-start) | copy-done | bytes 196632
  0.9 0.0 copy-start.2
  0.9 0.7 %copy-done.2 = s32[6,16]{1,0:T(8,128)S(1)} copy-done((s32[6,16]{1,0:T(8,128)S(1)}, s32[6,16]{1,0:T(8,128)}, u32[]{:S(2)}) %copy-start.2) | copy-done | bytes 408
  1.6 0.0 copy-start.4
  1.6 0.7 %copy-done.4 = s32[6,16]{1,0:T(8,128)S(1)} copy-done((s32[6,16]{1,0:T(8,128)S(1)}, s32[6,16]{1,0:T(8,128)}, u32[]{:S(2)}) %copy-start.4) | copy-done | bytes 408
  2.3 0.0 copy-start.1
  2.3 0.0 copy-start.5
  2.3 0.0 copy-start.6
  2.3 1.3 %pack_flux.1 = bf16[16,104,128]{2,1,0:T(8,128)(2,1)} custom-call(s32[1]{0:T(128)} %bitcast.me_ref, s32[6,16]{1,0:T(8,128)S(1)} %copy-done.2, s32[6,16]{1,0:T(8,128)S(1)} %copy-done.4, bf16[6,128,128]{2,1,0:T(8,128)(2,1)S(1)} %bitcast.8), custom_call_target="tpu_custom_call" | custom-call | tf_op jit(solution)/shard_map/pack_flux/pallas_call | solution.py:271
  3.6 7.4 %all-to-all-start = ((bf16[16,104,128]{2,1,0:T(8,128)(2,1)}), bf16[16,104,128]{2,1,0:T(8,128)(2,1)S(1)}, u32[]{:S(2)}, u32[]{:S(2)}) async-start(bf16[16,104,128]{2,1,0:T(8,128)(2,1)} %pack_flux.1), calls=%async_computation | async-start | bytes 851968 | tf_op jit(solution)/shard_map/all_to_all | solution.py:287
  11.0 0.0 copy-done.3
  11.0 0.0 copy-done.1
  11.0 1.3 %pack_weight.1 = bf16[16,96,128]{2,1,0:T(8,128)(2,1)} custom-call(s32[6,16]{1,0:T(8,128)S(1)} %copy-done.3, bf16[6,128,128]{2,1,0:T(8,128)(2,1)S(1)} %bitcast.9), custom_call_target="tpu_custom_call" | custom-call | tf_op jit(solution)/shard_map/pack_weight/pallas_call | solution.py:279
  12.3 11.4 %all-to-all-done.recv_ref = bf16[16,104,128]{2,1,0:T(8,128)(2,1)S(1)} async-done(((bf16[16,104,128]{2,1,0:T(8,128)(2,1)}), bf16[16,104,128]{2,1,0:T(8,128)(2,1)S(1)}, u32[]{:S(2)}, u32[]{:S(2)}) %all-to-all-start) | async-done | bytes 426016 | tf_op jit(solution)/shard_map/all_to_all | solution.py:287
  23.7 3.7 %all-to-all-start.1 = ((bf16[16,96,128]{2,1,0:T(8,128)(2,1)}), bf16[16,96,128]{2,1,0:T(8,128)(2,1)S(1)}, u32[]{:S(2)}, u32[]{:S(2)}) async-start(bf16[16,96,128]{2,1,0:T(8,128)(2,1)} %pack_weight.1), calls=%async_computation.1 | async-start | bytes 786432 | tf_op jit(solution)/shard_map/all_to_all | solution.py:288
  27.4 0.0 copy-done.5
  27.5 0.0 copy-done.6
  27.5 0.1 broadcast_in_dim.2.coord_ref
  27.6 0.7 %tables.1 = (bf16[256,2816]{1,0:T(8,128)(2,1)S(1)}, bf16[6,64,768]{2,1,0:T(8,128)(2,1)S(1)}, bf16[6,64,384]{2,1,0:T(8,128)(2,1)S(1)}) custom-call(s32[1]{0:T(128)} %bitcast.3.first_ref.up_ref, s32[1]{0:T(128)} %bitcast.3.first_ref.up_ref, bf16[24,31]{1,0:T(8,128)(2,1)S(1)} %get-tuple-element.20.column_ref, bf16[24,31]{1,0:T(8,128)(2,1)S(1)} %get-tuple-element.19.row_ref, ...), custom_call_target="tpu_custom_call" | custom-call | flops 1000000000 | bytes 4194304 | tf_op jit(solution)/shard_map/tables/pallas_call | solution.py:296
  28.4 0.4 place_flux.1
  28.8 1.6 %collective-permute-start = (bf16[6,4,16,128]{3,2,1,0:T(8,128)(2,1)S(1)}, bf16[6,4,16,128]{3,2,1,0:T(8,128)(2,1)S(1)}, u32[]{:S(2)}, u32[]{:S(2)}) collective-permute-start(bf16[6,4,16,128]{3,2,1,0:T(8,128)(2,1)S(1)} %broadcast_select_fusion), channel_id=1, source_target_pairs={{0,1},{1,0},{2,3},{3,2},{4,5},{5,4},{6,7},{7,6},{8,9},{9,8},{10,11... | collective-permute-start | bytes 294920 | tf_op jit(solution)/shard_map/ppermute | solution.py:326
  30.3 2.1 %filter_own.1.refs_0_ = f32[6,32,512]{2,1,0:T(8,128)S(1)} custom-call(bf16[6,4,32,128]{3,2,1,0:T(8,128)(2,1)S(1)} %get-tuple-element.13.frame_ref, bf16[256,2816]{1,0:T(8,128)(2,1)S(1)} %get-tuple-element.14.table_ref, bf16[6,64,768]{2,1,0:T(8,128)(2,1)S(1)} %get-tuple-element.15.mix_ref), custom_call_target="tpu_custom_call" | custom-call | flops 2113929216 | bytes 4194304 | tf_op jit(solution)/shard_map/filter_own/pallas_call | solution.py:248
  32.4 1.5 %collective-permute-done.frame_ref = bf16[6,4,16,128]{3,2,1,0:T(8,128)(2,1)S(1)} collective-permute-done((bf16[6,4,16,128]{3,2,1,0:T(8,128)(2,1)S(1)}, bf16[6,4,16,128]{3,2,1,0:T(8,128)(2,1)S(1)}, u32[]{:S(2)}, u32[]{:S(2)}) %collective-permute-start) | collective-permute-done | bytes 98336 | tf_op jit(solution)/shard_map/ppermute | solution.py:326
  34.0 1.2 %filter_halo.1.refs_1_ = f32[6,32,512]{2,1,0:T(8,128)S(1)} custom-call(bf16[6,4,16,128]{3,2,1,0:T(8,128)(2,1)S(1)} %collective-permute-done.frame_ref, bf16[256,2816]{1,0:T(8,128)(2,1)S(1)} %get-tuple-element.14.table_ref, bf16[6,64,384]{2,1,0:T(8,128)(2,1)S(1)} %get-tuple-element.18.mix_ref), custom_call_target="tpu_custom_call" | custom-call | flops 1056964608 | bytes 4194304 | tf_op jit(solution)/shard_map/filter_halo/pallas_call | solution.py:248
  35.2 4.4 %all-to-all-done.1.recv_ref = bf16[16,96,128]{2,1,0:T(8,128)(2,1)S(1)} async-done(((bf16[16,96,128]{2,1,0:T(8,128)(2,1)}), bf16[16,96,128]{2,1,0:T(8,128)(2,1)S(1)}, u32[]{:S(2)}, u32[]{:S(2)}) %all-to-all-start.1) | async-done | bytes 393248 | tf_op jit(solution)/shard_map/all_to_all | solution.py:288
  39.6 1.0 %final.1 = f32[1,32,512]{2,1,0:T(8,128)} custom-call(f32[8,128]{1,0:T(8,128)S(1)} %get-tuple-element.12.note_ref, bf16[16,96,128]{2,1,0:T(8,128)(2,1)S(1)} %all-to-all-done.1.recv_ref, f32[6,32,512]{2,1,0:T(8,128)S(1)} %filter_own.1.refs_0_, f32[6,32,512]{2,1,0:T(8,128)S(1)} %filter_halo.1.refs_1_), custom_call_target="tpu_custom_call" | custom-call | tf_op jit(solution)/shard_map/final/pallas_call | solution.py:340
  (6 shorter events, 0.1 us)
Async XLA Ops:
  0.0 11.0 %copy-start.3 = (s32[6,16]{1,0:T(8,128)S(1)}, s32[6,16]{1,0:T(8,128)}, u32[]{:S(2)}) copy-start(s32[6,16]{1,0:T(8,128)} %dest_ref.3) | copy-start | bytes 1156
  0.0 0.9 %copy-start = (bf16[6,16,8,128]{3,2,1,0:T(8,128)(2,1)S(1)}, bf16[6,16,8,128]{3,2,1,0:T(8,128)(2,1)}, u32[]{:S(2)}) copy-start(bf16[6,16,8,128]{3,2,1,0:T(8,128)(2,1)} %param.6) | copy-start | bytes 589828
  0.9 0.7 %copy-start.2 = (s32[6,16]{1,0:T(8,128)S(1)}, s32[6,16]{1,0:T(8,128)}, u32[]{:S(2)}) copy-start(s32[6,16]{1,0:T(8,128)} %dest_ref.3) | copy-start | bytes 1156
  1.6 0.7 %copy-start.4 = (s32[6,16]{1,0:T(8,128)S(1)}, s32[6,16]{1,0:T(8,128)}, u32[]{:S(2)}) copy-start(s32[6,16]{1,0:T(8,128)} %block_ref.1) | copy-start | bytes 1156
  2.3 8.7 %copy-start.1 = (bf16[6,16,8,128]{3,2,1,0:T(8,128)(2,1)S(1)}, bf16[6,16,8,128]{3,2,1,0:T(8,128)(2,1)}, u32[]{:S(2)}) copy-start(bf16[6,16,8,128]{3,2,1,0:T(8,128)(2,1)} %param.7) | copy-start | bytes 589828
  2.3 25.1 %copy-start.5 = (bf16[2,21,31]{2,0,1:T(2,128)(2,1)S(1)}, bf16[2,21,31]{2,0,1:T(2,128)(2,1)}, u32[]{:S(2)}) copy-start(bf16[2,21,31]{2,0,1:T(2,128)(2,1)} %param.10) | copy-start | bytes 7816
  2.3 25.1 %copy-start.6 = (f32[1,6,3,21]{3,0,2,1:T(1,128)S(1)}, f32[1,6,3,21]{3,0,2,1:T(1,128)}, u32[]{:S(2)}) copy-start(f32[1,6,3,21]{3,0,2,1:T(1,128)} %param.11) | copy-start | bytes 4540
  3.6 20.1 %all-to-all-start = ((bf16[16,104,128]{2,1,0:T(8,128)(2,1)}), bf16[16,104,128]{2,1,0:T(8,128)(2,1)S(1)}, u32[]{:S(2)}, u32[]{:S(2)}) async-start(bf16[16,104,128]{2,1,0:T(8,128)(2,1)} %pack_flux.1), calls=%async_computation | async-start | bytes 851968 | tf_op jit(solution)/shard_map/all_to_all | solution.py:287
  23.7 15.9 %all-to-all-start.1 = ((bf16[16,96,128]{2,1,0:T(8,128)(2,1)}), bf16[16,96,128]{2,1,0:T(8,128)(2,1)S(1)}, u32[]{:S(2)}, u32[]{:S(2)}) async-start(bf16[16,96,128]{2,1,0:T(8,128)(2,1)} %pack_weight.1), calls=%async_computation.1 | async-start | bytes 786432 | tf_op jit(solution)/shard_map/all_to_all | solution.py:288
  28.8 5.2 %collective-permute-start = (bf16[6,4,16,128]{3,2,1,0:T(8,128)(2,1)S(1)}, bf16[6,4,16,128]{3,2,1,0:T(8,128)(2,1)S(1)}, u32[]{:S(2)}, u32[]{:S(2)}) collective-permute-start(bf16[6,4,16,128]{3,2,1,0:T(8,128)(2,1)S(1)} %broadcast_select_fusion), channel_id=1, source_target_pairs={{0,1},{1,0},{2,3},{3,2},{4,5},{5,4},{6,7},{7,6},{8,9},{9,8},{10,11... | collective-permute-start | bytes 294920 | tf_op jit(solution)/shard_map/ppermute | solution.py:326

commit v2 on v1

--- a/solution.py
+++ b/solution.py
@@ -1,3 +1,5 @@
+import functools
+
 import jax
 import jax.numpy as jnp
 from jax import lax
@@ -16,6 +18,7 @@
 ACROSS = COLS // LANES
 DOWN = ROWS // TILE_ROWS
 CAP = 2
+NEAR = 4
 HALO = 16
 PAIR = 2 * LANES
 F32 = jnp.float32
@@ -35,8 +38,8 @@
     return pl.BlockSpec(memory_space=pltpu.SMEM)
 
 
-def params():
-    return pltpu.CompilerParams(vmem_limit_bytes=40 * 1024 * 1024)
+def params(mib=40):
+    return pltpu.CompilerParams(vmem_limit_bytes=mib * 1024 * 1024)
 
 
 def cost(flops, moved):
@@ -50,7 +53,7 @@
     for t in range(count - 1):
         same = jnp.logical_and(dest == dest[:, t : t + 1], lane > t)
         ordinal = ordinal + jnp.where(same, 1, 0)
-    return dest * CAP + ordinal, ordinal
+    return dest * CAP + ordinal
 
 
 def spread(values, width, repeat):
@@ -59,40 +62,61 @@
     return jnp.dot(values.astype(F32).astype(BF16), hot, preferred_element_type=F32).astype(I32)
 
 
-def pack(dest, tiles_ref, out_ref):
-    visits, depth, _ = tiles_ref.shape
-    patches = out_ref.shape[0]
+def start_copies(pairs, sems):
+    copies = [pltpu.make_async_copy(src, dst, sems.at[i]) for i, (src, dst) in enumerate(pairs)]
+    for copy in copies:
+        copy.start()
+    return copies
+
+
+def sort_visit(goal, tiles, slots):
+    row = iota((slots * TILE_ROWS, goal.shape[1]), 0)
+    hot = jnp.where(row == goal, 1.0, 0.0).astype(BF16)
+    return jnp.dot(hot, tiles, preferred_element_type=F32).astype(BF16)
+
+
+def pack_kernel(far, dest_hbm, block_hbm, flux_hbm, weight_hbm, *refs):
+    flux_out, weight_out = refs[:far], refs[far : far + NEAR]
+    landing, sems = refs[far + NEAR : -1], refs[-1]
+    copies = start_copies(zip((dest_hbm, block_hbm, flux_hbm, weight_hbm), landing), sems)
+    dest_ref, block_ref, flux_ref, weight_ref = landing
+    visits, depth, _ = flux_ref.shape
     block = CAP * TILE_ROWS
-    slot, _ = slots_of(dest)
+    copies[0].wait()
+    copies[1].wait()
+    slot = slots_of(jnp.bitwise_xor(dest_ref[...], lax.axis_index("patch")))
     goal = spread(slot, depth, TILE_ROWS) * TILE_ROWS + iota((visits, depth), 1) % TILE_ROWS
-    row = iota((patches * block, depth), 0)
-    for k in range(visits):
-        hot = jnp.where(row == goal[k : k + 1], 1.0, 0.0).astype(BF16)
-        moved = jnp.dot(hot, tiles_ref[k], preferred_element_type=F32).astype(BF16)
-        out_ref[:, k * block : (k + 1) * block, :] = moved.reshape(patches, block, LANES)
-
-
-def pack_flux_kernel(me_ref, dest_ref, block_ref, tiles_ref, out_ref):
-    dest = dest_ref[...]
-    visits = dest.shape[0]
-    patches = out_ref.shape[0]
-    pack(dest, tiles_ref, out_ref)
-    _, ordinal = slots_of(dest)
     place = block_ref[...] % ACROSS * DOWN + block_ref[...] // ACROSS + 1
     lane = iota((TILE_ROWS, LANES), 1)
-    first = CAP * me_ref[0]
-    for q in range(patches):
-        note = jnp.zeros((TILE_ROWS, LANES), F32)
-        for o in range(CAP):
-            chosen = jnp.logical_and(dest == q, ordinal == o)
-            value = jnp.sum(jnp.where(chosen, place, 0).astype(F32), axis=1, keepdims=True)
-            value = jnp.concatenate([value, jnp.zeros((TILE_ROWS - visits, 1), F32)], axis=0)
-            note = jnp.where(lane == first + o, value, note)
-        out_ref[q, visits * CAP * TILE_ROWS :, :] = note.astype(BF16)
-
-
-def pack_weight_kernel(dest_ref, tiles_ref, out_ref):
-    pack(dest_ref[...], tiles_ref, out_ref)
+    for x in range(far):
+        for y in range(NEAR):
+            note = jnp.zeros((TILE_ROWS, LANES), F32)
+            for o in range(CAP):
+                chosen = slot == CAP * (x * NEAR + y) + o
+                value = jnp.sum(jnp.where(chosen, place, 0).astype(F32), axis=1, keepdims=True)
+                value = jnp.concatenate([value, jnp.zeros((TILE_ROWS - visits, 1), F32)], axis=0)
+                note = jnp.where(lane == CAP * (y * far + x) + o, value, note)
+            flux_out[x][y, visits * block :, :] = note.astype(BF16)
+    copies[2].wait()
+    copies[3].wait()
+    for k in range(visits):
+        both = jnp.concatenate([flux_ref[k], weight_ref[k]], axis=1)
+        moved = sort_visit(goal[k : k + 1], both, far * NEAR * CAP)
+        lines = slice(k * block, (k + 1) * block)
+        for x in range(far):
+            for y in range(NEAR):
+                rel = x * NEAR + y
+                part = moved[rel * block : (rel + 1) * block]
+                flux_out[x][y, lines, :] = part[:, :LANES]
+                weight_out[y][x, lines, :] = part[:, LANES:]
+
+
+def regroup_kernel(count, backward, *refs):
+    ins = refs[:count][:: -1 if backward else 1]
+    outs = refs[-(ins[0].shape[0] - 1) :]
+    for j, out in enumerate(outs):
+        for i, part in enumerate(ins):
+            out[i] = part[j + 1]
 
 
 def placing(note, senders):
@@ -107,19 +131,29 @@
     return jnp.dot(hot, received, preferred_element_type=F32)
 
 
-def place_kernel(recv_ref, frame_ref, top_ref, bottom_ref, note_ref):
-    senders = recv_ref.shape[0]
+def place_kernel(far, swap, *refs):
+    chunks, others = refs[:far][::-1], refs[far : far + NEAR - 1]
+    frame_ref, note_ref, *edges = refs[far + NEAR - 1 :]
     visits = frame_ref.shape[0]
     block = CAP * TILE_ROWS
-    note = jnp.sum(recv_ref[:, visits * block :, :].astype(F32), axis=0)
+    note = sum(chunk[0, visits * block :, :].astype(F32) for chunk in chunks)
+    for other in others:
+        note = note + jnp.sum(other[:, visits * block :, :].astype(F32), axis=0)
     note_ref[...] = note
-    goal = placing(note, senders)
+    goal = placing(note, far * NEAR)
     for k in range(visits):
-        received = recv_ref[:, k * block : (k + 1) * block, :].reshape(senders * block, LANES)
-        frame = placed(goal[k : k + 1], received).astype(BF16).reshape(ACROSS, ROWS, LANES)
+        lines = slice(k * block, (k + 1) * block)
+        received = [chunk[0, lines, :] for chunk in chunks]
+        received += [other[:, lines, :].reshape(far * block, LANES) for other in others]
+        frame = placed(goal[k : k + 1], jnp.concatenate(received, axis=0)).astype(BF16)
+        frame = frame.reshape(ACROSS, ROWS, LANES)
         frame_ref[k] = frame
-        top_ref[k] = frame[:, :HALO]
-        bottom_ref[k] = frame[:, ROWS - HALO :]
+        top, bottom = frame[:, :HALO], frame[:, ROWS - HALO :]
+        if swap:
+            edges[0][k] = jnp.where(lax.axis_index("band") == 0, bottom, top)
+        else:
+            edges[0][k] = top
+            edges[1][k] = bottom
 
 
 def hot_rows(taps, shift_lane, width, used=None):
@@ -132,9 +166,14 @@
     return jnp.dot(taps, hot, preferred_element_type=F32)
 
 
-def table_kernel(first_ref, up_ref, column_ref, row_ref, spatial_ref, coord_ref, table_ref, own_ref, halo_ref):
+def table_kernel(bands, up_ref, taps_ref, spatial_ref, table_ref, own_ref, halo_ref):
+    taps = [taps_ref[b].astype(F32) for b in range(BASIS)]
+    blank = [jnp.zeros((GROUPS - BASIS, TAPS), F32)]
+    column, line_taps = (
+        jnp.concatenate([tap[i : i + 1] for tap in taps] + blank, axis=0).astype(BF16) for i in range(2)
+    )
     low = LANES // 2 - MARGIN
-    lines = hot_rows(column_ref[...], lambda tap: (-low - tap) % LANES, LANES)
+    lines = hot_rows(column, lambda tap: (-low - tap) % LANES, LANES)
     gap = iota((PAIR, LANES), 0) - iota((PAIR, LANES), 1) - low
     inside = jnp.logical_and(gap >= 0, gap < TAPS)
     for b in range(table_ref.shape[1] // LANES):
@@ -147,8 +186,9 @@
         table_ref[:, b * LANES : (b + 1) * LANES] = part.astype(BF16)
 
     visits = own_ref.shape[0]
-    coord = coord_ref[...]
-    spatial = spatial_ref[...]
+    row = lax.axis_index("band") * ROWS + iota((ROWS, LANES), 0)
+    coord = (2.0 * row.astype(F32) + 1.0) / (ROWS * bands) - 1.0
+    spatial = jnp.concatenate([spatial_ref[i] for i in range(3 * visits)], axis=0)
 
     def fill(out_ref, height, offset, used=None):
         fit = LANES // height
@@ -156,7 +196,7 @@
         which = iota((GROUPS, LANES), 0)
         for j in range(fit):
             part = hot_rows(
-                row_ref[...], lambda tap: (height * j + tap - offset + 2 * LANES) % LANES, LANES, used
+                line_taps, lambda tap: (height * j + tap - offset + 2 * LANES) % LANES, LANES, used
             )
             line = line + jnp.where(which % fit == j, part, 0.0)
         t = iota((ROWS, LANES), 1) % height
@@ -217,17 +257,20 @@
         out_ref[k] = both[:ROWS] + col * both[ROWS:]
 
 
-def final_kernel(note_ref, recv_ref, *refs):
-    parts, out_ref = refs[:-1], refs[-1]
-    senders = recv_ref.shape[0]
+def final_kernel(far, note_ref, *refs):
+    chunks, others = refs[:NEAR], refs[NEAR : NEAR + far - 1][::-1]
+    parts, out_ref = refs[NEAR + far - 1 : -1], refs[-1]
     visits = parts[0].shape[0]
     block = CAP * TILE_ROWS
-    goal = placing(note_ref[...], senders)
+    goal = placing(note_ref[...], far * NEAR)
     total = jnp.zeros((ACROSS * ROWS, LANES), F32)
     sums = [jnp.zeros((ROWS, LANES), F32) for _ in range(ACROSS)]
     for k in range(visits):
-        received = recv_ref[:, k * block : (k + 1) * block, :].reshape(senders * block, LANES)
-        weight = placed(goal[k : k + 1], received)
+        lines = slice(k * block, (k + 1) * block)
+        received = []
+        for y in range(NEAR):
+            received += [chunks[y][0, lines, :]] + [other[y, lines, :] for other in others]
+        weight = placed(goal[k : k + 1], jnp.concatenate(received, axis=0))
         total = total + weight
         for c in range(ACROSS):
             lanes = slice(c * LANES, (c + 1) * LANES)
@@ -260,91 +303,110 @@
     )(frame, table, mix)
 
 
+def regroup(parts, after, name, backward=False):
+    count = parts[0].shape[0]
+    return pl.pallas_call(
+        functools.partial(regroup_kernel, len(parts), backward),
+        out_shape=tuple(shape((len(parts),) + parts[0].shape[1:], BF16) for _ in range(count - 1)),
+        in_specs=[vmem()] * len(parts) + [pl.BlockSpec(memory_space=pl.ANY)] * len(after),
+        out_specs=(vmem(),) * (count - 1),
+        compiler_params=params(),
+        name=name,
+    )(*parts, *after)
+
+
 def per_device(tile_flux, tile_weight, dest_patch, dest_block, basis, spatial):
     visits, tile_count, tile_height, tile_width = tile_flux.shape
     patches, bands = lax.axis_size("patch"), lax.axis_size("band")
-    me, band = lax.axis_index("patch"), lax.axis_index("band")
+    band = lax.axis_index("band")
+    far = patches // NEAR
     depth = tile_count * tile_height
     block = CAP * TILE_ROWS
     flux = tile_flux.reshape(visits, depth, tile_width)
     weight = tile_weight.reshape(visits, depth, tile_width)
-    send_flux = pl.pallas_call(
-        pack_flux_kernel,
-        out_shape=shape((patches, visits * block + TILE_ROWS, LANES), BF16),
-        in_specs=[smem()] + [vmem()] * 3,
-        out_specs=vmem(),
-        compiler_params=params(),
-        name="pack_flux",
-    )(me.reshape(1), dest_patch, dest_block, flux)
-    send_weight = pl.pallas_call(
-        pack_weight_kernel,
-        out_shape=shape((patches, visits * block, LANES), BF16),
-        in_specs=[vmem()] * 2,
-        out_specs=vmem(),
-        compiler_params=params(),
-        name="pack_weight",
-    )(dest_patch, weight)
-    recv_flux = lax.all_to_all(send_flux, "patch", split_axis=0, concat_axis=0, tiled=True)
-    recv_weight = lax.all_to_all(send_weight, "patch", split_axis=0, concat_axis=0, tiled=True)
-
-    row = (band * ROWS).astype(F32) + jnp.arange(ROWS, dtype=F32)
-    coord = jnp.broadcast_to(((2.0 * row + 1.0) / (ROWS * bands) - 1.0)[:, None], (ROWS, LANES))
-    taps = jnp.pad(basis, ((0, 0), (0, GROUPS - BASIS), (0, 0)))
-    coefs = spatial[0].reshape(visits * 3, BASIS)
+
+    def swap(value, step):
+        return lax.ppermute(value, "patch", [(i, i ^ step) for i in range(patches)])
+
+    packed = pl.pallas_call(
+        functools.partial(pack_kernel, far),
+        out_shape=(shape((NEAR, visits * block + TILE_ROWS, LANES), BF16),) * far
+        + (shape((far, visits * block, LANES), BF16),) * NEAR,
+        in_specs=[pl.BlockSpec(memory_space=pltpu.HBM)] * 4,
+        out_specs=(vmem(),) * (far + NEAR),
+        scratch_shapes=[
+            pltpu.VMEM(dest_patch.shape, I32),
+            pltpu.VMEM(dest_block.shape, I32),
+            pltpu.VMEM(flux.shape, BF16),
+            pltpu.VMEM(weight.shape, BF16),
+            pltpu.SemaphoreType.DMA((4,)),
+        ],
+        compiler_params=params(60),
+        name="pack",
+    )(dest_patch, dest_block, flux, weight)
+    flux_far = [swap(packed[x], x * NEAR) for x in range(far - 1, 0, -1)] + [packed[0]]
+    weight_near = [packed[far]] + [swap(packed[far + y], y) for y in range(1, NEAR)]
+
+    coefs = spatial.reshape(visits * 3, 1, BASIS)
+    taps = basis.transpose(1, 0, 2)
 
     def tables(up):
         return pl.pallas_call(
-            table_kernel,
+            functools.partial(table_kernel, bands),
             out_shape=(
                 shape((PAIR, 2 * pl.cdiv(BASIS, 2) * LANES), BF16),
                 shape((visits, 2 * ROWS, GROUPS * ROWS), BF16),
                 shape((visits, 2 * ROWS, GROUPS * HALO), BF16),
             ),
-            in_specs=[smem()] * 2 + [vmem()] * 4,
+            in_specs=[smem()] + [vmem()] * 2,
             out_specs=(vmem(),) * 3,
             compiler_params=params(),
             cost_estimate=cost(10**9, 4 * 1024 * 1024),
             name="tables",
-        )(band.reshape(1), up.reshape(1).astype(I32), taps[0], taps[1], coefs, coord)
-
-    frame, top, bottom, note = pl.pallas_call(
-        place_kernel,
-        out_shape=(
-            shape((visits, ACROSS, ROWS, LANES), BF16),
-            shape((visits, ACROSS, HALO, LANES), BF16),
-            shape((visits, ACROSS, HALO, LANES), BF16),
-            shape((TILE_ROWS, LANES), F32),
-        ),
-        in_specs=[vmem()],
-        out_specs=(vmem(),) * 4,
+        )(up.reshape(1).astype(I32), taps, coefs)
+
+    if bands == 2:
+        ups = [band]
+    else:
+        ups = [jnp.int32(1), jnp.int32(0)]
+    built = [tables(up) for up in ups]
+    table, own_mix, _ = built[0]
+    weight_sent = regroup(weight_near, [own_mix], "regroup_weight")
+    weight_far = [swap(weight_sent[x - 1], x * NEAR) for x in range(far - 1, 0, -1)]
+    flux_sent = regroup(flux_far, [weight_sent[0]], "regroup_flux", backward=True)
+    flux_near = [swap(part, y + 1) for y, part in enumerate(flux_sent)]
+
+    edge_shape = shape((visits, ACROSS, HALO, LANES), BF16)
+    edge_count = 1 if bands == 2 else 2
+    frame, note, *edges = pl.pallas_call(
+        functools.partial(place_kernel, far, bands == 2),
+        out_shape=(shape((visits, ACROSS, ROWS, LANES), BF16), shape((TILE_ROWS, LANES), F32))
+        + (edge_shape,) * edge_count,
+        in_specs=[vmem()] * (far + NEAR - 1),
+        out_specs=(vmem(),) * (2 + edge_count),
         compiler_params=params(),
         name="place_flux",
-    )(recv_flux)
+    )(*flux_far, *flux_near)
 
     if bands == 2:
-        edge = jnp.where(band == 0, bottom, top)
-        halos = [lax.ppermute(edge, "band", [(0, 1), (1, 0)])]
-        ups = [band]
+        halos = [lax.ppermute(edges[0], "band", [(0, 1), (1, 0)])]
     else:
         down = [(i, i + 1) for i in range(bands - 1)]
         halos = [
-            lax.ppermute(bottom, "band", down),
-            lax.ppermute(top, "band", [(j, i) for i, j in down]),
+            lax.ppermute(edges[1], "band", down),
+            lax.ppermute(edges[0], "band", [(j, i) for i, j in down]),
         ]
-        ups = [jnp.int32(1), jnp.int32(0)]
-    built = [tables(up) for up in ups]
-    table, own_mix, _ = built[0]
     parts = [filter_rows(frame, table, own_mix, "filter_own")]
     for halo, (_, _, halo_mix) in zip(halos, built):
         parts.append(filter_rows(halo, table, halo_mix, "filter_halo"))
     return pl.pallas_call(
-        final_kernel,
+        functools.partial(final_kernel, far),
         out_shape=shape((1, ROWS, COLS), F32),
-        in_specs=[vmem()] * (2 + len(parts)),
+        in_specs=[vmem()] * (NEAR + far + len(parts)),
         out_specs=vmem(),
         compiler_params=params(),
         name="final",
-    )(note, recv_weight, *parts)
+    )(note, *weight_near, *weight_far, *parts)
 
 
 def solution(mesh):

time: 41 us -> 33.1 us (0.81)
  waiting for transfers between devices: 17.4 us -> 9.04 us
  starting transfers between devices: 12.6 us -> 14.5 us
  local copies, waits for them, and re-layouts: 2.43 us -> 1.41 us
    all_to_all x2 -> x0, waiting for transfers between devices: 15.9 us -> none  [the longest x1 11.4 us: per_device(): lax.all_to_all(send_flux, 'patch', split_axis=0, concat_axis=0, tiled=True)]
    ppermute x1 -> x13, starting transfers between devices: 1.56 us -> 14.5 us  [the longest x12 12.9 us: swap(): return lax.ppermute(value, 'patch', [(i, i ^ step) for i in range(patches)])]
    all_to_all x2 -> x0, starting transfers between devices: 11.1 us -> none  [the longest x1 7.39 us: per_device(): lax.all_to_all(send_flux, 'patch', split_axis=0, concat_axis=0, tiled=True)]
    ppermute x1 -> x13, waiting for transfers between devices: 1.54 us -> 9.04 us  [the longest x12 7.66 us: swap(): return lax.ppermute(value, 'patch', [(i, i ^ step) for i in range(patches)])]
    unnamed x15 -> x8, local copies, waits for them, and re-layouts: 2.33 us -> 1.41 us
    pallas_call x5 -> x6, Pallas kernels: 4.68 us -> 4.52 us  [the longest x1 2.29 us: per_device(): pl.pallas_call(functools.partial(pack_kernel, far), out_shape=(shape((NEA...]
  transfers between devices with their start and end apart: 3 -> 13, of which waited for: 3 -> 7; matrix products, arithmetic and copies ran while one was open for 0% -> 0% of each run, Pallas kernels for 14% -> 14%
where the time goes in v2:
time: 33.1 us; the launch traced here: 32.8 us
  starting transfers between devices  14.5 us (44%)
  waiting for transfers between devices  9.04 us (27%)
  Pallas kernels  7.82 us (24%)
  local copies, waits for them, and re-layouts  1.41 us (4%)
    ppermute x12, starting transfers between devices, swap(): return lax.ppermute(value, 'patch', [(i, i ^ step) for i in range(patches)])  12.9 us
    ppermute x12, waiting for transfers between devices, swap(): return lax.ppermute(value, 'patch', [(i, i ^ step) for i in range(patches)])  7.66 us
    pallas_call x2, Pallas kernels, filter_rows(): pl.pallas_call(filter_kernel, out_shape=shape((visits, ROWS, COLS), F32),...  3.3 us
    pallas_call x1, Pallas kernels, per_device(): pl.pallas_call(functools.partial(pack_kernel, far), out_shape=(shape((NEA...  2.29 us
    ppermute x1, starting transfers between devices, per_device(): halos = [lax.ppermute(edges[0], 'band', [(0, 1), (1, 0)])]  1.56 us
    unnamed x8, local copies, waits for them, and re-layouts  1.41 us
    ppermute x1, waiting for transfers between devices, per_device(): halos = [lax.ppermute(edges[0], 'band', [(0, 1), (1, 0)])]  1.38 us
    pallas_call x1, Pallas kernels, per_device(): pl.pallas_call(functools.partial(final_kernel, far), out_shape=shape((1,...  1.02 us
  transfers between devices with their start and end apart: 13, of which 7 were waited for; matrix products, arithmetic and copies ran while one was open for 0% of the time, Pallas kernels for 14%

profile of v2, /device:TPU:0, one launch (start us, length us, event | category | flops | bytes accessed | tf_op | source)
XLA Modules:
  0.0 32.8 jit_solution(3711285367649807930)
XLA Ops:
  0.0 2.3 %pack.1 = (bf16[4,104,128]{2,1,0:T(8,128)(2,1)}, bf16[4,104,128]{2,1,0:T(8,128)(2,1)}, bf16[4,104,128]{2,1,0:T(8,128)(2,1)}, bf16[4,104,128]{2,1,0:T(8,128)(2,1)...) custom-call(s32[6,16]{1,0:T(8,128)} %dest_hbm.1, ...), custom_call_target="tpu_custom_call" | custom-call | tf_op jit(solution)/shard_map/pack/pallas_call | solution.py:331
  2.3 0.5 %collective-permute-start.3 = (bf16[4,96,128]{2,1,0:T(8,128)(2,1)}, bf16[4,96,128]{2,1,0:T(8,128)(2,1)S(1)}, u32[]{:S(2)}, u32[]{:S(2)}) collective-permute-start(bf16[4,96,128]{2,1,0:T(8,128)(2,1)} %get-tuple-element.30), channel_id=1, source_target_pairs={{0,2},{2,0},{4,6},{6,4},{8,10},{10,8},{12,14},{14,12},{16,18},{18,... | collective-permute-start | bytes 294920 | tf_op jit(solution)/shard_map/ppermute | solution.py:329
  2.8 4.7 %collective-permute-start = (bf16[4,104,128]{2,1,0:T(8,128)(2,1)}, bf16[4,104,128]{2,1,0:T(8,128)(2,1)S(1)}, u32[]{:S(2)}, u32[]{:S(2)}) collective-permute-start(bf16[4,104,128]{2,1,0:T(8,128)(2,1)} %get-tuple-element.25), channel_id=1, source_target_pairs={{0,24},{2,26},{4,28},{6,30},{8,16},{10,18},{12,20},{14,22},{16,8},... | collective-permute-start | bytes 319496 | tf_op jit(solution)/shard_map/ppermute | solution.py:329
  7.5 0.0 collective-permute-start.1
  7.5 0.7 %collective-permute-start.2 = (bf16[4,104,128]{2,1,0:T(8,128)(2,1)}, bf16[4,104,128]{2,1,0:T(8,128)(2,1)S(1)}, u32[]{:S(2)}, u32[]{:S(2)}) collective-permute-start(bf16[4,104,128]{2,1,0:T(8,128)(2,1)} %get-tuple-element.27), channel_id=1, source_target_pairs={{0,8},{2,10},{4,12},{6,14},{8,0},{10,2},{12,4},{14,6},{16,24},{18,... | collective-permute-start | bytes 319496 | tf_op jit(solution)/shard_map/ppermute | solution.py:329
  8.1 1.6 %collective-permute-start.4 = (bf16[4,96,128]{2,1,0:T(8,128)(2,1)}, bf16[4,96,128]{2,1,0:T(8,128)(2,1)S(1)}, u32[]{:S(2)}, u32[]{:S(2)}) collective-permute-start(bf16[4,96,128]{2,1,0:T(8,128)(2,1)} %get-tuple-element.31), channel_id=1, source_target_pairs={{0,4},{2,6},{4,0},{6,2},{8,12},{10,14},{12,8},{14,10},{16,20},{18,... | collective-permute-start | bytes 294920 | tf_op jit(solution)/shard_map/ppermute | solution.py:329
  9.8 0.0 collective-permute-done.3.refs_1_
  9.8 0.0 collective-permute-start.5
  9.8 0.0 copy-start.2
  9.8 0.7 %copy-done.2 = bf16[2,21,31]{2,0,1:T(2,128)(2,1)S(1)} copy-done((bf16[2,21,31]{2,0,1:T(2,128)(2,1)S(1)}, bf16[2,21,31]{2,0,1:T(2,128)(2,1)}, u32[]{:S(2)}) %copy-start.2) | copy-done | bytes 2628
  10.5 0.0 copy-start.3
  10.5 0.7 %copy-done.3 = f32[1,6,3,21]{3,0,2,1:T(1,128)S(1)} copy-done((f32[1,6,3,21]{3,0,2,1:T(1,128)S(1)}, f32[1,6,3,21]{3,0,2,1:T(1,128)}, u32[]{:S(2)}) %copy-start.3) | copy-done | bytes 1536
  11.2 0.0 copy-start.1
  11.2 0.0 copy-start
  11.2 0.8 %tables.1 = (bf16[256,2816]{1,0:T(8,128)(2,1)S(1)}, bf16[6,64,768]{2,1,0:T(8,128)(2,1)S(1)}, bf16[6,64,384]{2,1,0:T(8,128)(2,1)S(1)}) custom-call(s32[1]{0:T(128)} %bitcast.2.up_ref, bf16[21,2,31]{2,1,0:T(2,128)(2,1)S(1)} %bitcast.5, f32[18,1,21]{2,1,0:T(1,128)S(1)} %bitcast.6), custom_call_target="tpu_custom_call" | custom-call | flops 1000000000 | bytes 4194304 | tf_op jit(solution)/shard_map/tables/pallas_call | solution.py:354
  12.0 1.1 %collective-permute-done.4.refs_2_ = bf16[4,96,128]{2,1,0:T(8,128)(2,1)S(1)} collective-permute-done((bf16[4,96,128]{2,1,0:T(8,128)(2,1)}, bf16[4,96,128]{2,1,0:T(8,128)(2,1)S(1)}, u32[]{:S(2)}, u32[]{:S(2)}) %collective-permute-start.4) | collective-permute-done | bytes 98336 | tf_op jit(solution)/shard_map/ppermute | solution.py:329
  13.1 2.0 %collective-permute-done.5.refs_3_ = bf16[4,96,128]{2,1,0:T(8,128)(2,1)S(1)} collective-permute-done((bf16[4,96,128]{2,1,0:T(8,128)(2,1)}, bf16[4,96,128]{2,1,0:T(8,128)(2,1)S(1)}, u32[]{:S(2)}, u32[]{:S(2)}) %collective-permute-start.5) | collective-permute-done | bytes 98336 | tf_op jit(solution)/shard_map/ppermute | solution.py:329
  15.1 0.0 copy-done.1
  15.1 0.0 collective-permute-done.refs_0_
  15.1 2.2 %collective-permute-done.1.refs_1_ = bf16[4,104,128]{2,1,0:T(8,128)(2,1)S(1)} collective-permute-done((bf16[4,104,128]{2,1,0:T(8,128)(2,1)}, bf16[4,104,128]{2,1,0:T(8,128)(2,1)S(1)}, u32[]{:S(2)}, u32[]{:S(2)}) %collective-permute-start.1) | collective-permute-done | bytes 106528 | tf_op jit(solution)/shard_map/ppermute | solution.py:329
  17.3 0.0 collective-permute-done.2.refs_2_
  17.3 0.0 copy-done
  17.3 0.1 collective-permute-start.6
  17.4 1.6 %collective-permute-start.7 = (bf16[4,104,128]{2,1,0:T(8,128)(2,1)S(1)}, bf16[4,104,128]{2,1,0:T(8,128)(2,1)S(1)}, u32[]{:S(2)}, u32[]{:S(2)}) collective-permute-start(bf16[4,104,128]{2,1,0:T(8,128)(2,1)S(1)} %get-tuple-element.36), channel_id=1, source_target_pairs={{0,4},{2,6},{4,0},{6,2},{8,12},{10,14},{12,8},{14,10},{16,20},{18,... | collective-permute-start | bytes 319496 | tf_op jit(solution)/shard_map/ppermute | solution.py:329
  19.0 0.3 collective-permute-start.8
  19.3 0.4 %collective-permute-start.11 = (bf16[4,96,128]{2,1,0:T(8,128)(2,1)S(1)}, bf16[4,96,128]{2,1,0:T(8,128)(2,1)S(1)}, u32[]{:S(2)}, u32[]{:S(2)}) collective-permute-start(bf16[4,96,128]{2,1,0:T(8,128)(2,1)S(1)} %get-tuple-element.34.refs_4_), channel_id=1, source_target_pairs={{0,8},{2,10},{4,12},{6,14},{8,0},{10,2},{12,4},{14,6},{16,24},{18,... | collective-permute-start | bytes 294920 | tf_op jit(solution)/shard_map/ppermute | solution.py:329
  19.6 2.1 %collective-permute-start.9 = (bf16[4,96,128]{2,1,0:T(8,128)(2,1)S(1)}, bf16[4,96,128]{2,1,0:T(8,128)(2,1)S(1)}, u32[]{:S(2)}, u32[]{:S(2)}) collective-permute-start(bf16[4,96,128]{2,1,0:T(8,128)(2,1)S(1)} %get-tuple-element.39), channel_id=1, source_target_pairs={{0,24},{2,26},{4,28},{6,30},{8,16},{10,18},{12,20},{14,22},{16,8},... | collective-permute-start | bytes 294920 | tf_op jit(solution)/shard_map/ppermute | solution.py:329
  21.7 0.0 collective-permute-done.6.refs_4_
  21.7 1.0 %collective-permute-start.10 = (bf16[4,96,128]{2,1,0:T(8,128)(2,1)S(1)}, bf16[4,96,128]{2,1,0:T(8,128)(2,1)S(1)}, u32[]{:S(2)}, u32[]{:S(2)}) collective-permute-start(bf16[4,96,128]{2,1,0:T(8,128)(2,1)S(1)} %get-tuple-element.40), channel_id=1, source_target_pairs={{0,16},{2,18},{4,20},{6,22},{8,24},{10,26},{12,28},{14,30},{16,0},... | collective-permute-start | bytes 294920 | tf_op jit(solution)/shard_map/ppermute | solution.py:329
  22.8 0.5 %collective-permute-done.7.refs_5_ = bf16[4,104,128]{2,1,0:T(8,128)(2,1)S(1)} collective-permute-done((bf16[4,104,128]{2,1,0:T(8,128)(2,1)S(1)}, bf16[4,104,128]{2,1,0:T(8,128)(2,1)S(1)}, u32[]{:S(2)}, u32[]{:S(2)}) %collective-permute-start.7) | collective-permute-done | bytes 106528 | tf_op jit(solution)/shard_map/ppermute | solution.py:329
  23.2 1.4 %collective-permute-done.8.refs_6_ = bf16[4,104,128]{2,1,0:T(8,128)(2,1)S(1)} collective-permute-done((bf16[4,104,128]{2,1,0:T(8,128)(2,1)S(1)}, bf16[4,104,128]{2,1,0:T(8,128)(2,1)S(1)}, u32[]{:S(2)}, u32[]{:S(2)}) %collective-permute-start.8) | collective-permute-done | bytes 106528 | tf_op jit(solution)/shard_map/ppermute | solution.py:329
  24.6 0.4 %place_flux.1 = (bf16[6,4,32,128]{3,2,1,0:T(8,128)(2,1)S(1)}, f32[8,128]{1,0:T(8,128)S(1)}, bf16[6,4,16,128]{3,2,1,0:T(8,128)(2,1)S(1)}) custom-call(bf16[4,104,128]{2,1,0:T(8,128)(2,1)S(1)} %collective-permute-done.refs_0_, bf16[4,104,128]{2,1,0:T(8,128)(2,1)S(1)} %collective-permute-done.1.refs_1_, ...), custom_call_target="tpu_custom_call" | custom-call | tf_op jit(solution)/shard_map/place_flux/pallas_call | solution.py:381
  25.0 1.6 %collective-permute-start.12 = (bf16[6,4,16,128]{3,2,1,0:T(8,128)(2,1)S(1)}, bf16[6,4,16,128]{3,2,1,0:T(8,128)(2,1)S(1)}, u32[]{:S(2)}, u32[]{:S(2)}) collective-permute-start(bf16[6,4,16,128]{3,2,1,0:T(8,128)(2,1)S(1)} %get-tuple-element.43), channel_id=1, source_target_pairs={{0,1},{1,0},{2,3},{3,2},{4,5},{5,4},{6,7},{7,6},{8,9},{9,8},{10,11... | collective-permute-start | bytes 294920 | tf_op jit(solution)/shard_map/ppermute | solution.py:392
  26.6 2.1 %filter_own.1.refs_7_ = f32[6,32,512]{2,1,0:T(8,128)S(1)} custom-call(bf16[6,4,32,128]{3,2,1,0:T(8,128)(2,1)S(1)} %get-tuple-element.41.frame_ref, bf16[256,2816]{1,0:T(8,128)(2,1)S(1)} %get-tuple-element.42.table_ref, bf16[6,64,768]{2,1,0:T(8,128)(2,1)S(1)} %get-tuple-element.33.refs_4_.mix_ref), custom_call_target="tpu_custom_call" | custom-call | flops 2113929216 | bytes 4194304 | tf_op jit(solution)/shard_map/filter_own/pallas_call | solution.py:291
  28.7 1.4 %collective-permute-done.12.frame_ref = bf16[6,4,16,128]{3,2,1,0:T(8,128)(2,1)S(1)} collective-permute-done((bf16[6,4,16,128]{3,2,1,0:T(8,128)(2,1)S(1)}, bf16[6,4,16,128]{3,2,1,0:T(8,128)(2,1)S(1)}, u32[]{:S(2)}, u32[]{:S(2)}) %collective-permute-start.12) | collective-permute-done | bytes 98336 | tf_op jit(solution)/shard_map/ppermute | solution.py:392
  30.0 1.2 %filter_halo.1.refs_8_ = f32[6,32,512]{2,1,0:T(8,128)S(1)} custom-call(bf16[6,4,16,128]{3,2,1,0:T(8,128)(2,1)S(1)} %collective-permute-done.12.frame_ref, bf16[256,2816]{1,0:T(8,128)(2,1)S(1)} %get-tuple-element.42.table_ref, bf16[6,64,384]{2,1,0:T(8,128)(2,1)S(1)} %get-tuple-element.44.mix_ref), custom_call_target="tpu_custom_call" | custom-call | flops 1056964608 | bytes 4194304 | tf_op jit(solution)/shard_map/filter_halo/pallas_call | solution.py:291
  31.3 0.0 collective-permute-done.9.refs_4_
  31.3 0.5 %collective-permute-done.10.refs_5_ = bf16[4,96,128]{2,1,0:T(8,128)(2,1)S(1)} collective-permute-done((bf16[4,96,128]{2,1,0:T(8,128)(2,1)S(1)}, bf16[4,96,128]{2,1,0:T(8,128)(2,1)S(1)}, u32[]{:S(2)}, u32[]{:S(2)}) %collective-permute-start.10) | collective-permute-done | bytes 98336 | tf_op jit(solution)/shard_map/ppermute | solution.py:329
  31.8 0.0 collective-permute-done.11.refs_6_
  31.8 1.0 %final.1 = f32[1,32,512]{2,1,0:T(8,128)} custom-call(f32[8,128]{1,0:T(8,128)S(1)} %get-tuple-element.38.note_ref, bf16[4,96,128]{2,1,0:T(8,128)(2,1)S(1)} %copy-done.1, bf16[4,96,128]{2,1,0:T(8,128)(2,1)S(1)} %collective-permute-done.3.refs_1_, bf16[4,96,128]{2,1,0:T(8,128)(2,1)S(1)} %collective-permute-done.4.refs_2_, ...), custom_call_target="tpu_custom_call" | custom-call | tf_op jit(solution)/shard_map/final/pallas_call | solution.py:402
  (2 shorter events, 0.0 us)
Async XLA Ops:
  2.3 7.5 %collective-permute-start.3 = (bf16[4,96,128]{2,1,0:T(8,128)(2,1)}, bf16[4,96,128]{2,1,0:T(8,128)(2,1)S(1)}, u32[]{:S(2)}, u32[]{:S(2)}) collective-permute-start(bf16[4,96,128]{2,1,0:T(8,128)(2,1)} %get-tuple-element.30), channel_id=1, source_target_pairs={{0,2},{2,0},{4,6},{6,4},{8,10},{10,8},{12,14},{14,12},{16,18},{18,... | collective-permute-start | bytes 294920 | tf_op jit(solution)/shard_map/ppermute | solution.py:329
  2.8 12.3 %collective-permute-start = (bf16[4,104,128]{2,1,0:T(8,128)(2,1)}, bf16[4,104,128]{2,1,0:T(8,128)(2,1)S(1)}, u32[]{:S(2)}, u32[]{:S(2)}) collective-permute-start(bf16[4,104,128]{2,1,0:T(8,128)(2,1)} %get-tuple-element.25), channel_id=1, source_target_pairs={{0,24},{2,26},{4,28},{6,30},{8,16},{10,18},{12,20},{14,22},{16,8},... | collective-permute-start | bytes 319496 | tf_op jit(solution)/shard_map/ppermute | solution.py:329
  7.5 9.8 %collective-permute-start.1 = (bf16[4,104,128]{2,1,0:T(8,128)(2,1)}, bf16[4,104,128]{2,1,0:T(8,128)(2,1)S(1)}, u32[]{:S(2)}, u32[]{:S(2)}) collective-permute-start(bf16[4,104,128]{2,1,0:T(8,128)(2,1)} %get-tuple-element.26), channel_id=1, source_target_pairs={{0,16},{2,18},{4,20},{6,22},{8,24},{10,26},{12,28},{14,30},{16,0},... | collective-permute-start | bytes 319496 | tf_op jit(solution)/shard_map/ppermute | solution.py:329
  7.5 9.8 %collective-permute-start.2 = (bf16[4,104,128]{2,1,0:T(8,128)(2,1)}, bf16[4,104,128]{2,1,0:T(8,128)(2,1)S(1)}, u32[]{:S(2)}, u32[]{:S(2)}) collective-permute-start(bf16[4,104,128]{2,1,0:T(8,128)(2,1)} %get-tuple-element.27), channel_id=1, source_target_pairs={{0,8},{2,10},{4,12},{6,14},{8,0},{10,2},{12,4},{14,6},{16,24},{18,... | collective-permute-start | bytes 319496 | tf_op jit(solution)/shard_map/ppermute | solution.py:329
  8.1 5.0 %collective-permute-start.4 = (bf16[4,96,128]{2,1,0:T(8,128)(2,1)}, bf16[4,96,128]{2,1,0:T(8,128)(2,1)S(1)}, u32[]{:S(2)}, u32[]{:S(2)}) collective-permute-start(bf16[4,96,128]{2,1,0:T(8,128)(2,1)} %get-tuple-element.31), channel_id=1, source_target_pairs={{0,4},{2,6},{4,0},{6,2},{8,12},{10,14},{12,8},{14,10},{16,20},{18,... | collective-permute-start | bytes 294920 | tf_op jit(solution)/shard_map/ppermute | solution.py:329
  9.8 5.3 %collective-permute-start.5 = (bf16[4,96,128]{2,1,0:T(8,128)(2,1)}, bf16[4,96,128]{2,1,0:T(8,128)(2,1)S(1)}, u32[]{:S(2)}, u32[]{:S(2)}) collective-permute-start(bf16[4,96,128]{2,1,0:T(8,128)(2,1)} %get-tuple-element.32), channel_id=1, source_target_pairs={{0,6},{2,4},{4,2},{6,0},{8,14},{10,12},{12,10},{14,8},{16,22},{18,... | collective-permute-start | bytes 294920 | tf_op jit(solution)/shard_map/ppermute | solution.py:329
  9.8 0.7 %copy-start.2 = (bf16[2,21,31]{2,0,1:T(2,128)(2,1)S(1)}, bf16[2,21,31]{2,0,1:T(2,128)(2,1)}, u32[]{:S(2)}) copy-start(bf16[2,21,31]{2,0,1:T(2,128)(2,1)} %param.10) | copy-start | bytes 7816
  10.5 0.7 %copy-start.3 = (f32[1,6,3,21]{3,0,2,1:T(1,128)S(1)}, f32[1,6,3,21]{3,0,2,1:T(1,128)}, u32[]{:S(2)}) copy-start(f32[1,6,3,21]{3,0,2,1:T(1,128)} %param.11) | copy-start | bytes 4540
  11.2 3.9 %copy-start.1 = (bf16[4,96,128]{2,1,0:T(8,128)(2,1)S(1)}, bf16[4,96,128]{2,1,0:T(8,128)(2,1)}, u32[]{:S(2)}) copy-start(bf16[4,96,128]{2,1,0:T(8,128)(2,1)} %get-tuple-element.29.refs_0_) | copy-start | bytes 294916
  11.2 6.1 %copy-start = (bf16[4,104,128]{2,1,0:T(8,128)(2,1)S(1)}, bf16[4,104,128]{2,1,0:T(8,128)(2,1)}, u32[]{:S(2)}) copy-start(bf16[4,104,128]{2,1,0:T(8,128)(2,1)} %get-tuple-element.28.refs_3_) | copy-start | bytes 319492
  17.3 4.4 %collective-permute-start.6 = (bf16[4,104,128]{2,1,0:T(8,128)(2,1)S(1)}, bf16[4,104,128]{2,1,0:T(8,128)(2,1)S(1)}, u32[]{:S(2)}, u32[]{:S(2)}) collective-permute-start(bf16[4,104,128]{2,1,0:T(8,128)(2,1)S(1)} %get-tuple-element.35), channel_id=1, source_target_pairs={{0,2},{2,0},{4,6},{6,4},{8,10},{10,8},{12,14},{14,12},{16,18},{18,... | collective-permute-start | bytes 319496 | tf_op jit(solution)/shard_map/ppermute | solution.py:329
  17.4 5.8 %collective-permute-start.7 = (bf16[4,104,128]{2,1,0:T(8,128)(2,1)S(1)}, bf16[4,104,128]{2,1,0:T(8,128)(2,1)S(1)}, u32[]{:S(2)}, u32[]{:S(2)}) collective-permute-start(bf16[4,104,128]{2,1,0:T(8,128)(2,1)S(1)} %get-tuple-element.36), channel_id=1, source_target_pairs={{0,4},{2,6},{4,0},{6,2},{8,12},{10,14},{12,8},{14,10},{16,20},{18,... | collective-permute-start | bytes 319496 | tf_op jit(solution)/shard_map/ppermute | solution.py:329
  19.0 5.6 %collective-permute-start.8 = (bf16[4,104,128]{2,1,0:T(8,128)(2,1)S(1)}, bf16[4,104,128]{2,1,0:T(8,128)(2,1)S(1)}, u32[]{:S(2)}, u32[]{:S(2)}) collective-permute-start(bf16[4,104,128]{2,1,0:T(8,128)(2,1)S(1)} %get-tuple-element.37), channel_id=1, source_target_pairs={{0,6},{2,4},{4,2},{6,0},{8,14},{10,12},{12,10},{14,8},{16,22},{18,... | collective-permute-start | bytes 319496 | tf_op jit(solution)/shard_map/ppermute | solution.py:329
  19.3 12.6 %collective-permute-start.11 = (bf16[4,96,128]{2,1,0:T(8,128)(2,1)S(1)}, bf16[4,96,128]{2,1,0:T(8,128)(2,1)S(1)}, u32[]{:S(2)}, u32[]{:S(2)}) collective-permute-start(bf16[4,96,128]{2,1,0:T(8,128)(2,1)S(1)} %get-tuple-element.34.refs_4_), channel_id=1, source_target_pairs={{0,8},{2,10},{4,12},{6,14},{8,0},{10,2},{12,4},{14,6},{16,24},{18,... | collective-permute-start | bytes 294920 | tf_op jit(solution)/shard_map/ppermute | solution.py:329
  19.6 11.6 %collective-permute-start.9 = (bf16[4,96,128]{2,1,0:T(8,128)(2,1)S(1)}, bf16[4,96,128]{2,1,0:T(8,128)(2,1)S(1)}, u32[]{:S(2)}, u32[]{:S(2)}) collective-permute-start(bf16[4,96,128]{2,1,0:T(8,128)(2,1)S(1)} %get-tuple-element.39), channel_id=1, source_target_pairs={{0,24},{2,26},{4,28},{6,30},{8,16},{10,18},{12,20},{14,22},{16,8},... | collective-permute-start | bytes 294920 | tf_op jit(solution)/shard_map/ppermute | solution.py:329
  21.7 10.1 %collective-permute-start.10 = (bf16[4,96,128]{2,1,0:T(8,128)(2,1)S(1)}, bf16[4,96,128]{2,1,0:T(8,128)(2,1)S(1)}, u32[]{:S(2)}, u32[]{:S(2)}) collective-permute-start(bf16[4,96,128]{2,1,0:T(8,128)(2,1)S(1)} %get-tuple-element.40), channel_id=1, source_target_pairs={{0,16},{2,18},{4,20},{6,22},{8,24},{10,26},{12,28},{14,30},{16,0},... | collective-permute-start | bytes 294920 | tf_op jit(solution)/shard_map/ppermute | solution.py:329
  25.0 5.0 %collective-permute-start.12 = (bf16[6,4,16,128]{3,2,1,0:T(8,128)(2,1)S(1)}, bf16[6,4,16,128]{3,2,1,0:T(8,128)(2,1)S(1)}, u32[]{:S(2)}, u32[]{:S(2)}) collective-permute-start(bf16[6,4,16,128]{3,2,1,0:T(8,128)(2,1)S(1)} %get-tuple-element.43), channel_id=1, source_target_pairs={{0,1},{1,0},{2,3},{3,2},{4,5},{5,4},{6,7},{7,6},{8,9},{9,8},{10,11... | collective-permute-start | bytes 294920 | tf_op jit(solution)/shard_map/ppermute | solution.py:392

commit v3 on v2

--- a/solution.py
+++ b/solution.py
@@ -38,8 +38,16 @@
     return pl.BlockSpec(memory_space=pltpu.SMEM)
 
 
-def params(mib=40):
-    return pltpu.CompilerParams(vmem_limit_bytes=mib * 1024 * 1024)
+def hbm():
+    return pl.BlockSpec(memory_space=pltpu.HBM)
+
+
+def in_hbm(value):
+    return pltpu.with_memory_space_constraint(value, pltpu.HBM)
+
+
+def params():
+    return pltpu.CompilerParams(vmem_limit_bytes=40 * 1024 * 1024)
 
 
 def cost(flops, moved):
@@ -76,12 +84,13 @@
 
 
 def pack_kernel(far, dest_hbm, block_hbm, flux_hbm, weight_hbm, *refs):
-    flux_out, weight_out = refs[:far], refs[far : far + NEAR]
-    landing, sems = refs[far + NEAR : -1], refs[-1]
+    far_out, near_out = refs[: far - 1], refs[far - 1 : far - 1 + NEAR]
+    landing, sems = refs[far - 1 + NEAR : -1], refs[-1]
     copies = start_copies(zip((dest_hbm, block_hbm, flux_hbm, weight_hbm), landing), sems)
     dest_ref, block_ref, flux_ref, weight_ref = landing
     visits, depth, _ = flux_ref.shape
     block = CAP * TILE_ROWS
+    span = visits * block
     copies[0].wait()
     copies[1].wait()
     slot = slots_of(jnp.bitwise_xor(dest_ref[...], lax.axis_index("patch")))
@@ -89,34 +98,48 @@
     place = block_ref[...] % ACROSS * DOWN + block_ref[...] // ACROSS + 1
     lane = iota((TILE_ROWS, LANES), 1)
     for x in range(far):
+        note = jnp.zeros((TILE_ROWS, LANES), F32)
         for y in range(NEAR):
-            note = jnp.zeros((TILE_ROWS, LANES), F32)
             for o in range(CAP):
                 chosen = slot == CAP * (x * NEAR + y) + o
                 value = jnp.sum(jnp.where(chosen, place, 0).astype(F32), axis=1, keepdims=True)
                 value = jnp.concatenate([value, jnp.zeros((TILE_ROWS - visits, 1), F32)], axis=0)
                 note = jnp.where(lane == CAP * (y * far + x) + o, value, note)
-            flux_out[x][y, visits * block :, :] = note.astype(BF16)
+        note = note.astype(BF16)
+        if x:
+            far_out[x - 1][NEAR * span :, :] = note
+        else:
+            for out in near_out:
+                out[(far + 1) * span :, :] = note
     copies[2].wait()
     copies[3].wait()
     for k in range(visits):
         both = jnp.concatenate([flux_ref[k], weight_ref[k]], axis=1)
         moved = sort_visit(goal[k : k + 1], both, far * NEAR * CAP)
-        lines = slice(k * block, (k + 1) * block)
         for x in range(far):
             for y in range(NEAR):
                 rel = x * NEAR + y
                 part = moved[rel * block : (rel + 1) * block]
-                flux_out[x][y, lines, :] = part[:, :LANES]
-                weight_out[y][x, lines, :] = part[:, LANES:]
-
-
-def regroup_kernel(count, backward, *refs):
-    ins = refs[:count][:: -1 if backward else 1]
-    outs = refs[-(ins[0].shape[0] - 1) :]
+                if x:
+                    far_out[x - 1][part_of(y, span, k, block), :] = part[:, :LANES]
+                else:
+                    near_out[y][part_of(far, span, k, block), :] = part[:, :LANES]
+                near_out[y][part_of(x, span, k, block), :] = part[:, LANES:]
+
+
+def part_of(i, span, k, block):
+    return slice(i * span + k * block, i * span + (k + 1) * block)
+
+
+def regroup_kernel(count, span, skip, *refs):
+    ins = refs[:count]
+    outs = refs[count + skip :]
     for j, out in enumerate(outs):
         for i, part in enumerate(ins):
-            out[i] = part[j + 1]
+            out[i * span : (i + 1) * span, :] = part[(j + 1) * span : (j + 2) * span, :]
+        if out.shape[0] > count * span:
+            tail = sum(part[part.shape[0] - TILE_ROWS :, :].astype(F32) for part in ins)
+            out[count * span :, :] = tail.astype(BF16)
 
 
 def placing(note, senders):
@@ -126,26 +149,31 @@
     return place * TILE_ROWS + iota((TILE_ROWS, width), 1) % TILE_ROWS
 
 
-def placed(goal, received):
-    hot = jnp.where(iota((ACROSS * ROWS, goal.shape[1]), 0) == goal, 1.0, 0.0).astype(BF16)
-    return jnp.dot(hot, received, preferred_element_type=F32)
-
-
 def place_kernel(far, swap, *refs):
-    chunks, others = refs[:far][::-1], refs[far : far + NEAR - 1]
-    frame_ref, note_ref, *edges = refs[far + NEAR - 1 :]
+    chunks, others = refs[: far - 1], refs[far - 1 : far + NEAR - 2]
+    nears, (frame_ref, hot_ref, *edges) = refs[far + NEAR - 2 : far + 2 * NEAR - 2], refs[far + 2 * NEAR - 2 :]
     visits = frame_ref.shape[0]
     block = CAP * TILE_ROWS
-    note = sum(chunk[0, visits * block :, :].astype(F32) for chunk in chunks)
-    for other in others:
-        note = note + jnp.sum(other[:, visits * block :, :].astype(F32), axis=0)
-    note_ref[...] = note
+    span = visits * block
+    path = iota((TILE_ROWS, LANES), 1) // (CAP * far)
+    note = jnp.zeros((TILE_ROWS, LANES), F32)
+    for y in range(NEAR):
+        tails = [nears[y]] + (list(chunks) if y == 0 else [others[y - 1]])
+        tail = sum(ref[ref.shape[0] - TILE_ROWS :, :].astype(F32) for ref in tails)
+        note = jnp.where(path == y, tail, note)
     goal = placing(note, far * NEAR)
     for k in range(visits):
-        lines = slice(k * block, (k + 1) * block)
-        received = [chunk[0, lines, :] for chunk in chunks]
-        received += [other[:, lines, :].reshape(far * block, LANES) for other in others]
-        frame = placed(goal[k : k + 1], jnp.concatenate(received, axis=0)).astype(BF16)
+        hot = jnp.where(iota((ACROSS * ROWS, goal.shape[1]), 0) == goal[k : k + 1], 1.0, 0.0).astype(BF16)
+        hot_ref[k] = hot
+        received = []
+        for y in range(NEAR):
+            received.append(nears[y][part_of(far, span, k, block), :])
+            for x in range(1, far):
+                if y:
+                    received.append(others[y - 1][part_of(x - 1, span, k, block), :])
+                else:
+                    received.append(chunks[x - 1][part_of(0, span, k, block), :])
+        frame = jnp.dot(hot, jnp.concatenate(received, axis=0), preferred_element_type=F32).astype(BF16)
         frame = frame.reshape(ACROSS, ROWS, LANES)
         frame_ref[k] = frame
         top, bottom = frame[:, :HALO], frame[:, ROWS - HALO :]
@@ -166,7 +194,10 @@
     return jnp.dot(taps, hot, preferred_element_type=F32)
 
 
-def table_kernel(bands, up_ref, taps_ref, spatial_ref, table_ref, own_ref, halo_ref):
+def table_kernel(bands, up_ref, taps_hbm, spatial_hbm, table_ref, own_ref, halo_ref, taps_ref, spatial_ref, sems):
+    copies = start_copies(((taps_hbm, taps_ref), (spatial_hbm, spatial_ref)), sems)
+    for copy in copies:
+        copy.wait()
     taps = [taps_ref[b].astype(F32) for b in range(BASIS)]
     blank = [jnp.zeros((GROUPS - BASIS, TAPS), F32)]
     column, line_taps = (
@@ -226,7 +257,8 @@
     )
 
 
-def filter_kernel(frame_ref, table_ref, mix_ref, out_ref, windows, filtered):
+def filter_kernel(frame_ref, table_ref, mix_ref, *refs):
+    before, (out_ref, windows, filtered) = refs[:-3], refs[-3:]
     visits, _, height, _ = frame_ref.shape
     half = LANES // 2
     left = iota((height, LANES), 1) < half
@@ -254,29 +286,26 @@
     col = (2.0 * iota((1, COLS), 1).astype(F32) + 1.0) / COLS - 1.0
     for k in range(visits):
         both = jnp.dot(mix_ref[k], filtered[k], preferred_element_type=F32)
-        out_ref[k] = both[:ROWS] + col * both[ROWS:]
-
-
-def final_kernel(far, note_ref, *refs):
-    chunks, others = refs[:NEAR], refs[NEAR : NEAR + far - 1][::-1]
-    parts, out_ref = refs[NEAR + far - 1 : -1], refs[-1]
-    visits = parts[0].shape[0]
+        out_ref[k] = sum((part[k] for part in before), both[:ROWS] + col * both[ROWS:])
+
+
+def final_kernel(order, hot_ref, *refs):
+    nears, fars = refs[:NEAR], dict(zip(order, refs[NEAR:]))
+    value_ref, out_ref = refs[-2:]
     block = CAP * TILE_ROWS
-    goal = placing(note_ref[...], far * NEAR)
+    visits = hot_ref.shape[0]
+    span = visits * block
     total = jnp.zeros((ACROSS * ROWS, LANES), F32)
     sums = [jnp.zeros((ROWS, LANES), F32) for _ in range(ACROSS)]
     for k in range(visits):
-        lines = slice(k * block, (k + 1) * block)
         received = []
         for y in range(NEAR):
-            received += [chunks[y][0, lines, :]] + [other[y, lines, :] for other in others]
-        weight = placed(goal[k : k + 1], jnp.concatenate(received, axis=0))
+            received.append(nears[y][part_of(0, span, k, block), :])
+            received += [fars[x][part_of(y, span, k, block), :] for x in sorted(order)]
+        weight = jnp.dot(hot_ref[k], jnp.concatenate(received, axis=0), preferred_element_type=F32)
         total = total + weight
         for c in range(ACROSS):
-            lanes = slice(c * LANES, (c + 1) * LANES)
-            value = parts[0][k, :, lanes]
-            for other in parts[1:]:
-                value = value + other[k, :, lanes]
+            value = value_ref[k, :, c * LANES : (c + 1) * LANES]
             sums[c] = sums[c] + weight[c * ROWS : (c + 1) * ROWS] * value
     for c in range(ACROSS):
         out_ref[0, :, c * LANES : (c + 1) * LANES] = sums[c] / total[c * ROWS : (c + 1) * ROWS]
@@ -286,12 +315,12 @@
     return jax.ShapeDtypeStruct(dims, kind)
 
 
-def filter_rows(frame, table, mix, name):
+def filter_rows(frame, table, mix, before, name):
     visits, _, height, _ = frame.shape
     return pl.pallas_call(
         filter_kernel,
         out_shape=shape((visits, ROWS, COLS), F32),
-        in_specs=[vmem()] * 3,
+        in_specs=[vmem()] * (3 + len(before)),
         out_specs=vmem(),
         scratch_shapes=[
             pltpu.VMEM((visits * ACROSS * height, PAIR), BF16),
@@ -300,14 +329,14 @@
         compiler_params=params(),
         cost_estimate=cost(4 * visits * ACROSS * height * PAIR * BASIS * LANES, 4 * 1024 * 1024),
         name=name,
-    )(frame, table, mix)
-
-
-def regroup(parts, after, name, backward=False):
-    count = parts[0].shape[0]
+    )(frame, table, mix, *before)
+
+
+def regroup(parts, count, span, tail, after, name):
+    rows = len(parts) * span + (TILE_ROWS if tail else 0)
     return pl.pallas_call(
-        functools.partial(regroup_kernel, len(parts), backward),
-        out_shape=tuple(shape((len(parts),) + parts[0].shape[1:], BF16) for _ in range(count - 1)),
+        functools.partial(regroup_kernel, len(parts), span, len(after)),
+        out_shape=(shape((rows, LANES), BF16),) * (count - 1),
         in_specs=[vmem()] * len(parts) + [pl.BlockSpec(memory_space=pl.ANY)] * len(after),
         out_specs=(vmem(),) * (count - 1),
         compiler_params=params(),
@@ -328,12 +357,14 @@
     def swap(value, step):
         return lax.ppermute(value, "patch", [(i, i ^ step) for i in range(patches)])
 
+    span = visits * block
+    fars = range(1, far)
     packed = pl.pallas_call(
         functools.partial(pack_kernel, far),
-        out_shape=(shape((NEAR, visits * block + TILE_ROWS, LANES), BF16),) * far
-        + (shape((far, visits * block, LANES), BF16),) * NEAR,
-        in_specs=[pl.BlockSpec(memory_space=pltpu.HBM)] * 4,
-        out_specs=(vmem(),) * (far + NEAR),
+        out_shape=(shape((NEAR * span + TILE_ROWS, LANES), BF16),) * (far - 1)
+        + (shape(((far + 1) * span + TILE_ROWS, LANES), BF16),) * NEAR,
+        in_specs=[hbm()] * 4,
+        out_specs=(vmem(),) * (far - 1 + NEAR),
         scratch_shapes=[
             pltpu.VMEM(dest_patch.shape, I32),
             pltpu.VMEM(dest_block.shape, I32),
@@ -341,11 +372,11 @@
             pltpu.VMEM(weight.shape, BF16),
             pltpu.SemaphoreType.DMA((4,)),
         ],
-        compiler_params=params(60),
+        compiler_params=params(),
         name="pack",
-    )(dest_patch, dest_block, flux, weight)
-    flux_far = [swap(packed[x], x * NEAR) for x in range(far - 1, 0, -1)] + [packed[0]]
-    weight_near = [packed[far]] + [swap(packed[far + y], y) for y in range(1, NEAR)]
+    )(*map(in_hbm, (dest_patch, dest_block, flux, weight)))
+    chunks = [swap(packed[x - 1], x * NEAR) for x in fars]
+    nears = [packed[far - 1]] + [swap(packed[far - 1 + y], y) for y in range(1, NEAR)]
 
     coefs = spatial.reshape(visits * 3, 1, BASIS)
     taps = basis.transpose(1, 0, 2)
@@ -358,12 +389,17 @@
                 shape((visits, 2 * ROWS, GROUPS * ROWS), BF16),
                 shape((visits, 2 * ROWS, GROUPS * HALO), BF16),
             ),
-            in_specs=[smem()] + [vmem()] * 2,
+            in_specs=[smem()] + [hbm()] * 2,
             out_specs=(vmem(),) * 3,
+            scratch_shapes=[
+                pltpu.VMEM(taps.shape, BF16),
+                pltpu.VMEM(coefs.shape, F32),
+                pltpu.SemaphoreType.DMA((2,)),
+            ],
             compiler_params=params(),
             cost_estimate=cost(10**9, 4 * 1024 * 1024),
             name="tables",
-        )(up.reshape(1).astype(I32), taps, coefs)
+        )(up.reshape(1).astype(I32), in_hbm(taps), in_hbm(coefs))
 
     if bands == 2:
         ups = [band]
@@ -371,22 +407,26 @@
         ups = [jnp.int32(1), jnp.int32(0)]
     built = [tables(up) for up in ups]
     table, own_mix, _ = built[0]
-    weight_sent = regroup(weight_near, [own_mix], "regroup_weight")
-    weight_far = [swap(weight_sent[x - 1], x * NEAR) for x in range(far - 1, 0, -1)]
-    flux_sent = regroup(flux_far, [weight_sent[0]], "regroup_flux", backward=True)
-    flux_near = [swap(part, y + 1) for y, part in enumerate(flux_sent)]
+    flux_sent = regroup(chunks, NEAR, span, True, [own_mix], "regroup_flux")
+    others = [swap(flux_sent[y - 1], y) for y in range(1, NEAR)]
+    weight_sent = regroup(nears, far, span, False, [flux_sent[0]], "regroup_weight")
+    order = sorted(fars, key=lambda x: (x != far // 2, x != 1, -x))
+    weights = [swap(weight_sent[x - 1], x * NEAR) for x in order]
 
     edge_shape = shape((visits, ACROSS, HALO, LANES), BF16)
     edge_count = 1 if bands == 2 else 2
-    frame, note, *edges = pl.pallas_call(
+    frame, hot, *edges = pl.pallas_call(
         functools.partial(place_kernel, far, bands == 2),
-        out_shape=(shape((visits, ACROSS, ROWS, LANES), BF16), shape((TILE_ROWS, LANES), F32))
+        out_shape=(
+            shape((visits, ACROSS, ROWS, LANES), BF16),
+            shape((visits, ACROSS * ROWS, patches * block), BF16),
+        )
         + (edge_shape,) * edge_count,
-        in_specs=[vmem()] * (far + NEAR - 1),
+        in_specs=[vmem()] * (far + 2 * NEAR - 2),
         out_specs=(vmem(),) * (2 + edge_count),
         compiler_params=params(),
         name="place_flux",
-    )(*flux_far, *flux_near)
+    )(*chunks, *others, *nears)
 
     if bands == 2:
         halos = [lax.ppermute(edges[0], "band", [(0, 1), (1, 0)])]
@@ -396,17 +436,17 @@
             lax.ppermute(edges[1], "band", down),
             lax.ppermute(edges[0], "band", [(j, i) for i, j in down]),
         ]
-    parts = [filter_rows(frame, table, own_mix, "filter_own")]
+    value = filter_rows(frame, table, own_mix, [], "filter_own")
     for halo, (_, _, halo_mix) in zip(halos, built):
-        parts.append(filter_rows(halo, table, halo_mix, "filter_halo"))
+        value = filter_rows(halo, table, halo_mix, [value], "filter_halo")
     return pl.pallas_call(
-        functools.partial(final_kernel, far),
+        functools.partial(final_kernel, order),
         out_shape=shape((1, ROWS, COLS), F32),
-        in_specs=[vmem()] * (NEAR + far + len(parts)),
+        in_specs=[vmem()] * (1 + NEAR + far),
         out_specs=vmem(),
         compiler_params=params(),
         name="final",
-    )(note, *weight_near, *weight_far, *parts)
+    )(hot, *nears, *weights, value)
 
 
 def solution(mesh):

time: 33.1 us -> 30.5 us (0.921)
  waiting for transfers between devices: 9.04 us -> 6.12 us
  starting transfers between devices: 14.5 us -> 16.4 us
  local copies, waits for them, and re-layouts: 1.41 us -> 0 us
    ppermute x12, waiting for transfers between devices: 7.66 us -> 5.09 us  [swap(): return lax.ppermute(value, 'patch', [(i, i ^ step) for i in range(patches)])]
    ppermute x12, starting transfers between devices: 12.9 us -> 14.8 us  [swap(): return lax.ppermute(value, 'patch', [(i, i ^ step) for i in range(patches)])]
    unnamed x8 -> x0, local copies, waits for them, and re-layouts: 1.41 us -> none
    pallas_call x1, Pallas kernels: 2.29 us -> 1.44 us  [per_device(): pl.pallas_call(functools.partial(pack_kernel, far), out_shape=(shape((NEA...]
    pallas_call x1, Pallas kernels: 0.77 us -> 1.51 us  [tables(): pl.pallas_call(functools.partial(table_kernel, bands), out_shape=(shape((...]
    ppermute x1, waiting for transfers between devices: 1.38 us -> 1.02 us  [per_device(): halos = [lax.ppermute(edges[0], 'band', [(0, 1), (1, 0)])]]
  transfers between devices with their start and end apart: 13 -> 13, of which waited for: 7 -> 3; matrix products, arithmetic and copies ran while one was open for 0% -> 0% of each run, Pallas kernels for 14% -> 18%
where the time goes in v3:
time: 30.5 us; the launch traced here: 30.3 us
  starting transfers between devices  16.4 us (54%)
  Pallas kernels  7.66 us (25%)
  waiting for transfers between devices  6.12 us (20%)
    ppermute x12, starting transfers between devices, swap(): return lax.ppermute(value, 'patch', [(i, i ^ step) for i in range(patches)])  14.8 us
    ppermute x12, waiting for transfers between devices, swap(): return lax.ppermute(value, 'patch', [(i, i ^ step) for i in range(patches)])  5.09 us
    pallas_call x2, Pallas kernels, filter_rows(): pl.pallas_call(filter_kernel, out_shape=shape((visits, ROWS, COLS), F32),...  3.33 us
    ppermute x1, starting transfers between devices, per_device(): halos = [lax.ppermute(edges[0], 'band', [(0, 1), (1, 0)])]  1.56 us
    pallas_call x1, Pallas kernels, tables(): pl.pallas_call(functools.partial(table_kernel, bands), out_shape=(shape((...  1.51 us
    pallas_call x1, Pallas kernels, per_device(): pl.pallas_call(functools.partial(pack_kernel, far), out_shape=(shape((NEA...  1.44 us
    ppermute x1, waiting for transfers between devices, per_device(): halos = [lax.ppermute(edges[0], 'band', [(0, 1), (1, 0)])]  1.02 us
    pallas_call x1, Pallas kernels, per_device(): pl.pallas_call(functools.partial(final_kernel, order), out_shape=shape((1...  0.9 us
  transfers between devices with their start and end apart: 13, of which 3 were waited for; matrix products, arithmetic and copies ran while one was open for 0% of the time, Pallas kernels for 18%

profile of v3, /device:TPU:0, one launch (start us, length us, event | category | flops | bytes accessed | tf_op | source)
XLA Modules:
  0.0 30.3 jit_solution(1070675844067222795)
XLA Ops:
  0.0 1.4 %pack.1 = (bf16[392,128]{1,0:T(8,128)(2,1)S(1)}, bf16[392,128]{1,0:T(8,128)(2,1)S(1)}, bf16[392,128]{1,0:T(8,128)(2,1)S(1)}, bf16[488,128]{1,0:T(8,128)(2,1)S(1)...) custom-call(s32[6,16]{1,0:T(8,128)} %dest_hbm.1, s32[6,16]{1,0:T(8,128)} %block_hbm.1, ...), custom_call_target="tpu_custom_call" | custom-call | tf_op jit(solution)/shard_map/pack/pallas_call | solution.py:362
  1.5 3.1 %collective-permute-start = (bf16[392,128]{1,0:T(8,128)(2,1)S(1)}, bf16[392,128]{1,0:T(8,128)(2,1)S(1)}, u32[]{:S(2)}, u32[]{:S(2)}) collective-permute-start(bf16[392,128]{1,0:T(8,128)(2,1)S(1)} %get-tuple-element.24), channel_id=1, source_target_pairs={{0,8},{2,10},{4,12},{6,14},{8,0},{10,2},{12,4},{14,6},{16,24},{18,... | collective-permute-start | bytes 301064 | tf_op jit(solution)/shard_map/ppermute | solution.py:358
  4.5 0.0 collective-permute-start.6
  4.5 2.6 %collective-permute-start.1 = (bf16[392,128]{1,0:T(8,128)(2,1)S(1)}, bf16[392,128]{1,0:T(8,128)(2,1)S(1)}, u32[]{:S(2)}, u32[]{:S(2)}) collective-permute-start(bf16[392,128]{1,0:T(8,128)(2,1)S(1)} %get-tuple-element.25), channel_id=1, source_target_pairs={{0,16},{2,18},{4,20},{6,22},{8,24},{10,26},{12,28},{14,30},{16,0},... | collective-permute-start | bytes 301064 | tf_op jit(solution)/shard_map/ppermute | solution.py:358
  7.1 0.0 collective-permute-start.2
  7.1 1.7 %collective-permute-start.7 = (bf16[488,128]{1,0:T(8,128)(2,1)S(1)}, bf16[488,128]{1,0:T(8,128)(2,1)S(1)}, u32[]{:S(2)}, u32[]{:S(2)}) collective-permute-start(bf16[488,128]{1,0:T(8,128)(2,1)S(1)} %get-tuple-element.33), channel_id=1, source_target_pairs={{0,4},{2,6},{4,0},{6,2},{8,12},{10,14},{12,8},{14,10},{16,20},{18,... | collective-permute-start | bytes 374792 | tf_op jit(solution)/shard_map/ppermute | solution.py:358
  8.9 0.0 collective-permute-done.refs_0_
  8.9 0.0 collective-permute-start.8
  8.9 1.5 %tables.1 = (bf16[256,2816]{1,0:T(8,128)(2,1)S(1)}, bf16[6,64,768]{2,1,0:T(8,128)(2,1)S(1)}, bf16[6,64,384]{2,1,0:T(8,128)(2,1)S(1)}) custom-call(s32[1]{0:T(128)} %bitcast.2.up_ref, bf16[21,2,31]{2,1,0:T(2,128)(2,1)} %bitcast.7, f32[18,1,21]{2,1,0:T(1,128)} %bitcast.8), custom_call_target="tpu_custom_call" | custom-call | flops 1000000000 | bytes 4194304 | tf_op jit(solution)/shard_map/tables/pallas_call | solution.py:385
  10.4 4.8 %collective-permute-done.1.refs_1_ = bf16[392,128]{1,0:T(8,128)(2,1)S(1)} collective-permute-done((bf16[392,128]{1,0:T(8,128)(2,1)S(1)}, bf16[392,128]{1,0:T(8,128)(2,1)S(1)}, u32[]{:S(2)}, u32[]{:S(2)}) %collective-permute-start.1) | collective-permute-done | bytes 100384 | tf_op jit(solution)/shard_map/ppermute | solution.py:358
  15.2 0.0 collective-permute-done.2.refs_2_
  15.2 1.6 %collective-permute-start.4 = (bf16[296,128]{1,0:T(8,128)(2,1)S(1)}, bf16[296,128]{1,0:T(8,128)(2,1)S(1)}, u32[]{:S(2)}, u32[]{:S(2)}) collective-permute-start(bf16[296,128]{1,0:T(8,128)(2,1)S(1)} %get-tuple-element.29), channel_id=1, source_target_pairs={{0,4},{2,6},{4,0},{6,2},{8,12},{10,14},{12,8},{14,10},{16,20},{18,... | collective-permute-start | bytes 227336 | tf_op jit(solution)/shard_map/ppermute | solution.py:358
  16.8 0.0 collective-permute-start.5
  16.8 0.0 collective-permute-done.6.refs_7_.refs_1_
  16.8 0.6 %collective-permute-start.3 = (bf16[296,128]{1,0:T(8,128)(2,1)S(1)}, bf16[296,128]{1,0:T(8,128)(2,1)S(1)}, u32[]{:S(2)}, u32[]{:S(2)}) collective-permute-start(bf16[296,128]{1,0:T(8,128)(2,1)S(1)} %get-tuple-element.28.refs_4_), channel_id=1, source_target_pairs={{0,2},{2,0},{4,6},{6,4},{8,10},{10,8},{12,14},{14,12},{16,18},{18,... | collective-permute-start | bytes 227336 | tf_op jit(solution)/shard_map/ppermute | solution.py:358
  17.4 0.0 collective-permute-done.7.refs_8_.refs_2_
  17.4 0.0 collective-permute-done.8.refs_9_.refs_3_
  17.4 3.7 %collective-permute-start.9 = (bf16[384,128]{1,0:T(8,128)(2,1)S(1)}, bf16[384,128]{1,0:T(8,128)(2,1)S(1)}, u32[]{:S(2)}, u32[]{:S(2)}) collective-permute-start(bf16[384,128]{1,0:T(8,128)(2,1)S(1)} %get-tuple-element.36), channel_id=1, source_target_pairs={{0,16},{2,18},{4,20},{6,22},{8,24},{10,26},{12,28},{14,30},{16,0},... | collective-permute-start | bytes 294920 | tf_op jit(solution)/shard_map/ppermute | solution.py:358
  21.1 0.0 collective-permute-start.10
  21.1 0.0 collective-permute-done.4.refs_4_
  21.1 1.5 %collective-permute-start.11 = (bf16[384,128]{1,0:T(8,128)(2,1)S(1)}, bf16[384,128]{1,0:T(8,128)(2,1)S(1)}, u32[]{:S(2)}, u32[]{:S(2)}) collective-permute-start(bf16[384,128]{1,0:T(8,128)(2,1)S(1)} %get-tuple-element.38), channel_id=1, source_target_pairs={{0,24},{2,26},{4,28},{6,30},{8,16},{10,18},{12,20},{14,22},{16,8},... | collective-permute-start | bytes 294920 | tf_op jit(solution)/shard_map/ppermute | solution.py:358
  22.6 0.0 collective-permute-done.5.refs_5_
  22.6 0.0 collective-permute-done.3.refs_3_
  22.6 0.4 %place_flux.1 = (bf16[6,4,32,128]{3,2,1,0:T(8,128)(2,1)S(1)}, bf16[6,128,256]{2,1,0:T(8,128)(2,1)S(1)}, bf16[6,4,16,128]{3,2,1,0:T(8,128)(2,1)S(1)}) custom-call(bf16[392,128]{1,0:T(8,128)(2,1)S(1)} %collective-permute-done.refs_0_, bf16[392,128]{1,0:T(8,128)(2,1)S(1)} %collective-permute-done.1.refs_1_, ...), custom_call_target="tpu_custom_call" | custom-call | tf_op jit(solution)/shard_map/place_flux/pallas_call | solution.py:418
  23.1 1.6 %collective-permute-start.12 = (bf16[6,4,16,128]{3,2,1,0:T(8,128)(2,1)S(1)}, bf16[6,4,16,128]{3,2,1,0:T(8,128)(2,1)S(1)}, u32[]{:S(2)}, u32[]{:S(2)}) collective-permute-start(bf16[6,4,16,128]{3,2,1,0:T(8,128)(2,1)S(1)} %get-tuple-element.39), channel_id=1, source_target_pairs={{0,1},{1,0},{2,3},{3,2},{4,5},{5,4},{6,7},{7,6},{8,9},{9,8},{10,11... | collective-permute-start | bytes 294920 | tf_op jit(solution)/shard_map/ppermute | solution.py:432
  24.6 2.1 %filter_own.1.refs_0_ = f32[6,32,512]{2,1,0:T(8,128)S(1)} custom-call(bf16[6,4,32,128]{3,2,1,0:T(8,128)(2,1)S(1)} %get-tuple-element.42.frame_ref, bf16[256,2816]{1,0:T(8,128)(2,1)S(1)} %get-tuple-element.40.table_ref, bf16[6,64,768]{2,1,0:T(8,128)(2,1)S(1)} %get-tuple-element.27.refs_3_.mix_ref), custom_call_target="tpu_custom_call" | custom-call | flops 2113929216 | bytes 4194304 | tf_op jit(solution)/shard_map/filter_own/pallas_call | solution.py:320
  26.7 1.0 %collective-permute-done.12.frame_ref = bf16[6,4,16,128]{3,2,1,0:T(8,128)(2,1)S(1)} collective-permute-done((bf16[6,4,16,128]{3,2,1,0:T(8,128)(2,1)S(1)}, bf16[6,4,16,128]{3,2,1,0:T(8,128)(2,1)S(1)}, u32[]{:S(2)}, u32[]{:S(2)}) %collective-permute-start.12) | collective-permute-done | bytes 98336 | tf_op jit(solution)/shard_map/ppermute | solution.py:432
  27.8 1.2 %filter_halo.1.refs_7_ = f32[6,32,512]{2,1,0:T(8,128)S(1)} custom-call(bf16[6,4,16,128]{3,2,1,0:T(8,128)(2,1)S(1)} %collective-permute-done.12.frame_ref, bf16[256,2816]{1,0:T(8,128)(2,1)S(1)} %get-tuple-element.40.table_ref, bf16[6,64,384]{2,1,0:T(8,128)(2,1)S(1)} %get-tuple-element.41.mix_ref, f32[6,32,512]{2,1,0:T(8,128)S(1)} %filter_own.1.refs_0_), custom_call_target="tpu_custom_call" | custom-call | flops 1056964608 | bytes 4194304 | tf_op jit(solution)/shard_map/filter_halo/pallas_call | solution.py:320
  29.0 0.0 collective-permute-done.9.refs_4_
  29.0 0.0 collective-permute-done.10.refs_5_
  29.0 0.3 %collective-permute-done.11.refs_6_ = bf16[384,128]{1,0:T(8,128)(2,1)S(1)} collective-permute-done((bf16[384,128]{1,0:T(8,128)(2,1)S(1)}, bf16[384,128]{1,0:T(8,128)(2,1)S(1)}, u32[]{:S(2)}, u32[]{:S(2)}) %collective-permute-start.11) | collective-permute-done | bytes 98336 | tf_op jit(solution)/shard_map/ppermute | solution.py:358
  29.4 0.9 %final.1 = f32[1,32,512]{2,1,0:T(8,128)} custom-call(bf16[6,128,256]{2,1,0:T(8,128)(2,1)S(1)} %get-tuple-element.35.hot_ref, bf16[488,128]{1,0:T(8,128)(2,1)S(1)} %get-tuple-element.31.refs_6_.refs_0_, bf16[488,128]{1,0:T(8,128)(2,1)S(1)} %collective-permute-done.6.refs_7_.refs_1_, bf16[488,128]{1,0:T(8,128)(2,1)S(1)} %collective-permute-done.7.refs_8_.refs_2_, ...), custom_call_target="tpu_custom_call" | custom-call | tf_op jit(solution)/shard_map/final/pallas_call | solution.py:442
  (2 shorter events, 0.0 us)
Async XLA Ops:
  1.5 7.4 %collective-permute-start = (bf16[392,128]{1,0:T(8,128)(2,1)S(1)}, bf16[392,128]{1,0:T(8,128)(2,1)S(1)}, u32[]{:S(2)}, u32[]{:S(2)}) collective-permute-start(bf16[392,128]{1,0:T(8,128)(2,1)S(1)} %get-tuple-element.24), channel_id=1, source_target_pairs={{0,8},{2,10},{4,12},{6,14},{8,0},{10,2},{12,4},{14,6},{16,24},{18,... | collective-permute-start | bytes 301064 | tf_op jit(solution)/shard_map/ppermute | solution.py:358
  4.5 12.2 %collective-permute-start.6 = (bf16[488,128]{1,0:T(8,128)(2,1)S(1)}, bf16[488,128]{1,0:T(8,128)(2,1)S(1)}, u32[]{:S(2)}, u32[]{:S(2)}) collective-permute-start(bf16[488,128]{1,0:T(8,128)(2,1)S(1)} %get-tuple-element.32), channel_id=1, source_target_pairs={{0,2},{2,0},{4,6},{6,4},{8,10},{10,8},{12,14},{14,12},{16,18},{18,... | collective-permute-start | bytes 374792 | tf_op jit(solution)/shard_map/ppermute | solution.py:358
  4.5 10.6 %collective-permute-start.1 = (bf16[392,128]{1,0:T(8,128)(2,1)S(1)}, bf16[392,128]{1,0:T(8,128)(2,1)S(1)}, u32[]{:S(2)}, u32[]{:S(2)}) collective-permute-start(bf16[392,128]{1,0:T(8,128)(2,1)S(1)} %get-tuple-element.25), channel_id=1, source_target_pairs={{0,16},{2,18},{4,20},{6,22},{8,24},{10,26},{12,28},{14,30},{16,0},... | collective-permute-start | bytes 301064 | tf_op jit(solution)/shard_map/ppermute | solution.py:358
  7.1 8.0 %collective-permute-start.2 = (bf16[392,128]{1,0:T(8,128)(2,1)S(1)}, bf16[392,128]{1,0:T(8,128)(2,1)S(1)}, u32[]{:S(2)}, u32[]{:S(2)}) collective-permute-start(bf16[392,128]{1,0:T(8,128)(2,1)S(1)} %get-tuple-element.26), channel_id=1, source_target_pairs={{0,24},{2,26},{4,28},{6,30},{8,16},{10,18},{12,20},{14,22},{16,8},... | collective-permute-start | bytes 301064 | tf_op jit(solution)/shard_map/ppermute | solution.py:358
  7.1 10.3 %collective-permute-start.7 = (bf16[488,128]{1,0:T(8,128)(2,1)S(1)}, bf16[488,128]{1,0:T(8,128)(2,1)S(1)}, u32[]{:S(2)}, u32[]{:S(2)}) collective-permute-start(bf16[488,128]{1,0:T(8,128)(2,1)S(1)} %get-tuple-element.33), channel_id=1, source_target_pairs={{0,4},{2,6},{4,0},{6,2},{8,12},{10,14},{12,8},{14,10},{16,20},{18,... | collective-permute-start | bytes 374792 | tf_op jit(solution)/shard_map/ppermute | solution.py:358
  8.9 8.5 %collective-permute-start.8 = (bf16[488,128]{1,0:T(8,128)(2,1)S(1)}, bf16[488,128]{1,0:T(8,128)(2,1)S(1)}, u32[]{:S(2)}, u32[]{:S(2)}) collective-permute-start(bf16[488,128]{1,0:T(8,128)(2,1)S(1)} %get-tuple-element.34), channel_id=1, source_target_pairs={{0,6},{2,4},{4,2},{6,0},{8,14},{10,12},{12,10},{14,8},{16,22},{18,... | collective-permute-start | bytes 374792 | tf_op jit(solution)/shard_map/ppermute | solution.py:358
  15.2 5.9 %collective-permute-start.4 = (bf16[296,128]{1,0:T(8,128)(2,1)S(1)}, bf16[296,128]{1,0:T(8,128)(2,1)S(1)}, u32[]{:S(2)}, u32[]{:S(2)}) collective-permute-start(bf16[296,128]{1,0:T(8,128)(2,1)S(1)} %get-tuple-element.29), channel_id=1, source_target_pairs={{0,4},{2,6},{4,0},{6,2},{8,12},{10,14},{12,8},{14,10},{16,20},{18,... | collective-permute-start | bytes 227336 | tf_op jit(solution)/shard_map/ppermute | solution.py:358
  16.8 5.9 %collective-permute-start.5 = (bf16[296,128]{1,0:T(8,128)(2,1)S(1)}, bf16[296,128]{1,0:T(8,128)(2,1)S(1)}, u32[]{:S(2)}, u32[]{:S(2)}) collective-permute-start(bf16[296,128]{1,0:T(8,128)(2,1)S(1)} %get-tuple-element.30), channel_id=1, source_target_pairs={{0,6},{2,4},{4,2},{6,0},{8,14},{10,12},{12,10},{14,8},{16,22},{18,... | collective-permute-start | bytes 227336 | tf_op jit(solution)/shard_map/ppermute | solution.py:358
  16.8 5.9 %collective-permute-start.3 = (bf16[296,128]{1,0:T(8,128)(2,1)S(1)}, bf16[296,128]{1,0:T(8,128)(2,1)S(1)}, u32[]{:S(2)}, u32[]{:S(2)}) collective-permute-start(bf16[296,128]{1,0:T(8,128)(2,1)S(1)} %get-tuple-element.28.refs_4_), channel_id=1, source_target_pairs={{0,2},{2,0},{4,6},{6,4},{8,10},{10,8},{12,14},{14,12},{16,18},{18,... | collective-permute-start | bytes 227336 | tf_op jit(solution)/shard_map/ppermute | solution.py:358
  17.4 11.6 %collective-permute-start.9 = (bf16[384,128]{1,0:T(8,128)(2,1)S(1)}, bf16[384,128]{1,0:T(8,128)(2,1)S(1)}, u32[]{:S(2)}, u32[]{:S(2)}) collective-permute-start(bf16[384,128]{1,0:T(8,128)(2,1)S(1)} %get-tuple-element.36), channel_id=1, source_target_pairs={{0,16},{2,18},{4,20},{6,22},{8,24},{10,26},{12,28},{14,30},{16,0},... | collective-permute-start | bytes 294920 | tf_op jit(solution)/shard_map/ppermute | solution.py:358
  21.1 7.9 %collective-permute-start.10 = (bf16[384,128]{1,0:T(8,128)(2,1)S(1)}, bf16[384,128]{1,0:T(8,128)(2,1)S(1)}, u32[]{:S(2)}, u32[]{:S(2)}) collective-permute-start(bf16[384,128]{1,0:T(8,128)(2,1)S(1)} %get-tuple-element.37), channel_id=1, source_target_pairs={{0,8},{2,10},{4,12},{6,14},{8,0},{10,2},{12,4},{14,6},{16,24},{18,... | collective-permute-start | bytes 294920 | tf_op jit(solution)/shard_map/ppermute | solution.py:358
  21.1 8.2 %collective-permute-start.11 = (bf16[384,128]{1,0:T(8,128)(2,1)S(1)}, bf16[384,128]{1,0:T(8,128)(2,1)S(1)}, u32[]{:S(2)}, u32[]{:S(2)}) collective-permute-start(bf16[384,128]{1,0:T(8,128)(2,1)S(1)} %get-tuple-element.38), channel_id=1, source_target_pairs={{0,24},{2,26},{4,28},{6,30},{8,16},{10,18},{12,20},{14,22},{16,8},... | collective-permute-start | bytes 294920 | tf_op jit(solution)/shard_map/ppermute | solution.py:358
  23.1 4.7 %collective-permute-start.12 = (bf16[6,4,16,128]{3,2,1,0:T(8,128)(2,1)S(1)}, bf16[6,4,16,128]{3,2,1,0:T(8,128)(2,1)S(1)}, u32[]{:S(2)}, u32[]{:S(2)}) collective-permute-start(bf16[6,4,16,128]{3,2,1,0:T(8,128)(2,1)S(1)} %get-tuple-element.39), channel_id=1, source_target_pairs={{0,1},{1,0},{2,3},{3,2},{4,5},{5,4},{6,7},{7,6},{8,9},{9,8},{10,11... | collective-permute-start | bytes 294920 | tf_op jit(solution)/shard_map/ppermute | solution.py:432

commit v4 on v3

--- a/solution.py
+++ b/solution.py
@@ -131,8 +131,13 @@
     return slice(i * span + k * block, i * span + (k + 1) * block)
 
 
-def regroup_kernel(count, span, skip, *refs):
-    ins = refs[:count]
+def sorted_refs(order, refs):
+    return [ref for _, ref in sorted(zip(order, refs), key=lambda pair: pair[0])]
+
+
+def regroup_kernel(order, span, skip, *refs):
+    count = len(order)
+    ins = sorted_refs(order, refs)
     outs = refs[count + skip :]
     for j, out in enumerate(outs):
         for i, part in enumerate(ins):
@@ -149,8 +154,8 @@
     return place * TILE_ROWS + iota((TILE_ROWS, width), 1) % TILE_ROWS
 
 
-def place_kernel(far, swap, *refs):
-    chunks, others = refs[: far - 1], refs[far - 1 : far + NEAR - 2]
+def place_kernel(far, order, swap, *refs):
+    chunks, others = sorted_refs(order, refs[: far - 1]), refs[far - 1 : far + NEAR - 2]
     nears, (frame_ref, hot_ref, *edges) = refs[far + NEAR - 2 : far + 2 * NEAR - 2], refs[far + 2 * NEAR - 2 :]
     visits = frame_ref.shape[0]
     block = CAP * TILE_ROWS
@@ -257,8 +262,12 @@
     )
 
 
-def filter_kernel(frame_ref, table_ref, mix_ref, *refs):
-    before, (out_ref, windows, filtered) = refs[:-3], refs[-3:]
+def filter_kernel(order, frame_ref, table_ref, mix_ref, *refs):
+    (*others, out_ref, windows, filtered) = refs
+    weighing = []
+    if order:
+        count = 1 + NEAR + len(order)
+        others, weighing = others[:-count], others[-count:]
     visits, _, height, _ = frame_ref.shape
     half = LANES // 2
     left = iota((height, LANES), 1) < half
@@ -284,43 +293,44 @@
                         k * count + c * height : k * count + (c + 1) * height, j * LANES : (j + 1) * LANES
                     ]
     col = (2.0 * iota((1, COLS), 1).astype(F32) + 1.0) / COLS - 1.0
+    total, sums = 0.0, [0.0] * ACROSS
     for k in range(visits):
         both = jnp.dot(mix_ref[k], filtered[k], preferred_element_type=F32)
-        out_ref[k] = sum((part[k] for part in before), both[:ROWS] + col * both[ROWS:])
-
-
-def final_kernel(order, hot_ref, *refs):
-    nears, fars = refs[:NEAR], dict(zip(order, refs[NEAR:]))
-    value_ref, out_ref = refs[-2:]
+        value = sum((part[k] for part in others), both[:ROWS] + col * both[ROWS:])
+        if order:
+            weight = weight_of(k, order, *weighing)
+            total = total + weight
+            for c in range(ACROSS):
+                part = value[:, c * LANES : (c + 1) * LANES]
+                sums[c] = sums[c] + weight[c * ROWS : (c + 1) * ROWS] * part
+        else:
+            out_ref[k] = value
+    if order:
+        for c in range(ACROSS):
+            out_ref[0, :, c * LANES : (c + 1) * LANES] = sums[c] / total[c * ROWS : (c + 1) * ROWS]
+
+
+def weight_of(k, order, hot_ref, *refs):
+    nears, fars = refs[:NEAR], sorted_refs(order, refs[NEAR:])
     block = CAP * TILE_ROWS
-    visits = hot_ref.shape[0]
-    span = visits * block
-    total = jnp.zeros((ACROSS * ROWS, LANES), F32)
-    sums = [jnp.zeros((ROWS, LANES), F32) for _ in range(ACROSS)]
-    for k in range(visits):
-        received = []
-        for y in range(NEAR):
-            received.append(nears[y][part_of(0, span, k, block), :])
-            received += [fars[x][part_of(y, span, k, block), :] for x in sorted(order)]
-        weight = jnp.dot(hot_ref[k], jnp.concatenate(received, axis=0), preferred_element_type=F32)
-        total = total + weight
-        for c in range(ACROSS):
-            value = value_ref[k, :, c * LANES : (c + 1) * LANES]
-            sums[c] = sums[c] + weight[c * ROWS : (c + 1) * ROWS] * value
-    for c in range(ACROSS):
-        out_ref[0, :, c * LANES : (c + 1) * LANES] = sums[c] / total[c * ROWS : (c + 1) * ROWS]
+    span = hot_ref.shape[0] * block
+    received = []
+    for y in range(NEAR):
+        received.append(nears[y][part_of(0, span, k, block), :])
+        received += [ref[part_of(y, span, k, block), :] for ref in fars]
+    return jnp.dot(hot_ref[k], jnp.concatenate(received, axis=0), preferred_element_type=F32)
 
 
 def shape(dims, kind):
     return jax.ShapeDtypeStruct(dims, kind)
 
 
-def filter_rows(frame, table, mix, before, name):
+def filter_rows(frame, table, mix, before, name, order=(), weighing=()):
     visits, _, height, _ = frame.shape
     return pl.pallas_call(
-        filter_kernel,
-        out_shape=shape((visits, ROWS, COLS), F32),
-        in_specs=[vmem()] * (3 + len(before)),
+        functools.partial(filter_kernel, order),
+        out_shape=shape((1 if order else visits, ROWS, COLS), F32),
+        in_specs=[vmem()] * (3 + len(before) + len(weighing)),
         out_specs=vmem(),
         scratch_shapes=[
             pltpu.VMEM((visits * ACROSS * height, PAIR), BF16),
@@ -329,13 +339,13 @@
         compiler_params=params(),
         cost_estimate=cost(4 * visits * ACROSS * height * PAIR * BASIS * LANES, 4 * 1024 * 1024),
         name=name,
-    )(frame, table, mix, *before)
-
-
-def regroup(parts, count, span, tail, after, name):
+    )(frame, table, mix, *before, *weighing)
+
+
+def regroup(parts, order, count, span, tail, after, name):
     rows = len(parts) * span + (TILE_ROWS if tail else 0)
     return pl.pallas_call(
-        functools.partial(regroup_kernel, len(parts), span, len(after)),
+        functools.partial(regroup_kernel, order, span, len(after)),
         out_shape=(shape((rows, LANES), BF16),) * (count - 1),
         in_specs=[vmem()] * len(parts) + [pl.BlockSpec(memory_space=pl.ANY)] * len(after),
         out_specs=(vmem(),) * (count - 1),
@@ -375,7 +385,8 @@
         compiler_params=params(),
         name="pack",
     )(*map(in_hbm, (dest_patch, dest_block, flux, weight)))
-    chunks = [swap(packed[x - 1], x * NEAR) for x in fars]
+    first = sorted(fars, key=lambda x: (x != far - 1, x))
+    chunks = [swap(packed[x - 1], x * NEAR) for x in first]
     nears = [packed[far - 1]] + [swap(packed[far - 1 + y], y) for y in range(1, NEAR)]
 
     coefs = spatial.reshape(visits * 3, 1, BASIS)
@@ -407,16 +418,16 @@
         ups = [jnp.int32(1), jnp.int32(0)]
     built = [tables(up) for up in ups]
     table, own_mix, _ = built[0]
-    flux_sent = regroup(chunks, NEAR, span, True, [own_mix], "regroup_flux")
+    flux_sent = regroup(chunks, first, NEAR, span, True, [own_mix], "regroup_flux")
     others = [swap(flux_sent[y - 1], y) for y in range(1, NEAR)]
-    weight_sent = regroup(nears, far, span, False, [flux_sent[0]], "regroup_weight")
+    weight_sent = regroup(nears, list(range(NEAR)), far, span, False, [flux_sent[0]], "regroup_weight")
     order = sorted(fars, key=lambda x: (x != far // 2, x != 1, -x))
     weights = [swap(weight_sent[x - 1], x * NEAR) for x in order]
 
     edge_shape = shape((visits, ACROSS, HALO, LANES), BF16)
     edge_count = 1 if bands == 2 else 2
     frame, hot, *edges = pl.pallas_call(
-        functools.partial(place_kernel, far, bands == 2),
+        functools.partial(place_kernel, far, first, bands == 2),
         out_shape=(
             shape((visits, ACROSS, ROWS, LANES), BF16),
             shape((visits, ACROSS * ROWS, patches * block), BF16),
@@ -437,16 +448,10 @@
             lax.ppermute(edges[0], "band", [(j, i) for i, j in down]),
         ]
     value = filter_rows(frame, table, own_mix, [], "filter_own")
-    for halo, (_, _, halo_mix) in zip(halos, built):
+    for halo, (_, _, halo_mix) in zip(halos[:-1], built):
         value = filter_rows(halo, table, halo_mix, [value], "filter_halo")
-    return pl.pallas_call(
-        functools.partial(final_kernel, order),
-        out_shape=shape((1, ROWS, COLS), F32),
-        in_specs=[vmem()] * (1 + NEAR + far),
-        out_specs=vmem(),
-        compiler_params=params(),
-        name="final",
-    )(hot, *nears, *weights, value)
+    weighing = (hot, *nears, *weights)
+    return filter_rows(halos[-1], table, built[-1][2], [value], "filter_halo_weigh", order, weighing)
 
 
 def solution(mesh):

time: 30.5 us -> 29.6 us (0.970)
  starting transfers between devices: 16.4 us -> 15.9 us
    ppermute x1, waiting for transfers between devices: 1.02 us -> 0.01 us  [per_device(): halos = [lax.ppermute(edges[0], 'band', [(0, 1), (1, 0)])]]
    ppermute x12, waiting for transfers between devices: 5.09 us -> 5.98 us  [swap(): return lax.ppermute(value, 'patch', [(i, i ^ step) for i in range(patches)])]
    ppermute x12, starting transfers between devices: 14.8 us -> 14.3 us  [swap(): return lax.ppermute(value, 'patch', [(i, i ^ step) for i in range(patches)])]
    pallas_call x6 -> x5, Pallas kernels: 4.71 us -> 4.49 us  [the longest x2 4.02 us: filter_rows(): pl.pallas_call(functools.partial(filter_kernel, order), out_shape=shape((...]
  transfers between devices with their start and end apart: 13 -> 13, of which waited for: 3 -> 5; matrix products, arithmetic and copies ran while one was open for 0% -> 0% of each run, Pallas kernels for 18% -> 14%
where the time goes in v4:
time: 29.6 us; the launch traced here: 29.4 us
  starting transfers between devices  15.9 us (54%)
  Pallas kernels  7.45 us (25%)
  waiting for transfers between devices  5.98 us (20%)
    ppermute x12, starting transfers between devices, swap(): return lax.ppermute(value, 'patch', [(i, i ^ step) for i in range(patches)])  14.3 us
    ppermute x12, waiting for transfers between devices, swap(): return lax.ppermute(value, 'patch', [(i, i ^ step) for i in range(patches)])  5.98 us
    pallas_call x2, Pallas kernels, filter_rows(): pl.pallas_call(functools.partial(filter_kernel, order), out_shape=shape((...  4.02 us
    ppermute x1, starting transfers between devices, per_device(): halos = [lax.ppermute(edges[0], 'band', [(0, 1), (1, 0)])]  1.55 us
    pallas_call x1, Pallas kernels, tables(): pl.pallas_call(functools.partial(table_kernel, bands), out_shape=(shape((...  1.51 us
    pallas_call x1, Pallas kernels, per_device(): pl.pallas_call(functools.partial(pack_kernel, far), out_shape=(shape((NEA...  1.44 us
  transfers between devices with their start and end apart: 13, of which 5 were waited for; matrix products, arithmetic and copies ran while one was open for 0% of the time, Pallas kernels for 14%

profile of v4, /device:TPU:0, one launch (start us, length us, event | category | flops | bytes accessed | tf_op | source)
XLA Modules:
  0.0 29.4 jit_solution(9396153558771908865)
XLA Ops:
  0.0 1.4 %pack.1 = (bf16[392,128]{1,0:T(8,128)(2,1)S(1)}, bf16[392,128]{1,0:T(8,128)(2,1)S(1)}, bf16[392,128]{1,0:T(8,128)(2,1)S(1)}, bf16[488,128]{1,0:T(8,128)(2,1)S(1)...) custom-call(s32[6,16]{1,0:T(8,128)} %dest_hbm.1, s32[6,16]{1,0:T(8,128)} %block_hbm.1, ...), custom_call_target="tpu_custom_call" | custom-call | tf_op jit(solution)/shard_map/pack/pallas_call | solution.py:372
  1.5 5.1 %collective-permute-start = (bf16[392,128]{1,0:T(8,128)(2,1)S(1)}, bf16[392,128]{1,0:T(8,128)(2,1)S(1)}, u32[]{:S(2)}, u32[]{:S(2)}) collective-permute-start(bf16[392,128]{1,0:T(8,128)(2,1)S(1)} %get-tuple-element.24), channel_id=1, source_target_pairs={{0,24},{2,26},{4,28},{6,30},{8,16},{10,18},{12,20},{14,22},{16,8},... | collective-permute-start | bytes 301064 | tf_op jit(solution)/shard_map/ppermute | solution.py:368
  6.6 0.0 collective-permute-start.6
  6.6 0.0 collective-permute-start.1
  6.6 0.7 %collective-permute-start.2 = (bf16[392,128]{1,0:T(8,128)(2,1)S(1)}, bf16[392,128]{1,0:T(8,128)(2,1)S(1)}, u32[]{:S(2)}, u32[]{:S(2)}) collective-permute-start(bf16[392,128]{1,0:T(8,128)(2,1)S(1)} %get-tuple-element.26), channel_id=1, source_target_pairs={{0,16},{2,18},{4,20},{6,22},{8,24},{10,26},{12,28},{14,30},{16,0},... | collective-permute-start | bytes 301064 | tf_op jit(solution)/shard_map/ppermute | solution.py:368
  7.3 1.6 %collective-permute-start.7 = (bf16[488,128]{1,0:T(8,128)(2,1)S(1)}, bf16[488,128]{1,0:T(8,128)(2,1)S(1)}, u32[]{:S(2)}, u32[]{:S(2)}) collective-permute-start(bf16[488,128]{1,0:T(8,128)(2,1)S(1)} %get-tuple-element.33), channel_id=1, source_target_pairs={{0,4},{2,6},{4,0},{6,2},{8,12},{10,14},{12,8},{14,10},{16,20},{18,... | collective-permute-start | bytes 374792 | tf_op jit(solution)/shard_map/ppermute | solution.py:368
  8.9 1.4 %collective-permute-done.refs_0_ = bf16[392,128]{1,0:T(8,128)(2,1)S(1)} collective-permute-done((bf16[392,128]{1,0:T(8,128)(2,1)S(1)}, bf16[392,128]{1,0:T(8,128)(2,1)S(1)}, u32[]{:S(2)}, u32[]{:S(2)}) %collective-permute-start) | collective-permute-done | bytes 100384 | tf_op jit(solution)/shard_map/ppermute | solution.py:368
  10.3 0.0 collective-permute-start.8
  10.3 1.5 %tables.1 = (bf16[256,2816]{1,0:T(8,128)(2,1)S(1)}, bf16[6,64,768]{2,1,0:T(8,128)(2,1)S(1)}, bf16[6,64,384]{2,1,0:T(8,128)(2,1)S(1)}) custom-call(s32[1]{0:T(128)} %bitcast.2.up_ref, bf16[21,2,31]{2,1,0:T(2,128)(2,1)} %bitcast.7, f32[18,1,21]{2,1,0:T(1,128)} %bitcast.8), custom_call_target="tpu_custom_call" | custom-call | flops 1000000000 | bytes 4194304 | tf_op jit(solution)/shard_map/tables/pallas_call | solution.py:396
  11.8 1.5 %collective-permute-done.1.refs_1_ = bf16[392,128]{1,0:T(8,128)(2,1)S(1)} collective-permute-done((bf16[392,128]{1,0:T(8,128)(2,1)S(1)}, bf16[392,128]{1,0:T(8,128)(2,1)S(1)}, u32[]{:S(2)}, u32[]{:S(2)}) %collective-permute-start.1) | collective-permute-done | bytes 100384 | tf_op jit(solution)/shard_map/ppermute | solution.py:368
  13.3 1.8 %collective-permute-done.2.refs_2_ = bf16[392,128]{1,0:T(8,128)(2,1)S(1)} collective-permute-done((bf16[392,128]{1,0:T(8,128)(2,1)S(1)}, bf16[392,128]{1,0:T(8,128)(2,1)S(1)}, u32[]{:S(2)}, u32[]{:S(2)}) %collective-permute-start.2) | collective-permute-done | bytes 100384 | tf_op jit(solution)/shard_map/ppermute | solution.py:368
  15.0 1.6 %collective-permute-start.4 = (bf16[296,128]{1,0:T(8,128)(2,1)S(1)}, bf16[296,128]{1,0:T(8,128)(2,1)S(1)}, u32[]{:S(2)}, u32[]{:S(2)}) collective-permute-start(bf16[296,128]{1,0:T(8,128)(2,1)S(1)} %get-tuple-element.29), channel_id=1, source_target_pairs={{0,4},{2,6},{4,0},{6,2},{8,12},{10,14},{12,8},{14,10},{16,20},{18,... | collective-permute-start | bytes 227336 | tf_op jit(solution)/shard_map/ppermute | solution.py:368
  16.6 0.0 collective-permute-start.5
  16.6 0.0 collective-permute-done.6.refs_7_.refs_1_.refs_3_
  16.6 0.6 %collective-permute-start.3 = (bf16[296,128]{1,0:T(8,128)(2,1)S(1)}, bf16[296,128]{1,0:T(8,128)(2,1)S(1)}, u32[]{:S(2)}, u32[]{:S(2)}) collective-permute-start(bf16[296,128]{1,0:T(8,128)(2,1)S(1)} %get-tuple-element.28.refs_4_), channel_id=1, source_target_pairs={{0,2},{2,0},{4,6},{6,4},{8,10},{10,8},{12,14},{14,12},{16,18},{18,... | collective-permute-start | bytes 227336 | tf_op jit(solution)/shard_map/ppermute | solution.py:368
  17.3 0.0 collective-permute-done.7.refs_8_.refs_2_.refs_4_
  17.3 0.0 collective-permute-done.8.refs_9_.refs_3_.refs_5_
  17.3 1.4 %collective-permute-start.10 = (bf16[384,128]{1,0:T(8,128)(2,1)S(1)}, bf16[384,128]{1,0:T(8,128)(2,1)S(1)}, u32[]{:S(2)}, u32[]{:S(2)}) collective-permute-start(bf16[384,128]{1,0:T(8,128)(2,1)S(1)} %get-tuple-element.40), channel_id=1, source_target_pairs={{0,16},{2,18},{4,20},{6,22},{8,24},{10,26},{12,28},{14,30},{16,0},... | collective-permute-start | bytes 294920 | tf_op jit(solution)/shard_map/ppermute | solution.py:368
  18.7 1.7 %collective-permute-start.11 = (bf16[384,128]{1,0:T(8,128)(2,1)S(1)}, bf16[384,128]{1,0:T(8,128)(2,1)S(1)}, u32[]{:S(2)}, u32[]{:S(2)}) collective-permute-start(bf16[384,128]{1,0:T(8,128)(2,1)S(1)} %get-tuple-element.41), channel_id=1, source_target_pairs={{0,8},{2,10},{4,12},{6,14},{8,0},{10,2},{12,4},{14,6},{16,24},{18,... | collective-permute-start | bytes 294920 | tf_op jit(solution)/shard_map/ppermute | solution.py:368
  20.4 0.0 collective-permute-done.4.refs_4_
  20.4 1.6 %collective-permute-start.12 = (bf16[384,128]{1,0:T(8,128)(2,1)S(1)}, bf16[384,128]{1,0:T(8,128)(2,1)S(1)}, u32[]{:S(2)}, u32[]{:S(2)}) collective-permute-start(bf16[384,128]{1,0:T(8,128)(2,1)S(1)} %get-tuple-element.42), channel_id=1, source_target_pairs={{0,24},{2,26},{4,28},{6,30},{8,16},{10,18},{12,20},{14,22},{16,8},... | collective-permute-start | bytes 294920 | tf_op jit(solution)/shard_map/ppermute | solution.py:368
  22.0 0.0 collective-permute-done.5.refs_5_
  22.0 0.0 collective-permute-done.3.refs_3_
  22.0 0.4 %place_flux.1 = (bf16[6,4,32,128]{3,2,1,0:T(8,128)(2,1)S(1)}, bf16[6,128,256]{2,1,0:T(8,128)(2,1)S(1)}, bf16[6,4,16,128]{3,2,1,0:T(8,128)(2,1)S(1)}) custom-call(bf16[392,128]{1,0:T(8,128)(2,1)S(1)} %collective-permute-done.refs_0_, bf16[392,128]{1,0:T(8,128)(2,1)S(1)} %collective-permute-done.1.refs_1_, ...), custom_call_target="tpu_custom_call" | custom-call | tf_op jit(solution)/shard_map/place_flux/pallas_call | solution.py:429
  22.4 1.6 %collective-permute-start.9 = (bf16[6,4,16,128]{3,2,1,0:T(8,128)(2,1)S(1)}, bf16[6,4,16,128]{3,2,1,0:T(8,128)(2,1)S(1)}, u32[]{:S(2)}, u32[]{:S(2)}) collective-permute-start(bf16[6,4,16,128]{3,2,1,0:T(8,128)(2,1)S(1)} %get-tuple-element.35), channel_id=1, source_target_pairs={{0,1},{1,0},{2,3},{3,2},{4,5},{5,4},{6,7},{7,6},{8,9},{9,8},{10,11... | collective-permute-start | bytes 294920 | tf_op jit(solution)/shard_map/ppermute | solution.py:443
  24.0 2.1 %filter_own.1.refs_0_ = f32[6,32,512]{2,1,0:T(8,128)S(1)} custom-call(bf16[6,4,32,128]{3,2,1,0:T(8,128)(2,1)S(1)} %get-tuple-element.38.frame_ref, bf16[256,2816]{1,0:T(8,128)(2,1)S(1)} %get-tuple-element.36.table_ref, bf16[6,64,768]{2,1,0:T(8,128)(2,1)S(1)} %get-tuple-element.27.refs_3_.mix_ref), custom_call_target="tpu_custom_call" | custom-call | flops 2113929216 | bytes 4194304 | tf_op jit(solution)/shard_map/filter_own/pallas_call | solution.py:330
  26.1 1.1 %collective-permute-done.10.refs_6_ = bf16[384,128]{1,0:T(8,128)(2,1)S(1)} collective-permute-done((bf16[384,128]{1,0:T(8,128)(2,1)S(1)}, bf16[384,128]{1,0:T(8,128)(2,1)S(1)}, u32[]{:S(2)}, u32[]{:S(2)}) %collective-permute-start.10) | collective-permute-done | bytes 98336 | tf_op jit(solution)/shard_map/ppermute | solution.py:368
  27.2 0.2 collective-permute-done.11.refs_7_
  27.4 0.0 collective-permute-done.12.refs_8_
  27.5 0.0 collective-permute-done.9.frame_ref
  27.5 1.9 %filter_halo_weigh.1 = f32[1,32,512]{2,1,0:T(8,128)} custom-call(bf16[6,4,16,128]{3,2,1,0:T(8,128)(2,1)S(1)} %collective-permute-done.9.frame_ref, bf16[256,2816]{1,0:T(8,128)(2,1)S(1)} %get-tuple-element.36.table_ref, bf16[6,64,384]{2,1,0:T(8,128)(2,1)S(1)} %get-tuple-element.37.mix_ref, f32[6,32,512]{2,1,0:T(8,128)S(1)} %filter_own.1.refs_0_, ...), custom_call_target="tpu_custom_call" | custom-call | flops 1056964608 | bytes 4194304 | tf_op jit(solution)/shard_map/filter_halo_weigh/pallas_call | solution.py:330
  (2 shorter events, 0.0 us)
Async XLA Ops:
  1.5 8.8 %collective-permute-start = (bf16[392,128]{1,0:T(8,128)(2,1)S(1)}, bf16[392,128]{1,0:T(8,128)(2,1)S(1)}, u32[]{:S(2)}, u32[]{:S(2)}) collective-permute-start(bf16[392,128]{1,0:T(8,128)(2,1)S(1)} %get-tuple-element.24), channel_id=1, source_target_pairs={{0,24},{2,26},{4,28},{6,30},{8,16},{10,18},{12,20},{14,22},{16,8},... | collective-permute-start | bytes 301064 | tf_op jit(solution)/shard_map/ppermute | solution.py:368
  6.6 10.1 %collective-permute-start.6 = (bf16[488,128]{1,0:T(8,128)(2,1)S(1)}, bf16[488,128]{1,0:T(8,128)(2,1)S(1)}, u32[]{:S(2)}, u32[]{:S(2)}) collective-permute-start(bf16[488,128]{1,0:T(8,128)(2,1)S(1)} %get-tuple-element.32), channel_id=1, source_target_pairs={{0,2},{2,0},{4,6},{6,4},{8,10},{10,8},{12,14},{14,12},{16,18},{18,... | collective-permute-start | bytes 374792 | tf_op jit(solution)/shard_map/ppermute | solution.py:368
  6.6 6.7 %collective-permute-start.1 = (bf16[392,128]{1,0:T(8,128)(2,1)S(1)}, bf16[392,128]{1,0:T(8,128)(2,1)S(1)}, u32[]{:S(2)}, u32[]{:S(2)}) collective-permute-start(bf16[392,128]{1,0:T(8,128)(2,1)S(1)} %get-tuple-element.25), channel_id=1, source_target_pairs={{0,8},{2,10},{4,12},{6,14},{8,0},{10,2},{12,4},{14,6},{16,24},{18,... | collective-permute-start | bytes 301064 | tf_op jit(solution)/shard_map/ppermute | solution.py:368
  6.6 8.4 %collective-permute-start.2 = (bf16[392,128]{1,0:T(8,128)(2,1)S(1)}, bf16[392,128]{1,0:T(8,128)(2,1)S(1)}, u32[]{:S(2)}, u32[]{:S(2)}) collective-permute-start(bf16[392,128]{1,0:T(8,128)(2,1)S(1)} %get-tuple-element.26), channel_id=1, source_target_pairs={{0,16},{2,18},{4,20},{6,22},{8,24},{10,26},{12,28},{14,30},{16,0},... | collective-permute-start | bytes 301064 | tf_op jit(solution)/shard_map/ppermute | solution.py:368
  7.3 10.0 %collective-permute-start.7 = (bf16[488,128]{1,0:T(8,128)(2,1)S(1)}, bf16[488,128]{1,0:T(8,128)(2,1)S(1)}, u32[]{:S(2)}, u32[]{:S(2)}) collective-permute-start(bf16[488,128]{1,0:T(8,128)(2,1)S(1)} %get-tuple-element.33), channel_id=1, source_target_pairs={{0,4},{2,6},{4,0},{6,2},{8,12},{10,14},{12,8},{14,10},{16,20},{18,... | collective-permute-start | bytes 374792 | tf_op jit(solution)/shard_map/ppermute | solution.py:368
  10.3 7.0 %collective-permute-start.8 = (bf16[488,128]{1,0:T(8,128)(2,1)S(1)}, bf16[488,128]{1,0:T(8,128)(2,1)S(1)}, u32[]{:S(2)}, u32[]{:S(2)}) collective-permute-start(bf16[488,128]{1,0:T(8,128)(2,1)S(1)} %get-tuple-element.34), channel_id=1, source_target_pairs={{0,6},{2,4},{4,2},{6,0},{8,14},{10,12},{12,10},{14,8},{16,22},{18,... | collective-permute-start | bytes 374792 | tf_op jit(solution)/shard_map/ppermute | solution.py:368
  15.0 5.4 %collective-permute-start.4 = (bf16[296,128]{1,0:T(8,128)(2,1)S(1)}, bf16[296,128]{1,0:T(8,128)(2,1)S(1)}, u32[]{:S(2)}, u32[]{:S(2)}) collective-permute-start(bf16[296,128]{1,0:T(8,128)(2,1)S(1)} %get-tuple-element.29), channel_id=1, source_target_pairs={{0,4},{2,6},{4,0},{6,2},{8,12},{10,14},{12,8},{14,10},{16,20},{18,... | collective-permute-start | bytes 227336 | tf_op jit(solution)/shard_map/ppermute | solution.py:368
  16.6 5.4 %collective-permute-start.5 = (bf16[296,128]{1,0:T(8,128)(2,1)S(1)}, bf16[296,128]{1,0:T(8,128)(2,1)S(1)}, u32[]{:S(2)}, u32[]{:S(2)}) collective-permute-start(bf16[296,128]{1,0:T(8,128)(2,1)S(1)} %get-tuple-element.30), channel_id=1, source_target_pairs={{0,6},{2,4},{4,2},{6,0},{8,14},{10,12},{12,10},{14,8},{16,22},{18,... | collective-permute-start | bytes 227336 | tf_op jit(solution)/shard_map/ppermute | solution.py:368
  16.6 5.4 %collective-permute-start.3 = (bf16[296,128]{1,0:T(8,128)(2,1)S(1)}, bf16[296,128]{1,0:T(8,128)(2,1)S(1)}, u32[]{:S(2)}, u32[]{:S(2)}) collective-permute-start(bf16[296,128]{1,0:T(8,128)(2,1)S(1)} %get-tuple-element.28.refs_4_), channel_id=1, source_target_pairs={{0,2},{2,0},{4,6},{6,4},{8,10},{10,8},{12,14},{14,12},{16,18},{18,... | collective-permute-start | bytes 227336 | tf_op jit(solution)/shard_map/ppermute | solution.py:368
  17.3 9.9 %collective-permute-start.10 = (bf16[384,128]{1,0:T(8,128)(2,1)S(1)}, bf16[384,128]{1,0:T(8,128)(2,1)S(1)}, u32[]{:S(2)}, u32[]{:S(2)}) collective-permute-start(bf16[384,128]{1,0:T(8,128)(2,1)S(1)} %get-tuple-element.40), channel_id=1, source_target_pairs={{0,16},{2,18},{4,20},{6,22},{8,24},{10,26},{12,28},{14,30},{16,0},... | collective-permute-start | bytes 294920 | tf_op jit(solution)/shard_map/ppermute | solution.py:368
  18.7 8.7 %collective-permute-start.11 = (bf16[384,128]{1,0:T(8,128)(2,1)S(1)}, bf16[384,128]{1,0:T(8,128)(2,1)S(1)}, u32[]{:S(2)}, u32[]{:S(2)}) collective-permute-start(bf16[384,128]{1,0:T(8,128)(2,1)S(1)} %get-tuple-element.41), channel_id=1, source_target_pairs={{0,8},{2,10},{4,12},{6,14},{8,0},{10,2},{12,4},{14,6},{16,24},{18,... | collective-permute-start | bytes 294920 | tf_op jit(solution)/shard_map/ppermute | solution.py:368
  20.4 7.0 %collective-permute-start.12 = (bf16[384,128]{1,0:T(8,128)(2,1)S(1)}, bf16[384,128]{1,0:T(8,128)(2,1)S(1)}, u32[]{:S(2)}, u32[]{:S(2)}) collective-permute-start(bf16[384,128]{1,0:T(8,128)(2,1)S(1)} %get-tuple-element.42), channel_id=1, source_target_pairs={{0,24},{2,26},{4,28},{6,30},{8,16},{10,18},{12,20},{14,22},{16,8},... | collective-permute-start | bytes 294920 | tf_op jit(solution)/shard_map/ppermute | solution.py:368
  22.4 5.0 %collective-permute-start.9 = (bf16[6,4,16,128]{3,2,1,0:T(8,128)(2,1)S(1)}, bf16[6,4,16,128]{3,2,1,0:T(8,128)(2,1)S(1)}, u32[]{:S(2)}, u32[]{:S(2)}) collective-permute-start(bf16[6,4,16,128]{3,2,1,0:T(8,128)(2,1)S(1)} %get-tuple-element.35), channel_id=1, source_target_pairs={{0,1},{1,0},{2,3},{3,2},{4,5},{5,4},{6,7},{7,6},{8,9},{9,8},{10,11... | collective-permute-start | bytes 294920 | tf_op jit(solution)/shard_map/ppermute | solution.py:443

commit v5 on v4

--- a/solution.py
+++ b/solution.py
@@ -93,7 +93,9 @@
     span = visits * block
     copies[0].wait()
     copies[1].wait()
-    slot = slots_of(jnp.bitwise_xor(dest_ref[...], lax.axis_index("patch")))
+    dest, me = dest_ref[...], lax.axis_index("patch")
+    across = (dest // NEAR - me // NEAR + far) % far
+    slot = slots_of(across * NEAR + jnp.bitwise_xor(dest % NEAR, me % NEAR))
     goal = spread(slot, depth, TILE_ROWS) * TILE_ROWS + iota((visits, depth), 1) % TILE_ROWS
     place = block_ref[...] % ACROSS * DOWN + block_ref[...] // ACROSS + 1
     lane = iota((TILE_ROWS, LANES), 1)
@@ -367,6 +369,9 @@
     def swap(value, step):
         return lax.ppermute(value, "patch", [(i, i ^ step) for i in range(patches)])
 
+    def shift(value, step):
+        return lax.ppermute(value, "patch", [(i, (i + step * NEAR) % patches) for i in range(patches)])
+
     span = visits * block
     fars = range(1, far)
     packed = pl.pallas_call(
@@ -385,8 +390,8 @@
         compiler_params=params(),
         name="pack",
     )(*map(in_hbm, (dest_patch, dest_block, flux, weight)))
-    first = sorted(fars, key=lambda x: (x != far - 1, x))
-    chunks = [swap(packed[x - 1], x * NEAR) for x in first]
+    first = list(fars)
+    chunks = [shift(packed[x - 1], x) for x in first]
     nears = [packed[far - 1]] + [swap(packed[far - 1 + y], y) for y in range(1, NEAR)]
 
     coefs = spatial.reshape(visits * 3, 1, BASIS)
@@ -421,8 +426,8 @@
     flux_sent = regroup(chunks, first, NEAR, span, True, [own_mix], "regroup_flux")
     others = [swap(flux_sent[y - 1], y) for y in range(1, NEAR)]
     weight_sent = regroup(nears, list(range(NEAR)), far, span, False, [flux_sent[0]], "regroup_weight")
-    order = sorted(fars, key=lambda x: (x != far // 2, x != 1, -x))
-    weights = [swap(weight_sent[x - 1], x * NEAR) for x in order]
+    order = sorted(fars, key=lambda x: (x != far // 2, x))
+    weights = [shift(weight_sent[x - 1], x) for x in order]
 
     edge_shape = shape((visits, ACROSS, HALO, LANES), BF16)
     edge_count = 1 if bands == 2 else 2

time: 29.6 us -> 29.3 us (0.990)
  waiting for transfers between devices: 5.98 us -> 3.61 us
  starting transfers between devices: 15.9 us -> 17.9 us
    ppermute x0 -> x6, starting transfers between devices: none -> 12.6 us  [shift(): lax.ppermute(value, 'patch', [(i, (i + step * NEAR) % patches) for i in r...]
    ppermute x12 -> x6, starting transfers between devices: 14.3 us -> 3.73 us  [swap(): return lax.ppermute(value, 'patch', [(i, i ^ step) for i in range(patches)])]
    ppermute x12 -> x6, waiting for transfers between devices: 5.98 us -> 0.02 us  [swap(): return lax.ppermute(value, 'patch', [(i, i ^ step) for i in range(patches)])]
    ppermute x0 -> x6, waiting for transfers between devices: none -> 3.4 us  [shift(): lax.ppermute(value, 'patch', [(i, (i + step * NEAR) % patches) for i in r...]
  transfers between devices with their start and end apart: 13 -> 13, of which waited for: 5 -> 4; matrix products, arithmetic and copies ran while one was open for 0% -> 0% of each run, Pallas kernels for 14% -> 14%
where the time goes in v5:
time: 29.3 us; the launch traced here: 29 us
  starting transfers between devices  17.9 us (61%)
  Pallas kernels  7.44 us (25%)
  waiting for transfers between devices  3.61 us (12%)
    ppermute x6, starting transfers between devices, shift(): lax.ppermute(value, 'patch', [(i, (i + step * NEAR) % patches) for i in r...  12.6 us
    pallas_call x2, Pallas kernels, filter_rows(): pl.pallas_call(functools.partial(filter_kernel, order), out_shape=shape((...  4.01 us
    ppermute x6, starting transfers between devices, swap(): return lax.ppermute(value, 'patch', [(i, i ^ step) for i in range(patches)])  3.73 us
    ppermute x6, waiting for transfers between devices, shift(): lax.ppermute(value, 'patch', [(i, (i + step * NEAR) % patches) for i in r...  3.4 us
    ppermute x1, starting transfers between devices, per_device(): halos = [lax.ppermute(edges[0], 'band', [(0, 1), (1, 0)])]  1.56 us
    pallas_call x1, Pallas kernels, tables(): pl.pallas_call(functools.partial(table_kernel, bands), out_shape=(shape((...  1.51 us
    pallas_call x1, Pallas kernels, per_device(): pl.pallas_call(functools.partial(pack_kernel, far), out_shape=(shape((NEA...  1.44 us
  transfers between devices with their start and end apart: 13, of which 4 were waited for; matrix products, arithmetic and copies ran while one was open for 0% of the time, Pallas kernels for 14%

profile of v5, /device:TPU:0, one launch (start us, length us, event | category | flops | bytes accessed | tf_op | source)
XLA Modules:
  0.0 29.0 jit_solution(15629861508752576996)
XLA Ops:
  0.0 1.4 %pack.1 = (bf16[392,128]{1,0:T(8,128)(2,1)S(1)}, bf16[392,128]{1,0:T(8,128)(2,1)S(1)}, bf16[392,128]{1,0:T(8,128)(2,1)S(1)}, bf16[488,128]{1,0:T(8,128)(2,1)S(1)...) custom-call(s32[6,16]{1,0:T(8,128)} %dest_hbm.1, s32[6,16]{1,0:T(8,128)} %block_hbm.1, ...), custom_call_target="tpu_custom_call" | custom-call | tf_op jit(solution)/shard_map/pack/pallas_call | solution.py:377
  1.5 3.1 %collective-permute-start = (bf16[392,128]{1,0:T(8,128)(2,1)S(1)}, bf16[392,128]{1,0:T(8,128)(2,1)S(1)}, u32[]{:S(2)}, u32[]{:S(2)}) collective-permute-start(bf16[392,128]{1,0:T(8,128)(2,1)S(1)} %get-tuple-element.24), channel_id=1, source_target_pairs={{0,8},{2,10},{4,12},{6,14},{8,16},{10,18},{12,20},{14,22},{16,24},... | collective-permute-start | bytes 301064 | tf_op jit(solution)/shard_map/ppermute | solution.py:373
  4.5 0.0 collective-permute-start.6
  4.5 2.6 %collective-permute-start.1 = (bf16[392,128]{1,0:T(8,128)(2,1)S(1)}, bf16[392,128]{1,0:T(8,128)(2,1)S(1)}, u32[]{:S(2)}, u32[]{:S(2)}) collective-permute-start(bf16[392,128]{1,0:T(8,128)(2,1)S(1)} %get-tuple-element.25), channel_id=1, source_target_pairs={{0,16},{2,18},{4,20},{6,22},{8,24},{10,26},{12,28},{14,30},{16,0},... | collective-permute-start | bytes 301064 | tf_op jit(solution)/shard_map/ppermute | solution.py:373
  7.1 1.3 %collective-permute-start.2 = (bf16[392,128]{1,0:T(8,128)(2,1)S(1)}, bf16[392,128]{1,0:T(8,128)(2,1)S(1)}, u32[]{:S(2)}, u32[]{:S(2)}) collective-permute-start(bf16[392,128]{1,0:T(8,128)(2,1)S(1)} %get-tuple-element.26), channel_id=1, source_target_pairs={{0,24},{2,26},{4,28},{6,30},{8,0},{10,2},{12,4},{14,6},{16,8},{18,... | collective-permute-start | bytes 301064 | tf_op jit(solution)/shard_map/ppermute | solution.py:373
  8.5 1.5 %collective-permute-start.7 = (bf16[488,128]{1,0:T(8,128)(2,1)S(1)}, bf16[488,128]{1,0:T(8,128)(2,1)S(1)}, u32[]{:S(2)}, u32[]{:S(2)}) collective-permute-start(bf16[488,128]{1,0:T(8,128)(2,1)S(1)} %get-tuple-element.33), channel_id=1, source_target_pairs={{0,4},{2,6},{4,0},{6,2},{8,12},{10,14},{12,8},{14,10},{16,20},{18,... | collective-permute-start | bytes 374792 | tf_op jit(solution)/shard_map/ppermute | solution.py:370
  10.0 0.0 collective-permute-done.refs_0_
  10.0 0.0 collective-permute-start.8
  10.0 1.5 %tables.1 = (bf16[256,2816]{1,0:T(8,128)(2,1)S(1)}, bf16[6,64,768]{2,1,0:T(8,128)(2,1)S(1)}, bf16[6,64,384]{2,1,0:T(8,128)(2,1)S(1)}) custom-call(s32[1]{0:T(128)} %bitcast.2.up_ref, bf16[21,2,31]{2,1,0:T(2,128)(2,1)} %bitcast.7, f32[18,1,21]{2,1,0:T(1,128)} %bitcast.8), custom_call_target="tpu_custom_call" | custom-call | flops 1000000000 | bytes 4194304 | tf_op jit(solution)/shard_map/tables/pallas_call | solution.py:401
  11.5 2.3 %collective-permute-done.1.refs_1_ = bf16[392,128]{1,0:T(8,128)(2,1)S(1)} collective-permute-done((bf16[392,128]{1,0:T(8,128)(2,1)S(1)}, bf16[392,128]{1,0:T(8,128)(2,1)S(1)}, u32[]{:S(2)}, u32[]{:S(2)}) %collective-permute-start.1) | collective-permute-done | bytes 100384 | tf_op jit(solution)/shard_map/ppermute | solution.py:373
  13.8 0.3 %collective-permute-done.2.refs_2_ = bf16[392,128]{1,0:T(8,128)(2,1)S(1)} collective-permute-done((bf16[392,128]{1,0:T(8,128)(2,1)S(1)}, bf16[392,128]{1,0:T(8,128)(2,1)S(1)}, u32[]{:S(2)}, u32[]{:S(2)}) %collective-permute-start.2) | collective-permute-done | bytes 100384 | tf_op jit(solution)/shard_map/ppermute | solution.py:373
  14.1 1.6 %collective-permute-start.4 = (bf16[296,128]{1,0:T(8,128)(2,1)S(1)}, bf16[296,128]{1,0:T(8,128)(2,1)S(1)}, u32[]{:S(2)}, u32[]{:S(2)}) collective-permute-start(bf16[296,128]{1,0:T(8,128)(2,1)S(1)} %get-tuple-element.29), channel_id=1, source_target_pairs={{0,4},{2,6},{4,0},{6,2},{8,12},{10,14},{12,8},{14,10},{16,20},{18,... | collective-permute-start | bytes 227336 | tf_op jit(solution)/shard_map/ppermute | solution.py:370
  15.7 0.0 collective-permute-start.5
  15.7 0.0 collective-permute-done.6.refs_7_.refs_1_.refs_3_
  15.7 0.6 %collective-permute-start.3 = (bf16[296,128]{1,0:T(8,128)(2,1)S(1)}, bf16[296,128]{1,0:T(8,128)(2,1)S(1)}, u32[]{:S(2)}, u32[]{:S(2)}) collective-permute-start(bf16[296,128]{1,0:T(8,128)(2,1)S(1)} %get-tuple-element.28.refs_4_), channel_id=1, source_target_pairs={{0,2},{2,0},{4,6},{6,4},{8,10},{10,8},{12,14},{14,12},{16,18},{18,... | collective-permute-start | bytes 227336 | tf_op jit(solution)/shard_map/ppermute | solution.py:370
  16.3 0.0 collective-permute-done.7.refs_8_.refs_2_.refs_4_
  16.3 0.0 collective-permute-done.8.refs_9_.refs_3_.refs_5_
  16.4 1.4 %collective-permute-start.10 = (bf16[384,128]{1,0:T(8,128)(2,1)S(1)}, bf16[384,128]{1,0:T(8,128)(2,1)S(1)}, u32[]{:S(2)}, u32[]{:S(2)}) collective-permute-start(bf16[384,128]{1,0:T(8,128)(2,1)S(1)} %get-tuple-element.40), channel_id=1, source_target_pairs={{0,16},{2,18},{4,20},{6,22},{8,24},{10,26},{12,28},{14,30},{16,0},... | collective-permute-start | bytes 294920 | tf_op jit(solution)/shard_map/ppermute | solution.py:373
  17.8 2.6 %collective-permute-start.11 = (bf16[384,128]{1,0:T(8,128)(2,1)S(1)}, bf16[384,128]{1,0:T(8,128)(2,1)S(1)}, u32[]{:S(2)}, u32[]{:S(2)}) collective-permute-start(bf16[384,128]{1,0:T(8,128)(2,1)S(1)} %get-tuple-element.41), channel_id=1, source_target_pairs={{0,8},{2,10},{4,12},{6,14},{8,16},{10,18},{12,20},{14,22},{16,24},... | collective-permute-start | bytes 294920 | tf_op jit(solution)/shard_map/ppermute | solution.py:373
  20.4 0.0 collective-permute-done.4.refs_4_
  20.4 1.6 %collective-permute-start.12 = (bf16[384,128]{1,0:T(8,128)(2,1)S(1)}, bf16[384,128]{1,0:T(8,128)(2,1)S(1)}, u32[]{:S(2)}, u32[]{:S(2)}) collective-permute-start(bf16[384,128]{1,0:T(8,128)(2,1)S(1)} %get-tuple-element.42), channel_id=1, source_target_pairs={{0,24},{2,26},{4,28},{6,30},{8,0},{10,2},{12,4},{14,6},{16,8},{18,... | collective-permute-start | bytes 294920 | tf_op jit(solution)/shard_map/ppermute | solution.py:373
  22.0 0.0 collective-permute-done.5.refs_5_
  22.0 0.0 collective-permute-done.3.refs_3_
  22.0 0.4 %place_flux.1 = (bf16[6,4,32,128]{3,2,1,0:T(8,128)(2,1)S(1)}, bf16[6,128,256]{2,1,0:T(8,128)(2,1)S(1)}, bf16[6,4,16,128]{3,2,1,0:T(8,128)(2,1)S(1)}) custom-call(bf16[392,128]{1,0:T(8,128)(2,1)S(1)} %collective-permute-done.refs_0_, bf16[392,128]{1,0:T(8,128)(2,1)S(1)} %collective-permute-done.1.refs_1_, ...), custom_call_target="tpu_custom_call" | custom-call | tf_op jit(solution)/shard_map/place_flux/pallas_call | solution.py:434
  22.4 1.6 %collective-permute-start.9 = (bf16[6,4,16,128]{3,2,1,0:T(8,128)(2,1)S(1)}, bf16[6,4,16,128]{3,2,1,0:T(8,128)(2,1)S(1)}, u32[]{:S(2)}, u32[]{:S(2)}) collective-permute-start(bf16[6,4,16,128]{3,2,1,0:T(8,128)(2,1)S(1)} %get-tuple-element.35), channel_id=1, source_target_pairs={{0,1},{1,0},{2,3},{3,2},{4,5},{5,4},{6,7},{7,6},{8,9},{9,8},{10,11... | collective-permute-start | bytes 294920 | tf_op jit(solution)/shard_map/ppermute | solution.py:448
  24.0 2.1 %filter_own.1.refs_0_ = f32[6,32,512]{2,1,0:T(8,128)S(1)} custom-call(bf16[6,4,32,128]{3,2,1,0:T(8,128)(2,1)S(1)} %get-tuple-element.38.frame_ref, bf16[256,2816]{1,0:T(8,128)(2,1)S(1)} %get-tuple-element.36.table_ref, bf16[6,64,768]{2,1,0:T(8,128)(2,1)S(1)} %get-tuple-element.27.refs_3_.mix_ref), custom_call_target="tpu_custom_call" | custom-call | flops 2113929216 | bytes 4194304 | tf_op jit(solution)/shard_map/filter_own/pallas_call | solution.py:332
  26.1 0.0 collective-permute-done.10.refs_6_
  26.1 0.8 %collective-permute-done.11.refs_7_ = bf16[384,128]{1,0:T(8,128)(2,1)S(1)} collective-permute-done((bf16[384,128]{1,0:T(8,128)(2,1)S(1)}, bf16[384,128]{1,0:T(8,128)(2,1)S(1)}, u32[]{:S(2)}, u32[]{:S(2)}) %collective-permute-start.11) | collective-permute-done | bytes 98336 | tf_op jit(solution)/shard_map/ppermute | solution.py:373
  26.9 0.0 collective-permute-done.12.refs_8_
  26.9 0.2 collective-permute-done.9.frame_ref
  27.1 1.9 %filter_halo_weigh.1 = f32[1,32,512]{2,1,0:T(8,128)} custom-call(bf16[6,4,16,128]{3,2,1,0:T(8,128)(2,1)S(1)} %collective-permute-done.9.frame_ref, bf16[256,2816]{1,0:T(8,128)(2,1)S(1)} %get-tuple-element.36.table_ref, bf16[6,64,384]{2,1,0:T(8,128)(2,1)S(1)} %get-tuple-element.37.mix_ref, f32[6,32,512]{2,1,0:T(8,128)S(1)} %filter_own.1.refs_0_, ...), custom_call_target="tpu_custom_call" | custom-call | flops 1056964608 | bytes 4194304 | tf_op jit(solution)/shard_map/filter_halo_weigh/pallas_call | solution.py:332
  (2 shorter events, 0.0 us)
Async XLA Ops:
  1.5 8.5 %collective-permute-start = (bf16[392,128]{1,0:T(8,128)(2,1)S(1)}, bf16[392,128]{1,0:T(8,128)(2,1)S(1)}, u32[]{:S(2)}, u32[]{:S(2)}) collective-permute-start(bf16[392,128]{1,0:T(8,128)(2,1)S(1)} %get-tuple-element.24), channel_id=1, source_target_pairs={{0,8},{2,10},{4,12},{6,14},{8,16},{10,18},{12,20},{14,22},{16,24},... | collective-permute-start | bytes 301064 | tf_op jit(solution)/shard_map/ppermute | solution.py:373
  4.5 11.2 %collective-permute-start.6 = (bf16[488,128]{1,0:T(8,128)(2,1)S(1)}, bf16[488,128]{1,0:T(8,128)(2,1)S(1)}, u32[]{:S(2)}, u32[]{:S(2)}) collective-permute-start(bf16[488,128]{1,0:T(8,128)(2,1)S(1)} %get-tuple-element.32), channel_id=1, source_target_pairs={{0,2},{2,0},{4,6},{6,4},{8,10},{10,8},{12,14},{14,12},{16,18},{18,... | collective-permute-start | bytes 374792 | tf_op jit(solution)/shard_map/ppermute | solution.py:370
  4.5 9.3 %collective-permute-start.1 = (bf16[392,128]{1,0:T(8,128)(2,1)S(1)}, bf16[392,128]{1,0:T(8,128)(2,1)S(1)}, u32[]{:S(2)}, u32[]{:S(2)}) collective-permute-start(bf16[392,128]{1,0:T(8,128)(2,1)S(1)} %get-tuple-element.25), channel_id=1, source_target_pairs={{0,16},{2,18},{4,20},{6,22},{8,24},{10,26},{12,28},{14,30},{16,0},... | collective-permute-start | bytes 301064 | tf_op jit(solution)/shard_map/ppermute | solution.py:373
  7.1 7.0 %collective-permute-start.2 = (bf16[392,128]{1,0:T(8,128)(2,1)S(1)}, bf16[392,128]{1,0:T(8,128)(2,1)S(1)}, u32[]{:S(2)}, u32[]{:S(2)}) collective-permute-start(bf16[392,128]{1,0:T(8,128)(2,1)S(1)} %get-tuple-element.26), channel_id=1, source_target_pairs={{0,24},{2,26},{4,28},{6,30},{8,0},{10,2},{12,4},{14,6},{16,8},{18,... | collective-permute-start | bytes 301064 | tf_op jit(solution)/shard_map/ppermute | solution.py:373
  8.5 7.9 %collective-permute-start.7 = (bf16[488,128]{1,0:T(8,128)(2,1)S(1)}, bf16[488,128]{1,0:T(8,128)(2,1)S(1)}, u32[]{:S(2)}, u32[]{:S(2)}) collective-permute-start(bf16[488,128]{1,0:T(8,128)(2,1)S(1)} %get-tuple-element.33), channel_id=1, source_target_pairs={{0,4},{2,6},{4,0},{6,2},{8,12},{10,14},{12,8},{14,10},{16,20},{18,... | collective-permute-start | bytes 374792 | tf_op jit(solution)/shard_map/ppermute | solution.py:370
  10.0 6.3 %collective-permute-start.8 = (bf16[488,128]{1,0:T(8,128)(2,1)S(1)}, bf16[488,128]{1,0:T(8,128)(2,1)S(1)}, u32[]{:S(2)}, u32[]{:S(2)}) collective-permute-start(bf16[488,128]{1,0:T(8,128)(2,1)S(1)} %get-tuple-element.34), channel_id=1, source_target_pairs={{0,6},{2,4},{4,2},{6,0},{8,14},{10,12},{12,10},{14,8},{16,22},{18,... | collective-permute-start | bytes 374792 | tf_op jit(solution)/shard_map/ppermute | solution.py:370
  14.1 6.3 %collective-permute-start.4 = (bf16[296,128]{1,0:T(8,128)(2,1)S(1)}, bf16[296,128]{1,0:T(8,128)(2,1)S(1)}, u32[]{:S(2)}, u32[]{:S(2)}) collective-permute-start(bf16[296,128]{1,0:T(8,128)(2,1)S(1)} %get-tuple-element.29), channel_id=1, source_target_pairs={{0,4},{2,6},{4,0},{6,2},{8,12},{10,14},{12,8},{14,10},{16,20},{18,... | collective-permute-start | bytes 227336 | tf_op jit(solution)/shard_map/ppermute | solution.py:370
  15.7 6.3 %collective-permute-start.5 = (bf16[296,128]{1,0:T(8,128)(2,1)S(1)}, bf16[296,128]{1,0:T(8,128)(2,1)S(1)}, u32[]{:S(2)}, u32[]{:S(2)}) collective-permute-start(bf16[296,128]{1,0:T(8,128)(2,1)S(1)} %get-tuple-element.30), channel_id=1, source_target_pairs={{0,6},{2,4},{4,2},{6,0},{8,14},{10,12},{12,10},{14,8},{16,22},{18,... | collective-permute-start | bytes 227336 | tf_op jit(solution)/shard_map/ppermute | solution.py:370
  15.7 6.3 %collective-permute-start.3 = (bf16[296,128]{1,0:T(8,128)(2,1)S(1)}, bf16[296,128]{1,0:T(8,128)(2,1)S(1)}, u32[]{:S(2)}, u32[]{:S(2)}) collective-permute-start(bf16[296,128]{1,0:T(8,128)(2,1)S(1)} %get-tuple-element.28.refs_4_), channel_id=1, source_target_pairs={{0,2},{2,0},{4,6},{6,4},{8,10},{10,8},{12,14},{14,12},{16,18},{18,... | collective-permute-start | bytes 227336 | tf_op jit(solution)/shard_map/ppermute | solution.py:370
  16.4 9.7 %collective-permute-start.10 = (bf16[384,128]{1,0:T(8,128)(2,1)S(1)}, bf16[384,128]{1,0:T(8,128)(2,1)S(1)}, u32[]{:S(2)}, u32[]{:S(2)}) collective-permute-start(bf16[384,128]{1,0:T(8,128)(2,1)S(1)} %get-tuple-element.40), channel_id=1, source_target_pairs={{0,16},{2,18},{4,20},{6,22},{8,24},{10,26},{12,28},{14,30},{16,0},... | collective-permute-start | bytes 294920 | tf_op jit(solution)/shard_map/ppermute | solution.py:373
  17.8 9.1 %collective-permute-start.11 = (bf16[384,128]{1,0:T(8,128)(2,1)S(1)}, bf16[384,128]{1,0:T(8,128)(2,1)S(1)}, u32[]{:S(2)}, u32[]{:S(2)}) collective-permute-start(bf16[384,128]{1,0:T(8,128)(2,1)S(1)} %get-tuple-element.41), channel_id=1, source_target_pairs={{0,8},{2,10},{4,12},{6,14},{8,16},{10,18},{12,20},{14,22},{16,24},... | collective-permute-start | bytes 294920 | tf_op jit(solution)/shard_map/ppermute | solution.py:373
  20.4 6.5 %collective-permute-start.12 = (bf16[384,128]{1,0:T(8,128)(2,1)S(1)}, bf16[384,128]{1,0:T(8,128)(2,1)S(1)}, u32[]{:S(2)}, u32[]{:S(2)}) collective-permute-start(bf16[384,128]{1,0:T(8,128)(2,1)S(1)} %get-tuple-element.42), channel_id=1, source_target_pairs={{0,24},{2,26},{4,28},{6,30},{8,0},{10,2},{12,4},{14,6},{16,8},{18,... | collective-permute-start | bytes 294920 | tf_op jit(solution)/shard_map/ppermute | solution.py:373
  22.4 4.7 %collective-permute-start.9 = (bf16[6,4,16,128]{3,2,1,0:T(8,128)(2,1)S(1)}, bf16[6,4,16,128]{3,2,1,0:T(8,128)(2,1)S(1)}, u32[]{:S(2)}, u32[]{:S(2)}) collective-permute-start(bf16[6,4,16,128]{3,2,1,0:T(8,128)(2,1)S(1)} %get-tuple-element.35), channel_id=1, source_target_pairs={{0,1},{1,0},{2,3},{3,2},{4,5},{5,4},{6,7},{7,6},{8,9},{9,8},{10,11... | collective-permute-start | bytes 294920 | tf_op jit(solution)/shard_map/ppermute | solution.py:448

commit v6 on v5

--- a/solution.py
+++ b/solution.py
@@ -156,10 +156,9 @@
     return place * TILE_ROWS + iota((TILE_ROWS, width), 1) % TILE_ROWS
 
 
-def place_kernel(far, order, swap, *refs):
+def arrived(far, order, refs, visits):
     chunks, others = sorted_refs(order, refs[: far - 1]), refs[far - 1 : far + NEAR - 2]
-    nears, (frame_ref, hot_ref, *edges) = refs[far + NEAR - 2 : far + 2 * NEAR - 2], refs[far + 2 * NEAR - 2 :]
-    visits = frame_ref.shape[0]
+    nears = refs[far + NEAR - 2 : far + 2 * NEAR - 2]
     block = CAP * TILE_ROWS
     span = visits * block
     path = iota((TILE_ROWS, LANES), 1) // (CAP * far)
@@ -168,10 +167,8 @@
         tails = [nears[y]] + (list(chunks) if y == 0 else [others[y - 1]])
         tail = sum(ref[ref.shape[0] - TILE_ROWS :, :].astype(F32) for ref in tails)
         note = jnp.where(path == y, tail, note)
-    goal = placing(note, far * NEAR)
-    for k in range(visits):
-        hot = jnp.where(iota((ACROSS * ROWS, goal.shape[1]), 0) == goal[k : k + 1], 1.0, 0.0).astype(BF16)
-        hot_ref[k] = hot
+
+    def rows(k):
         received = []
         for y in range(NEAR):
             received.append(nears[y][part_of(far, span, k, block), :])
@@ -180,15 +177,39 @@
                     received.append(others[y - 1][part_of(x - 1, span, k, block), :])
                 else:
                     received.append(chunks[x - 1][part_of(0, span, k, block), :])
-        frame = jnp.dot(hot, jnp.concatenate(received, axis=0), preferred_element_type=F32).astype(BF16)
-        frame = frame.reshape(ACROSS, ROWS, LANES)
-        frame_ref[k] = frame
-        top, bottom = frame[:, :HALO], frame[:, ROWS - HALO :]
-        if swap:
-            edges[0][k] = jnp.where(lax.axis_index("band") == 0, bottom, top)
-        else:
-            edges[0][k] = top
-            edges[1][k] = bottom
+        return jnp.concatenate(received, axis=0)
+
+    return placing(note, far * NEAR), rows
+
+
+def hot_of(row, goal):
+    return jnp.where(row == goal, 1.0, 0.0).astype(BF16)
+
+
+def edge_kernel(far, order, count, *refs):
+    edges = refs[far + 2 * NEAR - 2 :]
+    goal, rows = arrived(far, order, refs, edges[0].shape[0])
+    line = iota((ACROSS * HALO, goal.shape[1]), 0)
+    line = line // HALO * ROWS + line % HALO
+    low = ROWS - HALO
+    starts = [jnp.where(lax.axis_index("band") == 0, low, 0)] if count == 1 else [0, low]
+    for k in range(edges[0].shape[0]):
+        received = rows(k)
+        for edge, start in zip(edges, starts):
+            hot = hot_of(line + start, goal[k : k + 1])
+            part = jnp.dot(hot, received, preferred_element_type=F32).astype(BF16)
+            edge[k] = part.reshape(ACROSS, HALO, LANES)
+
+
+def place_kernel(far, order, *refs):
+    frame_ref, hot_ref = refs[-2:]
+    goal, rows = arrived(far, order, refs, frame_ref.shape[0])
+    row = iota((ACROSS * ROWS, goal.shape[1]), 0)
+    for k in range(frame_ref.shape[0]):
+        hot = hot_of(row, goal[k : k + 1])
+        hot_ref[k] = hot
+        frame = jnp.dot(hot, rows(k), preferred_element_type=F32).astype(BF16)
+        frame_ref[k] = frame.reshape(ACROSS, ROWS, LANES)
 
 
 def hot_rows(taps, shift_lane, width, used=None):
@@ -425,24 +446,32 @@
     table, own_mix, _ = built[0]
     flux_sent = regroup(chunks, first, NEAR, span, True, [own_mix], "regroup_flux")
     others = [swap(flux_sent[y - 1], y) for y in range(1, NEAR)]
-    weight_sent = regroup(nears, list(range(NEAR)), far, span, False, [flux_sent[0]], "regroup_weight")
+    weight_sent = regroup(nears, list(range(NEAR)), far, span, False, [], "regroup_weight")
     order = sorted(fars, key=lambda x: (x != far // 2, x))
     weights = [shift(weight_sent[x - 1], x) for x in order]
 
     edge_shape = shape((visits, ACROSS, HALO, LANES), BF16)
     edge_count = 1 if bands == 2 else 2
-    frame, hot, *edges = pl.pallas_call(
-        functools.partial(place_kernel, far, first, bands == 2),
+    received = (*chunks, *others, *nears)
+    edges = pl.pallas_call(
+        functools.partial(edge_kernel, far, first, edge_count),
+        out_shape=(edge_shape,) * edge_count,
+        in_specs=[vmem()] * len(received),
+        out_specs=(vmem(),) * edge_count,
+        compiler_params=params(),
+        name="edges",
+    )(*received)
+    frame, hot = pl.pallas_call(
+        functools.partial(place_kernel, far, first),
         out_shape=(
             shape((visits, ACROSS, ROWS, LANES), BF16),
             shape((visits, ACROSS * ROWS, patches * block), BF16),
-        )
-        + (edge_shape,) * edge_count,
-        in_specs=[vmem()] * (far + 2 * NEAR - 2),
-        out_specs=(vmem(),) * (2 + edge_count),
+        ),
+        in_specs=[vmem()] * len(received) + [pl.BlockSpec(memory_space=pl.ANY)],
+        out_specs=(vmem(),) * 2,
         compiler_params=params(),
         name="place_flux",
-    )(*chunks, *others, *nears)
+    )(*received, edges[0])
 
     if bands == 2:
         halos = [lax.ppermute(edges[0], "band", [(0, 1), (1, 0)])]

time: 29.3 us -> 29.2 us (level)
  starting transfers between devices: 17.9 us -> 17.3 us
  Pallas kernels: 7.44 us -> 7.82 us
    ppermute x6, starting transfers between devices: 12.6 us -> 12.3 us  [shift(): lax.ppermute(value, 'patch', [(i, (i + step * NEAR) % patches) for i in r...]
    ppermute x6, waiting for transfers between devices: 3.4 us -> 3.74 us  [shift(): lax.ppermute(value, 'patch', [(i, (i + step * NEAR) % patches) for i in r...]
    pallas_call x1 -> x2, Pallas kernels: 0.43 us -> 0.77 us  [the longest x1 0.43 us: per_device(): pl.pallas_call(functools.partial(place_kernel, far, first), out_shape=(sh...]
  transfers between devices with their start and end apart: 13 -> 13, of which waited for: 4 -> 5; matrix products, arithmetic and copies ran while one was open for 0% -> 0% of each run, Pallas kernels for 14% -> 15%
where the time goes in v6:
time: 29.2 us; the launch traced here: 28.9 us
  starting transfers between devices  17.3 us (59%)
  Pallas kernels  7.82 us (27%)
  waiting for transfers between devices  3.76 us (13%)
    ppermute x6, starting transfers between devices, shift(): lax.ppermute(value, 'patch', [(i, (i + step * NEAR) % patches) for i in r...  12.3 us
    pallas_call x2, Pallas kernels, filter_rows(): pl.pallas_call(functools.partial(filter_kernel, order), out_shape=shape((...  4.06 us
    ppermute x6, waiting for transfers between devices, shift(): lax.ppermute(value, 'patch', [(i, (i + step * NEAR) % patches) for i in r...  3.74 us
    ppermute x6, starting transfers between devices, swap(): return lax.ppermute(value, 'patch', [(i, i ^ step) for i in range(patches)])  3.46 us
    ppermute x1, starting transfers between devices, per_device(): halos = [lax.ppermute(edges[0], 'band', [(0, 1), (1, 0)])]  1.56 us
    pallas_call x1, Pallas kernels, tables(): pl.pallas_call(functools.partial(table_kernel, bands), out_shape=(shape((...  1.51 us
    pallas_call x1, Pallas kernels, per_device(): pl.pallas_call(functools.partial(pack_kernel, far), out_shape=(shape((NEA...  1.44 us
  transfers between devices with their start and end apart: 13, of which 5 were waited for; matrix products, arithmetic and copies ran while one was open for 0% of the time, Pallas kernels for 15%

profile of v6, /device:TPU:0, one launch (start us, length us, event | category | flops | bytes accessed | tf_op | source)
XLA Modules:
  0.0 28.9 jit_solution(14181737338591605582)
XLA Ops:
  0.0 1.4 %pack.1 = (bf16[392,128]{1,0:T(8,128)(2,1)S(1)}, bf16[392,128]{1,0:T(8,128)(2,1)S(1)}, bf16[392,128]{1,0:T(8,128)(2,1)S(1)}, bf16[488,128]{1,0:T(8,128)(2,1)S(1)...) custom-call(s32[6,16]{1,0:T(8,128)} %dest_hbm.1, s32[6,16]{1,0:T(8,128)} %block_hbm.1, ...), custom_call_target="tpu_custom_call" | custom-call | tf_op jit(solution)/shard_map/pack/pallas_call | solution.py:398
  1.5 3.1 %collective-permute-start = (bf16[392,128]{1,0:T(8,128)(2,1)S(1)}, bf16[392,128]{1,0:T(8,128)(2,1)S(1)}, u32[]{:S(2)}, u32[]{:S(2)}) collective-permute-start(bf16[392,128]{1,0:T(8,128)(2,1)S(1)} %get-tuple-element.23), channel_id=1, source_target_pairs={{0,8},{2,10},{4,12},{6,14},{8,16},{10,18},{12,20},{14,22},{16,24},... | collective-permute-start | bytes 301064 | tf_op jit(solution)/shard_map/ppermute | solution.py:394
  4.5 0.0 collective-permute-start.6
  4.5 2.6 %collective-permute-start.1 = (bf16[392,128]{1,0:T(8,128)(2,1)S(1)}, bf16[392,128]{1,0:T(8,128)(2,1)S(1)}, u32[]{:S(2)}, u32[]{:S(2)}) collective-permute-start(bf16[392,128]{1,0:T(8,128)(2,1)S(1)} %get-tuple-element.24), channel_id=1, source_target_pairs={{0,16},{2,18},{4,20},{6,22},{8,24},{10,26},{12,28},{14,30},{16,0},... | collective-permute-start | bytes 301064 | tf_op jit(solution)/shard_map/ppermute | solution.py:394
  7.1 1.3 %collective-permute-start.2 = (bf16[392,128]{1,0:T(8,128)(2,1)S(1)}, bf16[392,128]{1,0:T(8,128)(2,1)S(1)}, u32[]{:S(2)}, u32[]{:S(2)}) collective-permute-start(bf16[392,128]{1,0:T(8,128)(2,1)S(1)} %get-tuple-element.25), channel_id=1, source_target_pairs={{0,24},{2,26},{4,28},{6,30},{8,0},{10,2},{12,4},{14,6},{16,8},{18,... | collective-permute-start | bytes 301064 | tf_op jit(solution)/shard_map/ppermute | solution.py:394
  8.5 1.5 %collective-permute-start.7 = (bf16[488,128]{1,0:T(8,128)(2,1)S(1)}, bf16[488,128]{1,0:T(8,128)(2,1)S(1)}, u32[]{:S(2)}, u32[]{:S(2)}) collective-permute-start(bf16[488,128]{1,0:T(8,128)(2,1)S(1)} %get-tuple-element.32), channel_id=1, source_target_pairs={{0,4},{2,6},{4,0},{6,2},{8,12},{10,14},{12,8},{14,10},{16,20},{18,... | collective-permute-start | bytes 374792 | tf_op jit(solution)/shard_map/ppermute | solution.py:391
  10.0 0.0 collective-permute-done.refs_0_
  10.0 0.0 collective-permute-start.8
  10.0 1.5 %tables.1 = (bf16[256,2816]{1,0:T(8,128)(2,1)S(1)}, bf16[6,64,768]{2,1,0:T(8,128)(2,1)S(1)}, bf16[6,64,384]{2,1,0:T(8,128)(2,1)S(1)}) custom-call(s32[1]{0:T(128)} %bitcast.2.up_ref, bf16[21,2,31]{2,1,0:T(2,128)(2,1)} %bitcast.7, f32[18,1,21]{2,1,0:T(1,128)} %bitcast.8), custom_call_target="tpu_custom_call" | custom-call | flops 1000000000 | bytes 4194304 | tf_op jit(solution)/shard_map/tables/pallas_call | solution.py:422
  11.5 2.3 %collective-permute-done.1.refs_1_ = bf16[392,128]{1,0:T(8,128)(2,1)S(1)} collective-permute-done((bf16[392,128]{1,0:T(8,128)(2,1)S(1)}, bf16[392,128]{1,0:T(8,128)(2,1)S(1)}, u32[]{:S(2)}, u32[]{:S(2)}) %collective-permute-start.1) | collective-permute-done | bytes 100384 | tf_op jit(solution)/shard_map/ppermute | solution.py:394
  13.8 0.3 %collective-permute-done.2.refs_2_ = bf16[392,128]{1,0:T(8,128)(2,1)S(1)} collective-permute-done((bf16[392,128]{1,0:T(8,128)(2,1)S(1)}, bf16[392,128]{1,0:T(8,128)(2,1)S(1)}, u32[]{:S(2)}, u32[]{:S(2)}) %collective-permute-start.2) | collective-permute-done | bytes 100384 | tf_op jit(solution)/shard_map/ppermute | solution.py:394
  14.1 0.1 collective-permute-start.3
  14.2 1.6 %collective-permute-start.4 = (bf16[296,128]{1,0:T(8,128)(2,1)S(1)}, bf16[296,128]{1,0:T(8,128)(2,1)S(1)}, u32[]{:S(2)}, u32[]{:S(2)}) collective-permute-start(bf16[296,128]{1,0:T(8,128)(2,1)S(1)} %get-tuple-element.28), channel_id=1, source_target_pairs={{0,4},{2,6},{4,0},{6,2},{8,12},{10,14},{12,8},{14,10},{16,20},{18,... | collective-permute-start | bytes 227336 | tf_op jit(solution)/shard_map/ppermute | solution.py:391
  15.8 0.0 collective-permute-done.6.refs_7_.refs_1_.refs_3_
  15.8 0.3 collective-permute-start.5
  16.1 0.0 collective-permute-done.7.refs_8_.refs_2_.refs_4_
  16.1 0.0 collective-permute-done.8.refs_9_.refs_3_.refs_5_
  16.1 1.4 %collective-permute-start.10 = (bf16[384,128]{1,0:T(8,128)(2,1)S(1)}, bf16[384,128]{1,0:T(8,128)(2,1)S(1)}, u32[]{:S(2)}, u32[]{:S(2)}) collective-permute-start(bf16[384,128]{1,0:T(8,128)(2,1)S(1)} %get-tuple-element.38), channel_id=1, source_target_pairs={{0,16},{2,18},{4,20},{6,22},{8,24},{10,26},{12,28},{14,30},{16,0},... | collective-permute-start | bytes 294920 | tf_op jit(solution)/shard_map/ppermute | solution.py:394
  17.5 2.6 %collective-permute-start.11 = (bf16[384,128]{1,0:T(8,128)(2,1)S(1)}, bf16[384,128]{1,0:T(8,128)(2,1)S(1)}, u32[]{:S(2)}, u32[]{:S(2)}) collective-permute-start(bf16[384,128]{1,0:T(8,128)(2,1)S(1)} %get-tuple-element.39), channel_id=1, source_target_pairs={{0,8},{2,10},{4,12},{6,14},{8,16},{10,18},{12,20},{14,22},{16,24},... | collective-permute-start | bytes 294920 | tf_op jit(solution)/shard_map/ppermute | solution.py:394
  20.2 0.0 collective-permute-done.3.refs_3_
  20.2 1.2 %collective-permute-start.12 = (bf16[384,128]{1,0:T(8,128)(2,1)S(1)}, bf16[384,128]{1,0:T(8,128)(2,1)S(1)}, u32[]{:S(2)}, u32[]{:S(2)}) collective-permute-start(bf16[384,128]{1,0:T(8,128)(2,1)S(1)} %get-tuple-element.40), channel_id=1, source_target_pairs={{0,24},{2,26},{4,28},{6,30},{8,0},{10,2},{12,4},{14,6},{16,8},{18,... | collective-permute-start | bytes 294920 | tf_op jit(solution)/shard_map/ppermute | solution.py:394
  21.3 0.0 collective-permute-done.4.refs_4_
  21.3 0.0 collective-permute-done.5.refs_5_
  21.4 0.3 %edges.1.refs_10_ = bf16[6,4,16,128]{3,2,1,0:T(8,128)(2,1)S(1)} custom-call(bf16[392,128]{1,0:T(8,128)(2,1)S(1)} %collective-permute-done.refs_0_, bf16[392,128]{1,0:T(8,128)(2,1)S(1)} %collective-permute-done.1.refs_1_, bf16[392,128]{1,0:T(8,128)(2,1)S(1)} %collective-permute-done.2.refs_2_, bf16[296,128]{1,0:T(8,128)(2,1)S(1)} %collective-permute-done.3.refs_3_, ...), custom_call_target="tpu_custom_call" | custom-call | tf_op jit(solution)/shard_map/edges/pallas_call | solution.py:456
  21.7 1.6 %collective-permute-start.9 = (bf16[6,4,16,128]{3,2,1,0:T(8,128)(2,1)S(1)}, bf16[6,4,16,128]{3,2,1,0:T(8,128)(2,1)S(1)}, u32[]{:S(2)}, u32[]{:S(2)}) collective-permute-start(bf16[6,4,16,128]{3,2,1,0:T(8,128)(2,1)S(1)} %edges.1.refs_10_), channel_id=1, source_target_pairs={{0,1},{1,0},{2,3},{3,2},{4,5},{5,4},{6,7},{7,6},{8,9},{9,8},{10,11... | collective-permute-start | bytes 294920 | tf_op jit(solution)/shard_map/ppermute | solution.py:477
  23.3 0.4 %place_flux.1 = (bf16[6,4,32,128]{3,2,1,0:T(8,128)(2,1)S(1)}, bf16[6,128,256]{2,1,0:T(8,128)(2,1)S(1)}) custom-call(bf16[392,128]{1,0:T(8,128)(2,1)S(1)} %collective-permute-done.refs_0_, bf16[392,128]{1,0:T(8,128)(2,1)S(1)} %collective-permute-done.1.refs_1_, bf16[392,128]{1,0:T(8,128)(2,1)S(1)} %collective-permute-done.2.refs_2_, ...), custom_call_target="tpu_custom_call" | custom-call | tf_op jit(solution)/shard_map/place_flux/pallas_call | solution.py:464
  23.7 2.1 %filter_own.1.refs_0_ = f32[6,32,512]{2,1,0:T(8,128)S(1)} custom-call(bf16[6,4,32,128]{3,2,1,0:T(8,128)(2,1)S(1)} %get-tuple-element.36.frame_ref, bf16[256,2816]{1,0:T(8,128)(2,1)S(1)} %get-tuple-element.34.table_ref, bf16[6,64,768]{2,1,0:T(8,128)(2,1)S(1)} %get-tuple-element.26.refs_3_.mix_ref), custom_call_target="tpu_custom_call" | custom-call | flops 2113929216 | bytes 4194304 | tf_op jit(solution)/shard_map/filter_own/pallas_call | solution.py:353
  25.8 0.6 %collective-permute-done.10.refs_6_ = bf16[384,128]{1,0:T(8,128)(2,1)S(1)} collective-permute-done((bf16[384,128]{1,0:T(8,128)(2,1)S(1)}, bf16[384,128]{1,0:T(8,128)(2,1)S(1)}, u32[]{:S(2)}, u32[]{:S(2)}) %collective-permute-start.10) | collective-permute-done | bytes 98336 | tf_op jit(solution)/shard_map/ppermute | solution.py:394
  26.4 0.2 collective-permute-done.11.refs_7_
  26.6 0.4 %collective-permute-done.12.refs_8_ = bf16[384,128]{1,0:T(8,128)(2,1)S(1)} collective-permute-done((bf16[384,128]{1,0:T(8,128)(2,1)S(1)}, bf16[384,128]{1,0:T(8,128)(2,1)S(1)}, u32[]{:S(2)}, u32[]{:S(2)}) %collective-permute-start.12) | collective-permute-done | bytes 98336 | tf_op jit(solution)/shard_map/ppermute | solution.py:394
  27.0 0.0 collective-permute-done.9.frame_ref
  27.0 2.0 %filter_halo_weigh.1 = f32[1,32,512]{2,1,0:T(8,128)} custom-call(bf16[6,4,16,128]{3,2,1,0:T(8,128)(2,1)S(1)} %collective-permute-done.9.frame_ref, bf16[256,2816]{1,0:T(8,128)(2,1)S(1)} %get-tuple-element.34.table_ref, bf16[6,64,384]{2,1,0:T(8,128)(2,1)S(1)} %get-tuple-element.35.mix_ref, f32[6,32,512]{2,1,0:T(8,128)S(1)} %filter_own.1.refs_0_, ...), custom_call_target="tpu_custom_call" | custom-call | flops 1056964608 | bytes 4194304 | tf_op jit(solution)/shard_map/filter_halo_weigh/pallas_call | solution.py:353
  (2 shorter events, 0.0 us)
Async XLA Ops:
  1.5 8.5 %collective-permute-start = (bf16[392,128]{1,0:T(8,128)(2,1)S(1)}, bf16[392,128]{1,0:T(8,128)(2,1)S(1)}, u32[]{:S(2)}, u32[]{:S(2)}) collective-permute-start(bf16[392,128]{1,0:T(8,128)(2,1)S(1)} %get-tuple-element.23), channel_id=1, source_target_pairs={{0,8},{2,10},{4,12},{6,14},{8,16},{10,18},{12,20},{14,22},{16,24},... | collective-permute-start | bytes 301064 | tf_op jit(solution)/shard_map/ppermute | solution.py:394
  4.5 11.3 %collective-permute-start.6 = (bf16[488,128]{1,0:T(8,128)(2,1)S(1)}, bf16[488,128]{1,0:T(8,128)(2,1)S(1)}, u32[]{:S(2)}, u32[]{:S(2)}) collective-permute-start(bf16[488,128]{1,0:T(8,128)(2,1)S(1)} %get-tuple-element.31), channel_id=1, source_target_pairs={{0,2},{2,0},{4,6},{6,4},{8,10},{10,8},{12,14},{14,12},{16,18},{18,... | collective-permute-start | bytes 374792 | tf_op jit(solution)/shard_map/ppermute | solution.py:391
  4.5 9.3 %collective-permute-start.1 = (bf16[392,128]{1,0:T(8,128)(2,1)S(1)}, bf16[392,128]{1,0:T(8,128)(2,1)S(1)}, u32[]{:S(2)}, u32[]{:S(2)}) collective-permute-start(bf16[392,128]{1,0:T(8,128)(2,1)S(1)} %get-tuple-element.24), channel_id=1, source_target_pairs={{0,16},{2,18},{4,20},{6,22},{8,24},{10,26},{12,28},{14,30},{16,0},... | collective-permute-start | bytes 301064 | tf_op jit(solution)/shard_map/ppermute | solution.py:394
  7.1 7.0 %collective-permute-start.2 = (bf16[392,128]{1,0:T(8,128)(2,1)S(1)}, bf16[392,128]{1,0:T(8,128)(2,1)S(1)}, u32[]{:S(2)}, u32[]{:S(2)}) collective-permute-start(bf16[392,128]{1,0:T(8,128)(2,1)S(1)} %get-tuple-element.25), channel_id=1, source_target_pairs={{0,24},{2,26},{4,28},{6,30},{8,0},{10,2},{12,4},{14,6},{16,8},{18,... | collective-permute-start | bytes 301064 | tf_op jit(solution)/shard_map/ppermute | solution.py:394
  8.5 7.6 %collective-permute-start.7 = (bf16[488,128]{1,0:T(8,128)(2,1)S(1)}, bf16[488,128]{1,0:T(8,128)(2,1)S(1)}, u32[]{:S(2)}, u32[]{:S(2)}) collective-permute-start(bf16[488,128]{1,0:T(8,128)(2,1)S(1)} %get-tuple-element.32), channel_id=1, source_target_pairs={{0,4},{2,6},{4,0},{6,2},{8,12},{10,14},{12,8},{14,10},{16,20},{18,... | collective-permute-start | bytes 374792 | tf_op jit(solution)/shard_map/ppermute | solution.py:391
  10.0 6.1 %collective-permute-start.8 = (bf16[488,128]{1,0:T(8,128)(2,1)S(1)}, bf16[488,128]{1,0:T(8,128)(2,1)S(1)}, u32[]{:S(2)}, u32[]{:S(2)}) collective-permute-start(bf16[488,128]{1,0:T(8,128)(2,1)S(1)} %get-tuple-element.33), channel_id=1, source_target_pairs={{0,6},{2,4},{4,2},{6,0},{8,14},{10,12},{12,10},{14,8},{16,22},{18,... | collective-permute-start | bytes 374792 | tf_op jit(solution)/shard_map/ppermute | solution.py:391
  14.1 6.1 %collective-permute-start.3 = (bf16[296,128]{1,0:T(8,128)(2,1)S(1)}, bf16[296,128]{1,0:T(8,128)(2,1)S(1)}, u32[]{:S(2)}, u32[]{:S(2)}) collective-permute-start(bf16[296,128]{1,0:T(8,128)(2,1)S(1)} %get-tuple-element.27), channel_id=1, source_target_pairs={{0,2},{2,0},{4,6},{6,4},{8,10},{10,8},{12,14},{14,12},{16,18},{18,... | collective-permute-start | bytes 227336 | tf_op jit(solution)/shard_map/ppermute | solution.py:391
  14.2 7.2 %collective-permute-start.4 = (bf16[296,128]{1,0:T(8,128)(2,1)S(1)}, bf16[296,128]{1,0:T(8,128)(2,1)S(1)}, u32[]{:S(2)}, u32[]{:S(2)}) collective-permute-start(bf16[296,128]{1,0:T(8,128)(2,1)S(1)} %get-tuple-element.28), channel_id=1, source_target_pairs={{0,4},{2,6},{4,0},{6,2},{8,12},{10,14},{12,8},{14,10},{16,20},{18,... | collective-permute-start | bytes 227336 | tf_op jit(solution)/shard_map/ppermute | solution.py:391
  15.8 5.6 %collective-permute-start.5 = (bf16[296,128]{1,0:T(8,128)(2,1)S(1)}, bf16[296,128]{1,0:T(8,128)(2,1)S(1)}, u32[]{:S(2)}, u32[]{:S(2)}) collective-permute-start(bf16[296,128]{1,0:T(8,128)(2,1)S(1)} %get-tuple-element.29), channel_id=1, source_target_pairs={{0,6},{2,4},{4,2},{6,0},{8,14},{10,12},{12,10},{14,8},{16,22},{18,... | collective-permute-start | bytes 227336 | tf_op jit(solution)/shard_map/ppermute | solution.py:391
  16.1 10.3 %collective-permute-start.10 = (bf16[384,128]{1,0:T(8,128)(2,1)S(1)}, bf16[384,128]{1,0:T(8,128)(2,1)S(1)}, u32[]{:S(2)}, u32[]{:S(2)}) collective-permute-start(bf16[384,128]{1,0:T(8,128)(2,1)S(1)} %get-tuple-element.38), channel_id=1, source_target_pairs={{0,16},{2,18},{4,20},{6,22},{8,24},{10,26},{12,28},{14,30},{16,0},... | collective-permute-start | bytes 294920 | tf_op jit(solution)/shard_map/ppermute | solution.py:394
  17.5 9.1 %collective-permute-start.11 = (bf16[384,128]{1,0:T(8,128)(2,1)S(1)}, bf16[384,128]{1,0:T(8,128)(2,1)S(1)}, u32[]{:S(2)}, u32[]{:S(2)}) collective-permute-start(bf16[384,128]{1,0:T(8,128)(2,1)S(1)} %get-tuple-element.39), channel_id=1, source_target_pairs={{0,8},{2,10},{4,12},{6,14},{8,16},{10,18},{12,20},{14,22},{16,24},... | collective-permute-start | bytes 294920 | tf_op jit(solution)/shard_map/ppermute | solution.py:394
  20.2 6.8 %collective-permute-start.12 = (bf16[384,128]{1,0:T(8,128)(2,1)S(1)}, bf16[384,128]{1,0:T(8,128)(2,1)S(1)}, u32[]{:S(2)}, u32[]{:S(2)}) collective-permute-start(bf16[384,128]{1,0:T(8,128)(2,1)S(1)} %get-tuple-element.40), channel_id=1, source_target_pairs={{0,24},{2,26},{4,28},{6,30},{8,0},{10,2},{12,4},{14,6},{16,8},{18,... | collective-permute-start | bytes 294920 | tf_op jit(solution)/shard_map/ppermute | solution.py:394
  21.7 5.3 %collective-permute-start.9 = (bf16[6,4,16,128]{3,2,1,0:T(8,128)(2,1)S(1)}, bf16[6,4,16,128]{3,2,1,0:T(8,128)(2,1)S(1)}, u32[]{:S(2)}, u32[]{:S(2)}) collective-permute-start(bf16[6,4,16,128]{3,2,1,0:T(8,128)(2,1)S(1)} %edges.1.refs_10_), channel_id=1, source_target_pairs={{0,1},{1,0},{2,3},{3,2},{4,5},{5,4},{6,7},{7,6},{8,9},{9,8},{10,11... | collective-permute-start | bytes 294920 | tf_op jit(solution)/shard_map/ppermute | solution.py:477

commit v7 on v6

--- a/solution.py
+++ b/solution.py
@@ -86,17 +86,31 @@
 def pack_kernel(far, dest_hbm, block_hbm, flux_hbm, weight_hbm, *refs):
     far_out, near_out = refs[: far - 1], refs[far - 1 : far - 1 + NEAR]
     landing, sems = refs[far - 1 + NEAR : -1], refs[-1]
-    copies = start_copies(zip((dest_hbm, block_hbm, flux_hbm, weight_hbm), landing), sems)
     dest_ref, block_ref, flux_ref, weight_ref = landing
+    pairs = (dest_hbm, dest_ref), (flux_hbm, flux_ref), (weight_hbm, weight_ref), (block_hbm, block_ref)
+    copies = start_copies(pairs, sems)
     visits, depth, _ = flux_ref.shape
     block = CAP * TILE_ROWS
     span = visits * block
     copies[0].wait()
-    copies[1].wait()
     dest, me = dest_ref[...], lax.axis_index("patch")
     across = (dest // NEAR - me // NEAR + far) % far
     slot = slots_of(across * NEAR + jnp.bitwise_xor(dest % NEAR, me % NEAR))
     goal = spread(slot, depth, TILE_ROWS) * TILE_ROWS + iota((visits, depth), 1) % TILE_ROWS
+    for copy in copies[1:]:
+        copy.wait()
+    for k in range(visits):
+        both = jnp.concatenate([flux_ref[k], weight_ref[k]], axis=1)
+        moved = sort_visit(goal[k : k + 1], both, far * NEAR * CAP)
+        for x in range(far):
+            for y in range(NEAR):
+                rel = x * NEAR + y
+                part = moved[rel * block : (rel + 1) * block]
+                if x:
+                    far_out[x - 1][part_of(y, span, k, block), :] = part[:, :LANES]
+                else:
+                    near_out[y][part_of(far, span, k, block), :] = part[:, :LANES]
+                near_out[y][part_of(x, span, k, block), :] = part[:, LANES:]
     place = block_ref[...] % ACROSS * DOWN + block_ref[...] // ACROSS + 1
     lane = iota((TILE_ROWS, LANES), 1)
     for x in range(far):
@@ -113,20 +127,6 @@
         else:
             for out in near_out:
                 out[(far + 1) * span :, :] = note
-    copies[2].wait()
-    copies[3].wait()
-    for k in range(visits):
-        both = jnp.concatenate([flux_ref[k], weight_ref[k]], axis=1)
-        moved = sort_visit(goal[k : k + 1], both, far * NEAR * CAP)
-        for x in range(far):
-            for y in range(NEAR):
-                rel = x * NEAR + y
-                part = moved[rel * block : (rel + 1) * block]
-                if x:
-                    far_out[x - 1][part_of(y, span, k, block), :] = part[:, :LANES]
-                else:
-                    near_out[y][part_of(far, span, k, block), :] = part[:, :LANES]
-                near_out[y][part_of(x, span, k, block), :] = part[:, LANES:]
 
 
 def part_of(i, span, k, block):

time: 29.2 us -> 29.2 us (level)
  no operation moved by 1% of the time
where the time goes in v7:
time: 29.2 us; the launch traced here: 28.9 us
  starting transfers between devices  17.3 us (59%)
  Pallas kernels  7.79 us (27%)
  waiting for transfers between devices  3.76 us (13%)
    ppermute x6, starting transfers between devices, shift(): lax.ppermute(value, 'patch', [(i, (i + step * NEAR) % patches) for i in r...  12.3 us
    pallas_call x2, Pallas kernels, filter_rows(): pl.pallas_call(functools.partial(filter_kernel, order), out_shape=shape((...  4.04 us
    ppermute x6, waiting for transfers between devices, shift(): lax.ppermute(value, 'patch', [(i, (i + step * NEAR) % patches) for i in r...  3.75 us
    ppermute x6, starting transfers between devices, swap(): return lax.ppermute(value, 'patch', [(i, i ^ step) for i in range(patches)])  3.46 us
    ppermute x1, starting transfers between devices, per_device(): halos = [lax.ppermute(edges[0], 'band', [(0, 1), (1, 0)])]  1.55 us
    pallas_call x1, Pallas kernels, tables(): pl.pallas_call(functools.partial(table_kernel, bands), out_shape=(shape((...  1.51 us
    pallas_call x1, Pallas kernels, per_device(): pl.pallas_call(functools.partial(pack_kernel, far), out_shape=(shape((NEA...  1.43 us
  transfers between devices with their start and end apart: 13, of which 5 were waited for; matrix products, arithmetic and copies ran while one was open for 0% of the time, Pallas kernels for 15%

profile of v7, /device:TPU:0, one launch (start us, length us, event | category | flops | bytes accessed | tf_op | source)
XLA Modules:
  0.0 28.9 jit_solution(6285226418786808995)
XLA Ops:
  0.0 1.4 %pack.1 = (bf16[392,128]{1,0:T(8,128)(2,1)S(1)}, bf16[392,128]{1,0:T(8,128)(2,1)S(1)}, bf16[392,128]{1,0:T(8,128)(2,1)S(1)}, bf16[488,128]{1,0:T(8,128)(2,1)S(1)...) custom-call(s32[6,16]{1,0:T(8,128)} %dest_hbm.1, s32[6,16]{1,0:T(8,128)} %block_hbm.1, ...), custom_call_target="tpu_custom_call" | custom-call | tf_op jit(solution)/shard_map/pack/pallas_call | solution.py:398
  1.4 3.1 %collective-permute-start = (bf16[392,128]{1,0:T(8,128)(2,1)S(1)}, bf16[392,128]{1,0:T(8,128)(2,1)S(1)}, u32[]{:S(2)}, u32[]{:S(2)}) collective-permute-start(bf16[392,128]{1,0:T(8,128)(2,1)S(1)} %get-tuple-element.23), channel_id=1, source_target_pairs={{0,8},{2,10},{4,12},{6,14},{8,16},{10,18},{12,20},{14,22},{16,24},... | collective-permute-start | bytes 301064 | tf_op jit(solution)/shard_map/ppermute | solution.py:394
  4.5 0.0 collective-permute-start.6
  4.5 2.6 %collective-permute-start.1 = (bf16[392,128]{1,0:T(8,128)(2,1)S(1)}, bf16[392,128]{1,0:T(8,128)(2,1)S(1)}, u32[]{:S(2)}, u32[]{:S(2)}) collective-permute-start(bf16[392,128]{1,0:T(8,128)(2,1)S(1)} %get-tuple-element.24), channel_id=1, source_target_pairs={{0,16},{2,18},{4,20},{6,22},{8,24},{10,26},{12,28},{14,30},{16,0},... | collective-permute-start | bytes 301064 | tf_op jit(solution)/shard_map/ppermute | solution.py:394
  7.1 1.3 %collective-permute-start.2 = (bf16[392,128]{1,0:T(8,128)(2,1)S(1)}, bf16[392,128]{1,0:T(8,128)(2,1)S(1)}, u32[]{:S(2)}, u32[]{:S(2)}) collective-permute-start(bf16[392,128]{1,0:T(8,128)(2,1)S(1)} %get-tuple-element.25), channel_id=1, source_target_pairs={{0,24},{2,26},{4,28},{6,30},{8,0},{10,2},{12,4},{14,6},{16,8},{18,... | collective-permute-start | bytes 301064 | tf_op jit(solution)/shard_map/ppermute | solution.py:394
  8.5 1.5 %collective-permute-start.7 = (bf16[488,128]{1,0:T(8,128)(2,1)S(1)}, bf16[488,128]{1,0:T(8,128)(2,1)S(1)}, u32[]{:S(2)}, u32[]{:S(2)}) collective-permute-start(bf16[488,128]{1,0:T(8,128)(2,1)S(1)} %get-tuple-element.32), channel_id=1, source_target_pairs={{0,4},{2,6},{4,0},{6,2},{8,12},{10,14},{12,8},{14,10},{16,20},{18,... | collective-permute-start | bytes 374792 | tf_op jit(solution)/shard_map/ppermute | solution.py:391
  10.0 0.0 collective-permute-done.refs_0_
  10.0 0.0 collective-permute-start.8
  10.0 1.5 %tables.1 = (bf16[256,2816]{1,0:T(8,128)(2,1)S(1)}, bf16[6,64,768]{2,1,0:T(8,128)(2,1)S(1)}, bf16[6,64,384]{2,1,0:T(8,128)(2,1)S(1)}) custom-call(s32[1]{0:T(128)} %bitcast.2.up_ref, bf16[21,2,31]{2,1,0:T(2,128)(2,1)} %bitcast.7, f32[18,1,21]{2,1,0:T(1,128)} %bitcast.8), custom_call_target="tpu_custom_call" | custom-call | flops 1000000000 | bytes 4194304 | tf_op jit(solution)/shard_map/tables/pallas_call | solution.py:422
  11.5 2.3 %collective-permute-done.1.refs_1_ = bf16[392,128]{1,0:T(8,128)(2,1)S(1)} collective-permute-done((bf16[392,128]{1,0:T(8,128)(2,1)S(1)}, bf16[392,128]{1,0:T(8,128)(2,1)S(1)}, u32[]{:S(2)}, u32[]{:S(2)}) %collective-permute-start.1) | collective-permute-done | bytes 100384 | tf_op jit(solution)/shard_map/ppermute | solution.py:394
  13.8 0.3 %collective-permute-done.2.refs_2_ = bf16[392,128]{1,0:T(8,128)(2,1)S(1)} collective-permute-done((bf16[392,128]{1,0:T(8,128)(2,1)S(1)}, bf16[392,128]{1,0:T(8,128)(2,1)S(1)}, u32[]{:S(2)}, u32[]{:S(2)}) %collective-permute-start.2) | collective-permute-done | bytes 100384 | tf_op jit(solution)/shard_map/ppermute | solution.py:394
  14.1 0.1 collective-permute-start.3
  14.2 1.6 %collective-permute-start.4 = (bf16[296,128]{1,0:T(8,128)(2,1)S(1)}, bf16[296,128]{1,0:T(8,128)(2,1)S(1)}, u32[]{:S(2)}, u32[]{:S(2)}) collective-permute-start(bf16[296,128]{1,0:T(8,128)(2,1)S(1)} %get-tuple-element.28), channel_id=1, source_target_pairs={{0,4},{2,6},{4,0},{6,2},{8,12},{10,14},{12,8},{14,10},{16,20},{18,... | collective-permute-start | bytes 227336 | tf_op jit(solution)/shard_map/ppermute | solution.py:391
  15.8 0.0 collective-permute-done.6.refs_7_.refs_1_.refs_3_
  15.8 0.3 %collective-permute-start.5 = (bf16[296,128]{1,0:T(8,128)(2,1)S(1)}, bf16[296,128]{1,0:T(8,128)(2,1)S(1)}, u32[]{:S(2)}, u32[]{:S(2)}) collective-permute-start(bf16[296,128]{1,0:T(8,128)(2,1)S(1)} %get-tuple-element.29), channel_id=1, source_target_pairs={{0,6},{2,4},{4,2},{6,0},{8,14},{10,12},{12,10},{14,8},{16,22},{18,... | collective-permute-start | bytes 227336 | tf_op jit(solution)/shard_map/ppermute | solution.py:391
  16.1 0.0 collective-permute-done.7.refs_8_.refs_2_.refs_4_
  16.1 0.0 collective-permute-done.8.refs_9_.refs_3_.refs_5_
  16.1 1.4 %collective-permute-start.10 = (bf16[384,128]{1,0:T(8,128)(2,1)S(1)}, bf16[384,128]{1,0:T(8,128)(2,1)S(1)}, u32[]{:S(2)}, u32[]{:S(2)}) collective-permute-start(bf16[384,128]{1,0:T(8,128)(2,1)S(1)} %get-tuple-element.38), channel_id=1, source_target_pairs={{0,16},{2,18},{4,20},{6,22},{8,24},{10,26},{12,28},{14,30},{16,0},... | collective-permute-start | bytes 294920 | tf_op jit(solution)/shard_map/ppermute | solution.py:394
  17.5 2.6 %collective-permute-start.11 = (bf16[384,128]{1,0:T(8,128)(2,1)S(1)}, bf16[384,128]{1,0:T(8,128)(2,1)S(1)}, u32[]{:S(2)}, u32[]{:S(2)}) collective-permute-start(bf16[384,128]{1,0:T(8,128)(2,1)S(1)} %get-tuple-element.39), channel_id=1, source_target_pairs={{0,8},{2,10},{4,12},{6,14},{8,16},{10,18},{12,20},{14,22},{16,24},... | collective-permute-start | bytes 294920 | tf_op jit(solution)/shard_map/ppermute | solution.py:394
  20.1 0.0 collective-permute-done.3.refs_3_
  20.2 1.2 %collective-permute-start.12 = (bf16[384,128]{1,0:T(8,128)(2,1)S(1)}, bf16[384,128]{1,0:T(8,128)(2,1)S(1)}, u32[]{:S(2)}, u32[]{:S(2)}) collective-permute-start(bf16[384,128]{1,0:T(8,128)(2,1)S(1)} %get-tuple-element.40), channel_id=1, source_target_pairs={{0,24},{2,26},{4,28},{6,30},{8,0},{10,2},{12,4},{14,6},{16,8},{18,... | collective-permute-start | bytes 294920 | tf_op jit(solution)/shard_map/ppermute | solution.py:394
  21.3 0.0 collective-permute-done.4.refs_4_
  21.3 0.0 collective-permute-done.5.refs_5_
  21.4 0.3 %edges.1.refs_10_ = bf16[6,4,16,128]{3,2,1,0:T(8,128)(2,1)S(1)} custom-call(bf16[392,128]{1,0:T(8,128)(2,1)S(1)} %collective-permute-done.refs_0_, bf16[392,128]{1,0:T(8,128)(2,1)S(1)} %collective-permute-done.1.refs_1_, bf16[392,128]{1,0:T(8,128)(2,1)S(1)} %collective-permute-done.2.refs_2_, bf16[296,128]{1,0:T(8,128)(2,1)S(1)} %collective-permute-done.3.refs_3_, ...), custom_call_target="tpu_custom_call" | custom-call | tf_op jit(solution)/shard_map/edges/pallas_call | solution.py:456
  21.7 1.5 %collective-permute-start.9 = (bf16[6,4,16,128]{3,2,1,0:T(8,128)(2,1)S(1)}, bf16[6,4,16,128]{3,2,1,0:T(8,128)(2,1)S(1)}, u32[]{:S(2)}, u32[]{:S(2)}) collective-permute-start(bf16[6,4,16,128]{3,2,1,0:T(8,128)(2,1)S(1)} %edges.1.refs_10_), channel_id=1, source_target_pairs={{0,1},{1,0},{2,3},{3,2},{4,5},{5,4},{6,7},{7,6},{8,9},{9,8},{10,11... | collective-permute-start | bytes 294920 | tf_op jit(solution)/shard_map/ppermute | solution.py:477
  23.2 0.4 %place_flux.1 = (bf16[6,4,32,128]{3,2,1,0:T(8,128)(2,1)S(1)}, bf16[6,128,256]{2,1,0:T(8,128)(2,1)S(1)}) custom-call(bf16[392,128]{1,0:T(8,128)(2,1)S(1)} %collective-permute-done.refs_0_, bf16[392,128]{1,0:T(8,128)(2,1)S(1)} %collective-permute-done.1.refs_1_, bf16[392,128]{1,0:T(8,128)(2,1)S(1)} %collective-permute-done.2.refs_2_, ...), custom_call_target="tpu_custom_call" | custom-call | tf_op jit(solution)/shard_map/place_flux/pallas_call | solution.py:464
  23.7 2.1 %filter_own.1.refs_0_ = f32[6,32,512]{2,1,0:T(8,128)S(1)} custom-call(bf16[6,4,32,128]{3,2,1,0:T(8,128)(2,1)S(1)} %get-tuple-element.36.frame_ref, bf16[256,2816]{1,0:T(8,128)(2,1)S(1)} %get-tuple-element.34.table_ref, bf16[6,64,768]{2,1,0:T(8,128)(2,1)S(1)} %get-tuple-element.26.refs_3_.mix_ref), custom_call_target="tpu_custom_call" | custom-call | flops 2113929216 | bytes 4194304 | tf_op jit(solution)/shard_map/filter_own/pallas_call | solution.py:353
  25.8 0.6 %collective-permute-done.10.refs_6_ = bf16[384,128]{1,0:T(8,128)(2,1)S(1)} collective-permute-done((bf16[384,128]{1,0:T(8,128)(2,1)S(1)}, bf16[384,128]{1,0:T(8,128)(2,1)S(1)}, u32[]{:S(2)}, u32[]{:S(2)}) %collective-permute-start.10) | collective-permute-done | bytes 98336 | tf_op jit(solution)/shard_map/ppermute | solution.py:394
  26.4 0.2 collective-permute-done.11.refs_7_
  26.6 0.3 %collective-permute-done.12.refs_8_ = bf16[384,128]{1,0:T(8,128)(2,1)S(1)} collective-permute-done((bf16[384,128]{1,0:T(8,128)(2,1)S(1)}, bf16[384,128]{1,0:T(8,128)(2,1)S(1)}, u32[]{:S(2)}, u32[]{:S(2)}) %collective-permute-start.12) | collective-permute-done | bytes 98336 | tf_op jit(solution)/shard_map/ppermute | solution.py:394
  27.0 0.0 collective-permute-done.9.frame_ref
  27.0 1.9 %filter_halo_weigh.1 = f32[1,32,512]{2,1,0:T(8,128)} custom-call(bf16[6,4,16,128]{3,2,1,0:T(8,128)(2,1)S(1)} %collective-permute-done.9.frame_ref, bf16[256,2816]{1,0:T(8,128)(2,1)S(1)} %get-tuple-element.34.table_ref, bf16[6,64,384]{2,1,0:T(8,128)(2,1)S(1)} %get-tuple-element.35.mix_ref, f32[6,32,512]{2,1,0:T(8,128)S(1)} %filter_own.1.refs_0_, ...), custom_call_target="tpu_custom_call" | custom-call | flops 1056964608 | bytes 4194304 | tf_op jit(solution)/shard_map/filter_halo_weigh/pallas_call | solution.py:353
  (2 shorter events, 0.0 us)
Async XLA Ops:
  1.4 8.5 %collective-permute-start = (bf16[392,128]{1,0:T(8,128)(2,1)S(1)}, bf16[392,128]{1,0:T(8,128)(2,1)S(1)}, u32[]{:S(2)}, u32[]{:S(2)}) collective-permute-start(bf16[392,128]{1,0:T(8,128)(2,1)S(1)} %get-tuple-element.23), channel_id=1, source_target_pairs={{0,8},{2,10},{4,12},{6,14},{8,16},{10,18},{12,20},{14,22},{16,24},... | collective-permute-start | bytes 301064 | tf_op jit(solution)/shard_map/ppermute | solution.py:394
  4.5 11.2 %collective-permute-start.6 = (bf16[488,128]{1,0:T(8,128)(2,1)S(1)}, bf16[488,128]{1,0:T(8,128)(2,1)S(1)}, u32[]{:S(2)}, u32[]{:S(2)}) collective-permute-start(bf16[488,128]{1,0:T(8,128)(2,1)S(1)} %get-tuple-element.31), channel_id=1, source_target_pairs={{0,2},{2,0},{4,6},{6,4},{8,10},{10,8},{12,14},{14,12},{16,18},{18,... | collective-permute-start | bytes 374792 | tf_op jit(solution)/shard_map/ppermute | solution.py:391
  4.5 9.3 %collective-permute-start.1 = (bf16[392,128]{1,0:T(8,128)(2,1)S(1)}, bf16[392,128]{1,0:T(8,128)(2,1)S(1)}, u32[]{:S(2)}, u32[]{:S(2)}) collective-permute-start(bf16[392,128]{1,0:T(8,128)(2,1)S(1)} %get-tuple-element.24), channel_id=1, source_target_pairs={{0,16},{2,18},{4,20},{6,22},{8,24},{10,26},{12,28},{14,30},{16,0},... | collective-permute-start | bytes 301064 | tf_op jit(solution)/shard_map/ppermute | solution.py:394
  7.1 7.0 %collective-permute-start.2 = (bf16[392,128]{1,0:T(8,128)(2,1)S(1)}, bf16[392,128]{1,0:T(8,128)(2,1)S(1)}, u32[]{:S(2)}, u32[]{:S(2)}) collective-permute-start(bf16[392,128]{1,0:T(8,128)(2,1)S(1)} %get-tuple-element.25), channel_id=1, source_target_pairs={{0,24},{2,26},{4,28},{6,30},{8,0},{10,2},{12,4},{14,6},{16,8},{18,... | collective-permute-start | bytes 301064 | tf_op jit(solution)/shard_map/ppermute | solution.py:394
  8.5 7.6 %collective-permute-start.7 = (bf16[488,128]{1,0:T(8,128)(2,1)S(1)}, bf16[488,128]{1,0:T(8,128)(2,1)S(1)}, u32[]{:S(2)}, u32[]{:S(2)}) collective-permute-start(bf16[488,128]{1,0:T(8,128)(2,1)S(1)} %get-tuple-element.32), channel_id=1, source_target_pairs={{0,4},{2,6},{4,0},{6,2},{8,12},{10,14},{12,8},{14,10},{16,20},{18,... | collective-permute-start | bytes 374792 | tf_op jit(solution)/shard_map/ppermute | solution.py:391
  10.0 6.1 %collective-permute-start.8 = (bf16[488,128]{1,0:T(8,128)(2,1)S(1)}, bf16[488,128]{1,0:T(8,128)(2,1)S(1)}, u32[]{:S(2)}, u32[]{:S(2)}) collective-permute-start(bf16[488,128]{1,0:T(8,128)(2,1)S(1)} %get-tuple-element.33), channel_id=1, source_target_pairs={{0,6},{2,4},{4,2},{6,0},{8,14},{10,12},{12,10},{14,8},{16,22},{18,... | collective-permute-start | bytes 374792 | tf_op jit(solution)/shard_map/ppermute | solution.py:391
  14.1 6.0 %collective-permute-start.3 = (bf16[296,128]{1,0:T(8,128)(2,1)S(1)}, bf16[296,128]{1,0:T(8,128)(2,1)S(1)}, u32[]{:S(2)}, u32[]{:S(2)}) collective-permute-start(bf16[296,128]{1,0:T(8,128)(2,1)S(1)} %get-tuple-element.27), channel_id=1, source_target_pairs={{0,2},{2,0},{4,6},{6,4},{8,10},{10,8},{12,14},{14,12},{16,18},{18,... | collective-permute-start | bytes 227336 | tf_op jit(solution)/shard_map/ppermute | solution.py:391
  14.2 7.2 %collective-permute-start.4 = (bf16[296,128]{1,0:T(8,128)(2,1)S(1)}, bf16[296,128]{1,0:T(8,128)(2,1)S(1)}, u32[]{:S(2)}, u32[]{:S(2)}) collective-permute-start(bf16[296,128]{1,0:T(8,128)(2,1)S(1)} %get-tuple-element.28), channel_id=1, source_target_pairs={{0,4},{2,6},{4,0},{6,2},{8,12},{10,14},{12,8},{14,10},{16,20},{18,... | collective-permute-start | bytes 227336 | tf_op jit(solution)/shard_map/ppermute | solution.py:391
  15.8 5.6 %collective-permute-start.5 = (bf16[296,128]{1,0:T(8,128)(2,1)S(1)}, bf16[296,128]{1,0:T(8,128)(2,1)S(1)}, u32[]{:S(2)}, u32[]{:S(2)}) collective-permute-start(bf16[296,128]{1,0:T(8,128)(2,1)S(1)} %get-tuple-element.29), channel_id=1, source_target_pairs={{0,6},{2,4},{4,2},{6,0},{8,14},{10,12},{12,10},{14,8},{16,22},{18,... | collective-permute-start | bytes 227336 | tf_op jit(solution)/shard_map/ppermute | solution.py:391
  16.1 10.3 %collective-permute-start.10 = (bf16[384,128]{1,0:T(8,128)(2,1)S(1)}, bf16[384,128]{1,0:T(8,128)(2,1)S(1)}, u32[]{:S(2)}, u32[]{:S(2)}) collective-permute-start(bf16[384,128]{1,0:T(8,128)(2,1)S(1)} %get-tuple-element.38), channel_id=1, source_target_pairs={{0,16},{2,18},{4,20},{6,22},{8,24},{10,26},{12,28},{14,30},{16,0},... | collective-permute-start | bytes 294920 | tf_op jit(solution)/shard_map/ppermute | solution.py:394
  17.5 9.1 %collective-permute-start.11 = (bf16[384,128]{1,0:T(8,128)(2,1)S(1)}, bf16[384,128]{1,0:T(8,128)(2,1)S(1)}, u32[]{:S(2)}, u32[]{:S(2)}) collective-permute-start(bf16[384,128]{1,0:T(8,128)(2,1)S(1)} %get-tuple-element.39), channel_id=1, source_target_pairs={{0,8},{2,10},{4,12},{6,14},{8,16},{10,18},{12,20},{14,22},{16,24},... | collective-permute-start | bytes 294920 | tf_op jit(solution)/shard_map/ppermute | solution.py:394
  20.2 6.8 %collective-permute-start.12 = (bf16[384,128]{1,0:T(8,128)(2,1)S(1)}, bf16[384,128]{1,0:T(8,128)(2,1)S(1)}, u32[]{:S(2)}, u32[]{:S(2)}) collective-permute-start(bf16[384,128]{1,0:T(8,128)(2,1)S(1)} %get-tuple-element.40), channel_id=1, source_target_pairs={{0,24},{2,26},{4,28},{6,30},{8,0},{10,2},{12,4},{14,6},{16,8},{18,... | collective-permute-start | bytes 294920 | tf_op jit(solution)/shard_map/ppermute | solution.py:394
  21.7 5.3 %collective-permute-start.9 = (bf16[6,4,16,128]{3,2,1,0:T(8,128)(2,1)S(1)}, bf16[6,4,16,128]{3,2,1,0:T(8,128)(2,1)S(1)}, u32[]{:S(2)}, u32[]{:S(2)}) collective-permute-start(bf16[6,4,16,128]{3,2,1,0:T(8,128)(2,1)S(1)} %edges.1.refs_10_), channel_id=1, source_target_pairs={{0,1},{1,0},{2,3},{3,2},{4,5},{5,4},{6,7},{7,6},{8,9},{9,8},{10,11... | collective-permute-start | bytes 294920 | tf_op jit(solution)/shard_map/ppermute | solution.py:477
